TPU v7x, 32 devices: a whole 2x2x4 slice. The times are simulated.
32 devices in a mesh: parts: 2 (over y), src: 4 (over z), tile: 2 (over x), row: 2 (over core).
Axes of the slice: x: 2, y: 2, z: 4, core: 2. Of those that a mesh axis runs over, the one named last changes fastest.
Arguments:
- mask_windows: float32 [4, 256, 256], P(('parts', 'tile'), ('src', 'row')), parts along dimension 0, may hold values from -4 to 4
- target_windows: float32 [4, 256, 256], P(('parts', 'tile'), ('src', 'row')), parts along dimension 0, may hold values from 0 to 1
- pupil_bands: int32 [24, 128, 2], P(('parts', 'src')), parts along dimension 0, may hold values from 0 to 128, as said below
- pupil_phase: float32 [24, 128, 128], P(('parts', 'src')), parts along dimension 0, may hold values from -3.140625 to 3.140625
- source_weight: float32 [24], P(('parts', 'src')), parts along dimension 0, may hold values from 0.2 to 1
Outputs:
- mask_grad: float32 [4, 256, 256], P(('parts', 'tile'), ('src', 'row')), parts along dimension 0
- source_grad: float32 [24], P(('parts', 'src')), parts along dimension 0
There are 2 independent parts, one for each index of `parts`. A program takes and returns all parts, laid end to end along the dimension named above; each array names one. Nothing has to cross between parts.
Inputs may be any that keep to these rules, and one draw needn't show every extreme that they name: For every source point and frequency row, pupil_bands[s, kx, 0] <= pupil_bands[s, kx, 1]; a row that passes nothing holds (0, 0).
All inputs are finite; a program needn't handle non-finite values.
Results may differ from a plain program's by a relative error of at most 0.00019.
Values sent between devices are 32-bit elements; how exact they have to be, the bound alone decides.
No kernel may reach another device: no remote copies, remote signals or barrier semaphores. Data moves between devices by JAX's collectives and lax.ppermute only.
A program may use at most 64 MiB of HBM per device.

v0:
```python
import math

import jax
import jax.numpy as jnp
from jax import lax
from jax.sharding import PartitionSpec as P

M = 256
K = 128
OV = 32


STEEPNESS = 20.0
THRESHOLD = 0.15
LOSS_SCALE = 32.0


def with_halo(block, sides, width):
    for axis, dim in sides:
        count = lax.axis_size(axis)
        forward = [(i, i + 1) for i in range(count - 1)]
        backward = [(target, source) for source, target in forward]
        low = lax.ppermute(
            lax.slice_in_dim(block, block.shape[dim] - width, None, axis=dim), axis, forward
        )
        high = lax.ppermute(lax.slice_in_dim(block, 0, width, axis=dim), axis, backward)
        block = jnp.concatenate([low, block, high], axis=dim)
    return block


def matmul(left_op, right_op):
    return lax.dot_general(
        left_op,
        right_op,
        (((1,), (0,)), ((), ())),
        precision=lax.Precision.HIGHEST,
        preferred_element_type=jnp.float32,
    )


def matmul_tn(left_op, right_op):
    return lax.dot_general(
        left_op,
        right_op,
        (((0,), (0,)), ((), ())),
        precision=lax.Precision.HIGHEST,
        preferred_element_type=jnp.float32,
    )


def matmul_nt(left_op, right_op):
    return lax.dot_general(
        left_op,
        right_op,
        (((1,), (1,)), ((), ())),
        precision=lax.Precision.HIGHEST,
        preferred_element_type=jnp.float32,
    )


def wave_tables(positions):
    freq_index = jnp.arange(K, dtype=jnp.int32) - K // 2
    phase_index = freq_index[:, None] * positions[None, :] % M
    angles = 2.0 * math.pi / M * phase_index.astype(jnp.float32)
    return (jnp.cos(angles), jnp.sin(angles))


def shards(mask_windows, target_windows, pupil_bands, pupil_phase, source_weight):
    src_count = lax.axis_size("src")
    tile_count = lax.axis_size("tile")
    row_count = lax.axis_size("row")
    local_x = mask_windows.shape[1]
    per_device = pupil_phase.shape[0]
    sources = per_device * src_count
    field_scale = 1.0 / (M * K)
    src_id = lax.axis_index("src")
    row_id = lax.axis_index("row")
    x_start = (src_id * row_count + row_id) * local_x
    block_starts = (jnp.arange(src_count, dtype=jnp.int32) * row_count + row_id) * local_x
    row_set = (block_starts[:, None] + jnp.arange(local_x, dtype=jnp.int32)[None, :]).reshape(
        src_count * local_x
    )
    cos_all, sin_all = wave_tables(jnp.arange(M, dtype=jnp.int32))
    cos_set, sin_set = wave_tables(row_set)
    cos_own, sin_own = wave_tables(x_start + jnp.arange(local_x, dtype=jnp.int32))
    window = mask_windows[0]
    goal_block = target_windows[0]
    zero_spec = jnp.zeros((K, K), jnp.float32)
    shard_rows = lax.all_gather(window, ("src", "row"), axis=0, tiled=True)
    part_real = matmul_nt(shard_rows, cos_all)
    part_imag = -matmul_nt(shard_rows, sin_all)
    spec_real = matmul(cos_all, part_real) + matmul(sin_all, part_imag)
    spec_imag = matmul(cos_all, part_imag) - matmul(sin_all, part_real)
    freq_cols = jnp.arange(K, dtype=jnp.int32)
    inside = (freq_cols[None, None, :] >= pupil_bands[:, :, 0:1]) & (
        freq_cols[None, None, :] < pupil_bands[:, :, 1:2]
    )
    passing = inside.astype(jnp.float32)
    pupil_real = passing * jnp.cos(pupil_phase)
    pupil_imag = passing * jnp.sin(pupil_phase)
    amp_real = (pupil_real * spec_real - pupil_imag * spec_imag).reshape(per_device * K, K)
    amp_imag = (pupil_imag * spec_real + pupil_real * spec_imag).reshape(per_device * K, K)
    half_real = (matmul(amp_real, cos_all) - matmul(amp_imag, sin_all)).reshape(per_device, K, M)
    half_imag = (matmul(amp_real, sin_all) + matmul(amp_imag, cos_all)).reshape(per_device, K, M)
    weights = source_weight / sources

    def fields(pair_in):
        one_real, one_imag = pair_in
        field_real = field_scale * (matmul_tn(cos_set, one_real) - matmul_tn(sin_set, one_imag))
        field_imag = field_scale * (matmul_tn(cos_set, one_imag) + matmul_tn(sin_set, one_real))
        return (field_real, field_imag)

    stack_real, stack_imag = lax.map(fields, (half_real, half_imag))
    part_real = stack_real
    part_imag = stack_imag
    intensity = lax.psum_scatter(
        jnp.sum(weights[:, None, None] * (part_real * part_real + part_imag * part_imag), axis=0),
        "src",
        scatter_dimension=0,
        tiled=True,
    )
    resist = jax.nn.sigmoid(STEEPNESS * (intensity - THRESHOLD))
    cotangent = LOSS_SCALE * (resist - goal_block) * STEEPNESS * resist * (1.0 - resist)
    cotangent_all = lax.all_gather(cotangent, "src", axis=0, tiled=True)
    source_ids = jnp.arange(per_device, dtype=jnp.int32)

    def add_back(source_id, totals):
        grad_real, grad_imag, source_terms = totals
        field_real = stack_real[source_id]
        field_imag = stack_imag[source_id]
        back_scale = 2.0 * weights[source_id] * cotangent_all
        back_real = back_scale * field_real
        back_imag = back_scale * field_imag
        adj_real = matmul(cos_set, back_real) + matmul(sin_set, back_imag)
        adj_imag = matmul(cos_set, back_imag) - matmul(sin_set, back_real)
        amp_grad_real = field_scale * (matmul_nt(adj_real, cos_all) + matmul_nt(adj_imag, sin_all))
        amp_grad_imag = field_scale * (matmul_nt(adj_imag, cos_all) - matmul_nt(adj_real, sin_all))
        pass_real = pupil_real[source_id]
        pass_imag = pupil_imag[source_id]
        grad_real = grad_real + pass_real * amp_grad_real + pass_imag * amp_grad_imag
        grad_imag = grad_imag + pass_real * amp_grad_imag - pass_imag * amp_grad_real
        term_value = jnp.sum(cotangent_all * (field_real * field_real + field_imag * field_imag))
        source_terms = source_terms + jnp.where(source_ids == source_id, term_value, 0.0)
        return (grad_real, grad_imag, source_terms)

    grad_real, grad_imag, source_terms = lax.fori_loop(
        0, per_device, add_back, (zero_spec, zero_spec, jnp.zeros((per_device,), jnp.float32))
    )
    grad_real, grad_imag = lax.psum((grad_real, grad_imag), ("src", "row"))
    source_sum = lax.psum(source_terms, ("tile", "row"))
    source_grad = source_sum / (sources * M * tile_count)
    q_one = matmul(grad_real, cos_all) - matmul(grad_imag, sin_all)
    q_two = matmul(grad_real, sin_all) + matmul(grad_imag, cos_all)
    grad_block = matmul_tn(cos_own, q_one) - matmul_tn(sin_own, q_two)
    padded = with_halo(grad_block, (("tile", 1),), OV)
    from_below = padded[:, :OV]
    from_above = padded[:, M + OV :]
    middle = jnp.zeros((local_x, M - 2 * OV), jnp.float32)
    grad_block = grad_block + jnp.concatenate([from_below, middle, from_above], axis=1)
    return (grad_block[None], source_grad)


def solution(mesh):
    return jax.shard_map(
        shards,
        mesh=mesh,
        in_specs=(
            P(("parts", "tile"), ("src", "row"), None),
            P(("parts", "tile"), ("src", "row"), None),
            P(("parts", "src"), None, None),
            P(("parts", "src"), None, None),
            P(("parts", "src")),
        ),
        out_specs=(P(("parts", "tile"), ("src", "row"), None), P(("parts", "src"))),
        check_vma=False,
    )
```

profile of v0, /device:TPU:0, one launch (start us, length us, event | category | flops | bytes accessed | tf_op | source)
XLA Modules:
  0.0 178.1 jit_solution(342020758289789825)
XLA Ops:
  7.2 16.1 %all-gather = f32[1,256,256]{2,1,0:T(8,128)S(1)} all-gather(f32[1,32,256]{2,1,0:T(8,128)} %param.9), channel_id=2, replica_groups=mesh['parts'=2,'src'=4,'tile'=2,'row'=2] {'src','row'}, dimensions={1}, use_global_device_ids=true | all-gather | bytes 294912 | tf_op jit(solution)/shard_map/all_gather | solution.py:89
  23.3 0.9 fusion.123
  24.2 0.9 convolution_negate_fusion
  25.1 0.8 fusion.146
  25.9 0.8 fusion.144
  26.7 0.8 convolution_add_fusion.5
  27.5 0.8 convolution_subtract_fusion.5
  28.5 0.7 multiply_add_fusion
  29.2 1.0 fusion.152
  30.3 1.0 fusion.142
  31.3 1.0 convolution_add_fusion.3
  32.3 1.0 convolution_subtract_fusion.3
  33.5 7.2 %while.35 = (s32[]{:T(128)}, f32[3,128,256]{1,2,0:T(8,128)S(1)}, f32[3,128,256]{1,2,0:T(8,128)S(1)}, f32[3,128,256]{2,1,0:T(8,128)S(1)}, f32[3,128,256]{2,1,0:T(...) while((s32[]{:T(128)}, f32[3,128,256]{1,2,0:T(8,128)S(1)}, ...), condition=%wide.region_1.2_spmd.clone.clone, body=%wide.region_0.1_spmd.clone.clone.sunk | while | flops 202375168 | bytes 1316957 | solution.py:113
  34.1 0.6 fusion.290
  35.3 0.6 fusion.292
  36.6 0.6 fusion.290
  37.8 0.6 fusion.292
  39.0 0.6 fusion.290
  40.9 0.7 copy.22
  41.8 20.2 %reduce-scatter.4.cloned.1.call-done = f32[32,256]{1,0:T(8,128)} async-done(((f32[128,256]{1,0:T(8,128)}), f32[32,256]{1,0:T(8,128)}) %reduce-scatter.4.cloned.1.call-update) | async-done | bytes 32784 | tf_op jit(solution)/shard_map/reduce_scatter | solution.py:116
  62.1 0.8 fusion.163
  62.9 13.6 %all_gather.7 = f32[128,256]{1,0:T(8,128)S(1)} all-gather(f32[32,256]{1,0:T(8,128)S(1)} %fusion.163), channel_id=1, replica_groups=mesh['parts'=2,'src'=4,'tile'=2,'row'=2] {'src'}, dimensions={0}, use_global_device_ids=true | all-gather | bytes 163840 | tf_op jit(solution)/shard_map/all_gather | solution.py:124
  76.5 26.2 %while.36 = (s32[]{:T(128)}, f32[128,128]{1,0:T(8,128)S(1)}, f32[128,128]{1,0:T(8,128)S(1)}, f32[3]{0:T(128)S(1)}, f32[3,128,128]{2,1,0:T(8,128)S(1)}, /*index=5...) while((s32[]{:T(128)}, f32[128,128]{1,0:T(8,128)S(1)}, ...), condition=%wide.region_6.7_spmd.clone.clone.clone.clone, body=%wide.region_4.6_spmd.clone.clone.clone.clone.sunk | while | flops 406126592 | bytes 4593900 | solution.py:146
  77.8 0.6 fusion.306
  78.5 0.6 convolution_add_fusion.7
  79.2 0.6 fusion.304
  79.8 0.6 convolution_subtract_fusion.8
  80.4 0.8 fusion.305
  81.3 0.9 fusion.307
  82.1 0.8 fusion.308
  83.0 0.9 fusion.309
  83.9 0.6 fusion.310
  84.5 0.7 fusion.311
  86.6 0.6 fusion.306
  87.3 0.6 convolution_add_fusion.7
  87.9 0.6 fusion.304
  88.5 0.6 convolution_subtract_fusion.8
  89.2 0.8 fusion.305
  90.0 0.8 fusion.307
  90.9 0.8 fusion.308
  91.7 0.9 fusion.309
  92.6 0.6 fusion.310
  93.2 0.7 fusion.311
  95.3 0.6 fusion.306
  96.0 0.6 convolution_add_fusion.7
  96.6 0.6 fusion.304
  97.3 0.6 convolution_subtract_fusion.8
  97.9 0.8 fusion.305
  98.7 0.8 fusion.307
  99.6 0.8 fusion.308
  100.4 0.9 fusion.309
  101.3 0.6 fusion.310
  102.0 0.7 fusion.311
  102.7 0.6 copy-done.1
  103.3 5.7 %psum.23 = f32[3]{0:T(128)S(1)} all-reduce(f32[3]{0:T(128)S(1)} %get-tuple-element.296), channel_id=1, replica_groups=mesh['parts'=2,'src'=4,'tile'=2,'row'=2] {'tile','row'}, use_global_device_ids=true, to_apply=%region_9.10 | all-reduce | flops 3 | bytes 24 | tf_op jit(solution)/shard_map/psum | solution.py:150
  109.0 47.2 %all-reduce.3.cloned.1.call-done = (f32[128,128]{1,0:T(8,128)}, f32[128,128]{1,0:T(8,128)}) async-done(((f32[128,128]{1,0:T(8,128)}, f32[128,128]{1,0:T(8,128)}), (f32[128,128]{1,0:T(8,128)}, f32[128,128]{1,0:T(8,128)})) %all-reduce.3.cloned.1.call-update) | async-done | bytes 131088 | tf_op jit(solution)/shard_map/psum | solution.py:149
  156.2 1.7 fusion.150
  157.9 0.8 fusion.138
  158.7 0.8 convolution_add_fusion.4
  159.6 0.8 convolution_subtract_fusion.4
  161.6 3.4 %collective-permute-start = (f32[32,32]{1,0:T(8,128)S(1)}, f32[32,32]{1,0:T(8,128)S(1)}, u32[]{:S(2)}, u32[]{:S(2)}) collective-permute-start(f32[32,32]{1,0:T(8,128)S(1)} %get-tuple-element.617), channel_id=1, source_target_pairs={{0,2},{1,3},{4,6},{5,7},{8,10},{9,11},{12,14},{13,15},{16,18},{17,... | collective-permute-start | bytes 12296 | tf_op jit(solution)/shard_map/ppermute | solution.py:23
  165.0 1.3 collective-permute-start.1
  166.8 3.8 %collective-permute-done.1 = f32[32,32]{1,0:T(8,128)S(1)} collective-permute-done((f32[32,32]{1,0:T(8,128)S(1)}, f32[32,32]{1,0:T(8,128)S(1)}, u32[]{:S(2)}, u32[]{:S(2)}) %collective-permute-start.1) | collective-permute-done | bytes 4128 | tf_op jit(solution)/shard_map/ppermute | solution.py:26
  170.6 0.7 fusion.160
  (60 shorter events, 8.9 us)
Async XLA Ops:
  7.2 54.9 %reduce-scatter.4.cloned.1.call-start = ((), (), s32[]{:S(2)}) async-start(), calls=%async_computation.1 | async-start | bytes 163840 | tf_op jit(solution)/shard_map/reduce_scatter | solution.py:116
  27.5 0.8 copy-start.4
  27.5 0.9 copy-start
  33.5 7.2 %copy-start.7 = (f32[3]{0:T(128)S(1)}, f32[3]{0:T(128)}, u32[]{:S(2)}) copy-start(f32[3]{0:T(128)} %param.13) | copy-start | bytes 40
  41.6 20.4 %copy-start.3 = (f32[1,32,256]{2,1,0:T(8,128)S(1)}, f32[1,32,256]{2,1,0:T(8,128)}, u32[]{:S(2)}) copy-start(f32[1,32,256]{2,1,0:T(8,128)} %param.10) | copy-start | bytes 98308
  41.7 114.5 %all-reduce.3.cloned.1.call-start = ((), (), s32[]{:S(2)}) async-start(), calls=%async_computation.2 | async-start | bytes 262144 | tf_op jit(solution)/shard_map/psum | solution.py:149
  102.6 0.6 copy-start.1
  102.7 0.6 copy-start.2
  156.2 1.7 copy-start.6
  157.9 0.8 copy-start.5
  161.6 5.2 %collective-permute-start = (f32[32,32]{1,0:T(8,128)S(1)}, f32[32,32]{1,0:T(8,128)S(1)}, u32[]{:S(2)}, u32[]{:S(2)}) collective-permute-start(f32[32,32]{1,0:T(8,128)S(1)} %get-tuple-element.617), channel_id=1, source_target_pairs={{0,2},{1,3},{4,6},{5,7},{8,10},{9,11},{12,14},{13,15},{16,18},{17,... | collective-permute-start | bytes 12296 | tf_op jit(solution)/shard_map/ppermute | solution.py:23
  165.0 5.6 %collective-permute-start.1 = (f32[32,32]{1,0:T(8,128)S(1)}, f32[32,32]{1,0:T(8,128)S(1)}, u32[]{:S(2)}, u32[]{:S(2)}) collective-permute-start(f32[32,32]{1,0:T(8,128)S(1)} %get-tuple-element.618), channel_id=1, source_target_pairs={{2,0},{3,1},{6,4},{7,5},{10,8},{11,9},{14,12},{15,13},{18,16},{19,... | collective-permute-start | bytes 12296 | tf_op jit(solution)/shard_map/ppermute | solution.py:26
Sparse Core Ops, SparseCore 0:
  41.8 20.2 reduce-scatter.3
  103.4 52.6 all-reduce.2
where the time goes:
time: 179 us; the launch traced here: 178 us
  waiting for transfers between devices  71.2 us (40%)
  matrix products  39.1 us (22%)
  blocking collectives  35.3 us (20%)
  between operations  14.4 us (8%)
  other arithmetic  6.82 us (4%)
  starting transfers between devices  4.73 us (3%)
  local copies, waits for them, and re-layouts  4.13 us (2%)
  loops' own time  2.34 us (1%)
    psum x1, waiting for transfers between devices, shards(): grad_real, grad_imag = lax.psum((grad_real, grad_imag), ('src', 'row'))  47.2 us
    reduce_scatter x1, waiting for transfers between devices, shards(): lax.psum_scatter(jnp.sum(weights[:, None, None] * (part_real * part_real...  20.2 us
    dot_general x24, matrix products, matmul(): lax.dot_general(left_op, right_op, (((1,), (0,)), ((), ())), precision=la...  18.9 us
    all_gather x1, blocking collectives, shards(): shard_rows = lax.all_gather(window, ('src', 'row'), axis=0, tiled=True)  16.1 us
    all_gather x1, blocking collectives, shards(): cotangent_all = lax.all_gather(cotangent, 'src', axis=0, tiled=True)  13.6 us
    dot_general x14, matrix products, matmul_nt(): lax.dot_general(left_op, right_op, (((1,), (1,)), ((), ())), precision=la...  12 us
    dot_general x14, matrix products, matmul_tn(): lax.dot_general(left_op, right_op, (((0,), (0,)), ((), ())), precision=la...  8.24 us
    psum x1, blocking collectives, shards(): source_sum = lax.psum(source_terms, ('tile', 'row'))  5.67 us
  transfers between devices with their start and end apart: 4, of which 3 were waited for; matrix products, arithmetic and copies ran while one was open for 0% of the time, Pallas kernels for 0%

commit v1 on v0

--- a/solution.py
+++ b/solution.py
@@ -1,18 +1,315 @@
+import functools
 import math
 
 import jax
 import jax.numpy as jnp
+import ml_dtypes
+import numpy as np
 from jax import lax
+from jax.experimental import pallas as pl
+from jax.experimental.pallas import tpu as pltpu
 from jax.sharding import PartitionSpec as P
 
-M = 256
-K = 128
 OV = 32
-
-
 STEEPNESS = 20.0
 THRESHOLD = 0.15
 LOSS_SCALE = 32.0
+PAD = 8
+F32 = jnp.float32
+BF16 = jnp.bfloat16
+VMEM_BUDGET = 24 * 1024 * 1024
+
+
+def wave_blocks(pixels, freqs):
+    freq = np.arange(freqs) - freqs // 2
+    angle = 2.0 * np.pi / pixels * ((freq[:, None] * np.arange(pixels)[None, :]) % pixels)
+    c, s = np.cos(angle), np.sin(angle)
+    fwd = np.block([[c, s], [-s, c]]).astype(np.float32)
+
+    def pair(a):
+        high = a.astype(ml_dtypes.bfloat16)
+        low = (a - high.astype(np.float32)).astype(ml_dtypes.bfloat16)
+        return high, low
+
+    return pair(fwd), pair(np.ascontiguousarray(fwd.T))
+
+
+def split(a):
+    high = a.astype(BF16)
+    return high, (a - high.astype(F32)).astype(BF16)
+
+
+def dot(a, b):
+    return jnp.dot(a, b, preferred_element_type=F32)
+
+
+def dot_nt(a, b):
+    return lax.dot_general(a, b, (((1,), (1,)), ((), ())), preferred_element_type=F32)
+
+
+def mm3(left, right, op=dot):
+    (lh, ll), (rh, rl) = left, right
+    return op(lh, rh) + (op(lh, rl) + op(ll, rh))
+
+
+def sincos(phase):
+    h = 0.5 * phase
+    u = h * h
+    s = 1.0 / 6227020800.0
+    for coef in (-1.0 / 39916800.0, 1.0 / 362880.0, -1.0 / 5040.0, 1.0 / 120.0, -1.0 / 6.0, 1.0):
+        s = s * u + coef
+    s = s * h
+    c = 1.0 / 479001600.0
+    for coef in (-1.0 / 3628800.0, 1.0 / 40320.0, -1.0 / 720.0, 1.0 / 24.0, -0.5, 1.0):
+        c = c * u + coef
+    two_s = s + s
+    return two_s * c, 1.0 - two_s * s
+
+
+def offset_of(index, offset, count):
+    return index ^ offset if count & (count - 1) == 0 else lax.rem(index + offset, count)
+
+
+def pick(values):
+    row = lax.axis_index("row")
+    out = values[0]
+    for r in range(1, len(values)):
+        out = jnp.where(row == r, values[r], out)
+    return out
+
+
+def spectrum_kernel(src_count, row_count, *refs):
+    blocks = refs[:src_count]
+    fwd_h, fwd_l, adj_h, adj_l, spec, goal, meta, part = refs[src_count:]
+    rows, pixels = goal.shape[1], goal.shape[2]
+    freqs = spec.shape[1]
+    src, row = lax.axis_index("src"), lax.axis_index("row")
+    slots = meta.shape[0]
+    own = jnp.concatenate([b[:rows] for b in blocks], axis=0)
+    waves = mm3(split(own), (adj_h[:pixels], adj_l[:pixels]))
+    part[...] = jnp.zeros_like(part)
+    for d in range(src_count):
+        block = offset_of(src, d, src_count)
+        start = pl.multiple_of((block * row_count + row) * rows, rows)
+        mine = waves[d * rows : (d + 1) * rows]
+        part[pl.ds(start, rows), :] = mine[:, :freqs]
+        part[pl.ds(pl.multiple_of(pixels + start, rows), rows), :] = mine[:, freqs:]
+        goal[block] = blocks[d][rows : 2 * rows]
+    for j in range(slots):
+        meta[j] = pick([blocks[r * slots + j][2 * rows :] for r in range(row_count)])
+    spec[...] = mm3((fwd_h[...], fwd_l[...]), split(part[...]))
+
+
+def fields_kernel(per_device, sources, slots, *refs):
+    phases = refs[:slots]
+    spec_a, spec_b, meta, fwd_h, fwd_l, adj_h, adj_l = refs[slots : slots + 7]
+    field, pupil, intensity, amp_h, amp_l = refs[slots + 7 :]
+    pixels = intensity.shape[1]
+    freqs = spec_a.shape[1]
+    spec = (spec_a[...] + spec_b[...]) * (1.0 / (pixels * freqs))
+    spec_r, spec_i = spec[:freqs], spec[freqs:]
+    column = lax.broadcasted_iota(jnp.int32, (freqs, freqs), 1).astype(F32)
+    weight = []
+    for j in range(slots):
+        info = meta[j]
+        bounds = info.T
+        for i in range(per_device):
+            s = j * per_device + i
+            weight.append(info[per_device : per_device + 1, i : i + 1] * (1.0 / sources))
+            inside = (column >= bounds[:freqs, i : i + 1]) & (
+                column < bounds[freqs : 2 * freqs, i : i + 1]
+            )
+            sin_p, cos_p = sincos(phases[j][i])
+            pass_r = jnp.where(inside, cos_p, 0.0)
+            pass_i = jnp.where(inside, sin_p, 0.0)
+            pupil[s, :freqs] = pass_r
+            pupil[s, freqs:] = pass_i
+            lanes = slice(s * freqs, (s + 1) * freqs)
+            for half, value in enumerate(
+                (pass_r * spec_r - pass_i * spec_i, pass_i * spec_r + pass_r * spec_i)
+            ):
+                high, low = split(value)
+                amp_h[half * freqs : (half + 1) * freqs, lanes] = high
+                amp_l[half * freqs : (half + 1) * freqs, lanes] = low
+    total = jnp.zeros_like(intensity)
+    group = 2
+    for first in range(0, slots * per_device, group):
+        members = range(first, min(first + group, slots * per_device))
+        lanes = slice(first * freqs, (members[-1] + 1) * freqs)
+        half = mm3((adj_h[...], adj_l[...]), (amp_h[:, lanes], amp_l[:, lanes]))
+        for n, s in enumerate(members):
+            lanes = slice(n * freqs, (n + 1) * freqs)
+            pair = jnp.concatenate([half[:pixels, lanes], half[pixels:, lanes]], axis=1)
+            out = mm3(split(pair), (fwd_h[...], fwd_l[...]))
+            field[s] = out
+            out_r, out_i = out[:, :pixels], out[:, pixels:]
+            total = total + weight[s] * (out_r * out_r + out_i * out_i)
+    intensity[...] = total
+
+
+def adjoint_kernel(per_device, sources, *refs):
+    (field, pupil, inten_a, inten_b, goal_a, goal_b, meta, fwd_h, fwd_l, adj_h, adj_l) = refs[:11]
+    grad, strip, cot_ref, back_h, back_l = refs[11:]
+    src_count, rows = goal_a.shape[0], goal_a.shape[1]
+    pixels = inten_a.shape[1]
+    freqs = grad.shape[1]
+    row = lax.axis_index("row")
+    tile = lax.axis_index("tile")
+    for z in range(src_count):
+        for r in range(2):
+            here = slice((2 * z + r) * rows, (2 * z + r + 1) * rows)
+            goal = jnp.where(row == r, goal_a[z], goal_b[z])
+            intensity = inten_a[here] + inten_b[here]
+            resist = 1.0 / (1.0 + jnp.exp(-STEEPNESS * (intensity - THRESHOLD)))
+            cot_ref[here] = (LOSS_SCALE * STEEPNESS) * (resist - goal) * resist * (1.0 - resist)
+    cot = cot_ref[...]
+    count = field.shape[0]
+    lane = lax.broadcasted_iota(jnp.int32, (PAD, freqs), 1)
+    terms = jnp.zeros((PAD, freqs), F32)
+    for s in range(count):
+        value = field[s]
+        back_r, back_i = cot * value[:, :pixels], cot * value[:, pixels:]
+        power = back_r * value[:, :pixels] + back_i * value[:, pixels:]
+        power = jnp.sum(jnp.sum(power, axis=0, keepdims=True), axis=1, keepdims=True)
+        terms = terms + jnp.where(lane == s, power, 0.0)
+        back = jnp.concatenate([back_r, back_i], axis=1)
+        half = mm3(split(back), (adj_h[...], adj_l[...]))
+        lanes = slice(s * freqs, (s + 1) * freqs)
+        for n in range(2):
+            high, low = split(half[:, n * freqs : (n + 1) * freqs])
+            back_h[n * pixels : (n + 1) * pixels, lanes] = high
+            back_l[n * pixels : (n + 1) * pixels, lanes] = low
+    grad_r = jnp.zeros((freqs, freqs), F32)
+    grad_i = jnp.zeros((freqs, freqs), F32)
+    group = 2
+    for first in range(0, count, group):
+        members = range(first, min(first + group, count))
+        lanes = slice(first * freqs, (members[-1] + 1) * freqs)
+        out = mm3((fwd_h[...], fwd_l[...]), (back_h[:, lanes], back_l[:, lanes]))
+        for n, s in enumerate(members):
+            lanes = slice(n * freqs, (n + 1) * freqs)
+            j, i = divmod(s, per_device)
+            weight = meta[j][per_device : per_device + 1, i : i + 1] * (
+                2.0 / (sources * pixels * freqs)
+            )
+            pass_r, pass_i = weight * pupil[s, :freqs], weight * pupil[s, freqs:]
+            out_r, out_i = out[:freqs, lanes], out[freqs:, lanes]
+            grad_r = grad_r + (pass_r * out_r + pass_i * out_i)
+            grad_i = grad_i + (pass_r * out_i - pass_i * out_r)
+    grad[:freqs] = grad_r
+    grad[freqs : 2 * freqs] = grad_i
+    grad[2 * freqs :] = terms
+    flat = split(jnp.concatenate([grad_r, grad_i], axis=1))
+
+    def edge(start):
+        def part(table):
+            return jnp.concatenate(
+                [table[start : start + OV], table[pixels + start : pixels + start + OV]], axis=0
+            )
+
+        return part(adj_h), part(adj_l)
+
+    high_h, high_l = edge(pixels - OV)
+    low_h, low_l = edge(0)
+    table = (jnp.where(tile == 0, high_h, low_h), jnp.where(tile == 0, high_l, low_l))
+    strip[: 2 * OV] = mm3(table, flat, dot_nt)
+    strip[2 * OV :] = terms
+
+
+def window_kernel(per_device, term_scale, *refs):
+    grad_a, grad_b, strip_a, strip_b, fwd_h, fwd_l, adj_h, adj_l, out, source = refs
+    rows, pixels = out.shape
+    freqs = grad_a.shape[1]
+    src, row, tile = lax.axis_index("src"), lax.axis_index("row"), lax.axis_index("tile")
+    total = grad_a[: 2 * freqs] + grad_b[: 2 * freqs]
+    flat = split(jnp.concatenate([total[:freqs], total[freqs:]], axis=1))
+    waves = mm3(flat, (fwd_h[...], fwd_l[...]))
+    waves = jnp.concatenate([waves[:, :pixels], waves[:, pixels:]], axis=0)
+    start = pl.multiple_of((src * 2 + row) * rows, rows)
+    table = (adj_h[pl.ds(start, rows), :], adj_l[pl.ds(start, rows), :])
+    window = mm3(table, split(waves))
+    edge = strip_a[: 2 * OV] + strip_b[: 2 * OV]
+    edge = mm3(table, split(jnp.concatenate([edge[:OV], edge[OV:]], axis=1)), dot_nt)
+    zero = jnp.zeros_like(edge)
+    middle = jnp.zeros((rows, pixels - 2 * OV), F32)
+    low, high = jnp.where(tile == 1, edge, zero), jnp.where(tile == 0, edge, zero)
+    out[...] = window + jnp.concatenate([low, middle, high], axis=1)
+    first = jnp.where(row == 0, grad_a[2 * freqs :], grad_b[2 * freqs :])
+    second = jnp.where(row == 0, strip_a[2 * OV :], strip_b[2 * OV :])
+    source[...] = (first + second) * term_scale
+
+
+def call(kernel, outs, scratch=()):
+    return pl.pallas_call(
+        kernel,
+        out_shape=[jax.ShapeDtypeStruct(shape, F32) for shape in outs],
+        out_specs=[pl.BlockSpec(memory_space=pltpu.VMEM) for _ in outs],
+        scratch_shapes=[pltpu.VMEM(shape, kind) for shape, kind in scratch],
+        compiler_params=pltpu.CompilerParams(vmem_limit_bytes=VMEM_BUDGET),
+    )
+
+
+def swap(x, axis, count, offset):
+    return lax.ppermute(x, axis, [(i, i ^ offset) for i in range(count)])
+
+
+def shards_full(mask_windows, target_windows, pupil_bands, pupil_phase, source_weight):
+    src_count, tile_count, row_count = (lax.axis_size(a) for a in ("src", "tile", "row"))
+    rows, pixels = mask_windows.shape[1:]
+    per_device, freqs = pupil_phase.shape[:2]
+    sources = per_device * src_count
+    slots = src_count // row_count
+    count = slots * per_device
+    (fwd_h, fwd_l), (adj_h, adj_l) = wave_blocks(pixels, freqs)
+    tables = [jnp.asarray(t) for t in (fwd_h, fwd_l, adj_h, adj_l)]
+
+    bands = pupil_bands.astype(F32).transpose(0, 2, 1).reshape(per_device, 2 * freqs)
+    weights = jnp.pad(source_weight[None, :], ((0, 0), (0, pixels - per_device)))
+    meta = jnp.concatenate([bands, weights, jnp.zeros((PAD - per_device - 1, pixels), F32)])
+    message = jnp.concatenate([mask_windows[0], target_windows[0], meta], axis=0)
+
+    blocks = [message] + [swap(message, "src", src_count, d) for d in range(1, src_count)]
+    phases = []
+    for j in range(slots):
+        pairs = []
+        for z in range(src_count):
+            for r in range(row_count):
+                pairs.append(((z ^ (r * slots + j)) * row_count + r, z * row_count + r))
+        phases.append(lax.ppermute(pupil_phase, ("src", "row"), pairs))
+
+    spec, goal, meta = call(
+        functools.partial(spectrum_kernel, src_count, row_count),
+        [(2 * freqs, freqs), (src_count, rows, pixels), (slots, PAD, pixels)],
+        [((2 * pixels, freqs), F32)],
+    )(*blocks, *tables)
+    spec_other = swap(spec, "row", row_count, 1)
+    goal_other = swap(goal, "row", row_count, 1)
+
+    field, pupil, inten = call(
+        functools.partial(fields_kernel, per_device, sources, slots),
+        [(count, pixels, 2 * pixels), (count, 2 * freqs, freqs), (pixels, pixels)],
+        [((2 * freqs, count * freqs), BF16)] * 2,
+    )(*phases, spec, spec_other, meta, *tables)
+    inten_other = swap(inten, "row", row_count, 1)
+
+    grad, strip = call(
+        functools.partial(adjoint_kernel, per_device, sources),
+        [(2 * freqs + PAD, freqs), (2 * OV + PAD, freqs)],
+        [((pixels, pixels), F32)] + [((2 * pixels, count * freqs), BF16)] * 2,
+    )(field, pupil, inten, inten_other, goal, goal_other, meta, *tables)
+    grad_other = swap(grad, "row", row_count, 1)
+    strip_a = swap(strip, "tile", tile_count, 1)
+    strip_b = swap(strip, ("tile", "row"), tile_count * row_count, 3)
+
+    out, source = call(
+        functools.partial(window_kernel, per_device, 1.0 / (sources * pixels * tile_count)),
+        [(rows, pixels), (PAD, freqs)],
+    )(grad, grad_other, strip_a, strip_b, *tables)
+    return out[None], source[0, :per_device]
+
+
+M = 256
+K = 128
 
 
 def with_halo(block, sides, width):
@@ -161,8 +458,9 @@
 
 
 def solution(mesh):
+    small = mesh.shape["src"] == 4 and mesh.shape["tile"] == 2 and mesh.shape["row"] == 2
     return jax.shard_map(
-        shards,
+        shards_full if small else shards,
         mesh=mesh,
         in_specs=(
             P(("parts", "tile"), ("src", "row"), None),

time: 179 us -> 44 us (0.25)
  the two profiles are of different devices: /device:TPU:0 before, /device:TPU:16 now
where the time goes in v1:
time: 44 us; the launch traced here: 43.5 us
  waiting for transfers between devices  13.7 us (31%)
  starting transfers between devices  10.4 us (24%)
  local copies, waits for them, and re-layouts  10.3 us (23%)
  Pallas kernels  7.62 us (17%)
  other arithmetic  0.69 us (2%)
  between operations  0.69 us (2%)
    ppermute x9, waiting for transfers between devices, swap(): return lax.ppermute(x, axis, [(i, i ^ offset) for i in range(count)])  13.7 us
    unnamed x17, local copies, waits for them, and re-layouts  7.6 us
    ppermute x9, starting transfers between devices, swap(): return lax.ppermute(x, axis, [(i, i ^ offset) for i in range(count)])  6.37 us
    ppermute x2, starting transfers between devices, shards_full(): phases.append(lax.ppermute(pupil_phase, ('src', 'row'), pairs))  4.05 us
    pallas_call x1, Pallas kernels, shards_full(): call(functools.partial(fields_kernel, per_device, sources, slots), [(coun...  3.17 us
    pallas_call x1, Pallas kernels, shards_full(): call(functools.partial(adjoint_kernel, per_device, sources), [(2 * freqs...  2.65 us
    concatenate x1, local copies, waits for them, and re-layouts, shards_full(): jnp.concatenate([mask_windows[0], target_windows[0], meta], axis=0)  1.54 us
    pallas_call x1, Pallas kernels, shards_full(): call(functools.partial(window_kernel, per_device, 1.0 / (sources * pixels...  1.14 us
  transfers between devices with their start and end apart: 11, of which 5 were waited for; matrix products, arithmetic and copies ran while one was open for 0% of the time, Pallas kernels for 2%

profile of v1, /device:TPU:16, one launch (start us, length us, event | category | flops | bytes accessed | tf_op | source)
XLA Modules:
  0.0 43.5 jit_solution(9689880706136854670)
XLA Ops:
  0.6 0.7 %convert_bitcast_fusion = f32[1,3,2,128]{3,2,1,0:T(2,128)S(1)} fusion(s32[3,128,2]{1,2,0:T(2,128)} %param.11), kind=kLoop, calls=%fused_computation.1 | loop fusion | flops 768 | bytes 6144
  1.3 0.7 %pad.4 = f32[1,256]{1,0:T(1,128)S(1)} pad(f32[1,3]{1,0:T(1,128)} %bitcast.15, f32[]{:T(128)} %constant.5.clone.1), padding=0_0x0_253 | pad | bytes 1040 | tf_op jit(solution)/shard_map/jit(_pad)/pad | solution.py:267
  2.0 1.5 %concatenate.3.refs_0_ = f32[72,256]{1,0:T(8,128)S(1)} concatenate(f32[32,256]{1,0:T(8,128)} %bitcast.12, f32[32,256]{1,0:T(8,128)} %bitcast.13, f32[3,256]{1,0:T(4,128)S(1)} %bitcast.14, f32[1,256]{1,0:T(1,128)S(1)} %pad.4, f32[4,256]{1,0:T(4,128)S(1)} %broadcast_in_dim.10), dimensions={0} | concatenate | bytes 147456 | tf_op jit(solution)/shard_map/concatenate | solution.py:269
  3.5 1.6 %collective-permute-start.2 = (f32[72,256]{1,0:T(8,128)S(1)}, f32[72,256]{1,0:T(8,128)S(1)}, u32[]{:S(2)}, u32[]{:S(2)}) collective-permute-start(f32[72,256]{1,0:T(8,128)S(1)} %concatenate.3.refs_0_), channel_id=1, source_target_pairs={{0,4},{4,0},{8,12},{12,8},{1,5},{5,1},{9,13},{13,9},{2,6},{6,2},{1... | collective-permute-start | bytes 221192 | tf_op jit(solution)/shard_map/ppermute | solution.py:253
  5.2 0.3 collective-permute-start.3
  5.5 1.6 %collective-permute-start.4 = (f32[72,256]{1,0:T(8,128)S(1)}, f32[72,256]{1,0:T(8,128)S(1)}, u32[]{:S(2)}, u32[]{:S(2)}) collective-permute-start(f32[72,256]{1,0:T(8,128)S(1)} %concatenate.3.refs_0_), channel_id=1, source_target_pairs={{0,12},{4,8},{8,4},{12,0},{1,13},{5,9},{9,5},{13,1},{2,14},{6,10},... | collective-permute-start | bytes 221192 | tf_op jit(solution)/shard_map/ppermute | solution.py:253
  7.1 1.6 %collective-permute-start = (f32[3,128,128]{2,1,0:T(8,128)}, f32[3,128,128]{2,1,0:T(8,128)S(1)}, u32[]{:S(2)}, u32[]{:S(2)}) collective-permute-start(f32[3,128,128]{2,1,0:T(8,128)} %param.12), channel_id=1, source_target_pairs={{0,0},{9,1},{4,4},{13,5},{8,8},{1,9},{12,12},{5,13},{2,2},{11,3},{... | collective-permute-start | bytes 589832 | tf_op jit(solution)/shard_map/ppermute | solution.py:278
  8.6 2.5 %collective-permute-start.1 = (f32[3,128,128]{2,1,0:T(8,128)}, f32[3,128,128]{2,1,0:T(8,128)S(1)}, u32[]{:S(2)}, u32[]{:S(2)}) collective-permute-start(f32[3,128,128]{2,1,0:T(8,128)} %param.12), channel_id=1, source_target_pairs={{4,0},{13,1},{0,4},{9,5},{12,8},{5,9},{8,12},{1,13},{6,2},{15,3},{... | collective-permute-start | bytes 589832 | tf_op jit(solution)/shard_map/ppermute | solution.py:278
  11.1 0.0 collective-permute-done.2.refs_1_
  11.1 0.0 collective-permute-done.3.refs_2_
  11.1 7.8 %collective-permute-done.4.refs_3_ = f32[72,256]{1,0:T(8,128)S(1)} collective-permute-done((f32[72,256]{1,0:T(8,128)S(1)}, f32[72,256]{1,0:T(8,128)S(1)}, u32[]{:S(2)}, u32[]{:S(2)}) %collective-permute-start.4) | collective-permute-done | bytes 73760 | tf_op jit(solution)/shard_map/ppermute | solution.py:253
  18.9 0.0 copy-start
  18.9 0.9 %copy-done = bf16[256,512]{1,0:T(8,128)(2,1)S(1)} copy-done((bf16[256,512]{1,0:T(8,128)(2,1)S(1)}, bf16[256,512]{1,0:T(8,128)(2,1)}, u32[]{:S(2)}) %copy-start) | copy-done | bytes 262168
  19.8 0.0 copy-start.2
  19.8 0.9 %copy-done.2 = bf16[256,512]{1,0:T(8,128)(2,1)S(1)} copy-done((bf16[256,512]{1,0:T(8,128)(2,1)S(1)}, bf16[256,512]{1,0:T(8,128)(2,1)}, u32[]{:S(2)}) %copy-start.2) | copy-done | bytes 262168
  20.8 0.0 copy-start.4
  20.8 0.9 %copy-done.4 = bf16[512,256]{1,0:T(8,128)(2,1)S(1)} copy-done((bf16[512,256]{1,0:T(8,128)(2,1)S(1)}, bf16[512,256]{1,0:T(8,128)(2,1)}, u32[]{:S(2)}) %copy-start.4) | copy-done | bytes 262168
  21.7 0.0 copy-start.6
  21.7 0.9 %copy-done.6 = bf16[512,256]{1,0:T(8,128)(2,1)S(1)} copy-done((bf16[512,256]{1,0:T(8,128)(2,1)S(1)}, bf16[512,256]{1,0:T(8,128)(2,1)}, u32[]{:S(2)}) %copy-start.6) | copy-done | bytes 262168
  22.7 0.7 %shard_map.104 = (f32[256,128]{1,0:T(8,128)S(1)}, f32[4,32,256]{2,1,0:T(8,128)S(1)}, f32[2,8,256]{2,1,0:T(8,128)S(1)}) custom-call(f32[72,256]{1,0:T(8,128)S(1)} %concatenate.3.refs_0_, f32[72,256]{1,0:T(8,128)S(1)} %collective-permute-done.2.refs_1_, f32[72,256]{1,0:T(8,128)S(1)} %collective-permute-done.3.refs_2_, ...), custom_call_target="tpu_custom_call" | custom-call | tf_op jit(solution)/shard_map/pallas_call | solution.py:280
  23.4 0.1 collective-permute-start.5
  23.4 0.0 collective-permute-done.refs_0_
  23.4 0.0 collective-permute-done.1.refs_1_
  23.5 1.3 %collective-permute-done.5.refs_3_ = f32[256,128]{1,0:T(8,128)S(1)} collective-permute-done((f32[256,128]{1,0:T(8,128)S(1)}, f32[256,128]{1,0:T(8,128)S(1)}, u32[]{:S(2)}, u32[]{:S(2)}) %collective-permute-start.5) | collective-permute-done | bytes 131104 | tf_op jit(solution)/shard_map/ppermute | solution.py:253
  24.8 0.0 copy-start.1
  24.8 0.9 %copy-done.1 = bf16[256,512]{1,0:T(8,128)(2,1)S(1)} copy-done((bf16[256,512]{1,0:T(8,128)(2,1)S(1)}, bf16[256,512]{1,0:T(8,128)(2,1)}, u32[]{:S(2)}) %copy-start.1) | copy-done | bytes 262168
  25.7 0.0 copy-start.3
  25.7 0.9 %copy-done.3 = bf16[256,512]{1,0:T(8,128)(2,1)S(1)} copy-done((bf16[256,512]{1,0:T(8,128)(2,1)S(1)}, bf16[256,512]{1,0:T(8,128)(2,1)}, u32[]{:S(2)}) %copy-start.3) | copy-done | bytes 262168
  26.7 0.0 copy-start.5
  26.7 0.9 %copy-done.5 = bf16[512,256]{1,0:T(8,128)(2,1)S(1)} copy-done((bf16[512,256]{1,0:T(8,128)(2,1)S(1)}, bf16[512,256]{1,0:T(8,128)(2,1)}, u32[]{:S(2)}) %copy-start.5) | copy-done | bytes 262168
  27.6 0.0 copy-start.7
  27.6 0.9 %copy-done.7 = bf16[512,256]{1,0:T(8,128)(2,1)S(1)} copy-done((bf16[512,256]{1,0:T(8,128)(2,1)S(1)}, bf16[512,256]{1,0:T(8,128)(2,1)}, u32[]{:S(2)}) %copy-start.7) | copy-done | bytes 262168
  28.6 3.2 %shard_map.105 = (f32[6,256,512]{2,1,0:T(8,128)S(1)}, f32[6,256,128]{2,1,0:T(8,128)S(1)}, f32[256,256]{1,0:T(8,128)S(1)}) custom-call(f32[3,128,128]{2,1,0:T(8,128)S(1)} %collective-permute-done.refs_0_, f32[3,128,128]{2,1,0:T(8,128)S(1)} %collective-permute-done.1.refs_1_, f32[256,128]{1,0:T(8,128)S(1)} %get-tuple-element.12.refs_2_, ...), custom_call_target="tpu_custom_call" | custom-call | tf_op jit(solution)/shard_map/pallas_call | solution.py:288
  31.7 0.2 collective-permute-start.6
  32.0 0.4 collective-permute-start.7
  32.3 1.2 %collective-permute-done.7.refs_5_ = f32[4,32,256]{2,1,0:T(8,128)S(1)} collective-permute-done((f32[4,32,256]{2,1,0:T(8,128)S(1)}, f32[4,32,256]{2,1,0:T(8,128)S(1)}, u32[]{:S(2)}, u32[]{:S(2)}) %collective-permute-start.7) | collective-permute-done | bytes 131104 | tf_op jit(solution)/shard_map/ppermute | solution.py:253
  33.5 0.0 collective-permute-done.6.refs_3_
  33.5 2.7 %shard_map.106 = (f32[264,128]{1,0:T(8,128)S(1)}, f32[72,128]{1,0:T(8,128)S(1)}) custom-call(f32[6,256,512]{2,1,0:T(8,128)S(1)} %get-tuple-element.14.refs_0_, f32[6,256,128]{2,1,0:T(8,128)S(1)} %get-tuple-element.15.refs_1_, f32[256,256]{1,0:T(8,128)S(1)} %get-tuple-element.16.refs_2_, f32[256,256]{1,0:T(8,128)S(1)} %collective-permute-done.6.refs_3_, ...), custom_call_target="tpu_custom_call" | custom-call | tf_op jit(solution)/shard_map/pallas_call | solution.py:295
  36.2 0.2 collective-permute-start.8
  36.4 1.5 %collective-permute-start.10 = (f32[72,128]{1,0:T(8,128)S(1)}, f32[72,128]{1,0:T(8,128)S(1)}, u32[]{:S(2)}, u32[]{:S(2)}) collective-permute-start(f32[72,128]{1,0:T(8,128)S(1)} %get-tuple-element.19), channel_id=1, source_target_pairs={{0,3},{1,2},{2,1},{3,0},{4,7},{5,6},{6,5},{7,4},{8,11},{9,10},{10,... | collective-permute-start | bytes 110600 | tf_op jit(solution)/shard_map/ppermute | solution.py:253
  37.8 0.5 %collective-permute-start.9 = (f32[72,128]{1,0:T(8,128)S(1)}, f32[72,128]{1,0:T(8,128)S(1)}, u32[]{:S(2)}, u32[]{:S(2)}) collective-permute-start(f32[72,128]{1,0:T(8,128)S(1)} %get-tuple-element.19), channel_id=1, source_target_pairs={{0,2},{2,0},{1,3},{3,1},{4,6},{6,4},{5,7},{7,5},{8,10},{10,8},{9,1... | collective-permute-start | bytes 110600 | tf_op jit(solution)/shard_map/ppermute | solution.py:253
  38.4 1.4 %collective-permute-done.10.refs_3_ = f32[72,128]{1,0:T(8,128)S(1)} collective-permute-done((f32[72,128]{1,0:T(8,128)S(1)}, f32[72,128]{1,0:T(8,128)S(1)}, u32[]{:S(2)}, u32[]{:S(2)}) %collective-permute-start.10) | collective-permute-done | bytes 36896 | tf_op jit(solution)/shard_map/ppermute | solution.py:253
  39.8 2.0 %collective-permute-done.9.refs_2_ = f32[72,128]{1,0:T(8,128)S(1)} collective-permute-done((f32[72,128]{1,0:T(8,128)S(1)}, f32[72,128]{1,0:T(8,128)S(1)}, u32[]{:S(2)}, u32[]{:S(2)}) %collective-permute-start.9) | collective-permute-done | bytes 36896 | tf_op jit(solution)/shard_map/ppermute | solution.py:253
  41.8 0.0 collective-permute-done.8.refs_1_
  41.8 1.1 %shard_map.107 = (f32[32,256]{1,0:T(8,128)}, f32[8,128]{1,0:T(8,128)S(1)}) custom-call(f32[264,128]{1,0:T(8,128)S(1)} %get-tuple-element.18.refs_0_, f32[264,128]{1,0:T(8,128)S(1)} %collective-permute-done.8.refs_1_, f32[72,128]{1,0:T(8,128)S(1)} %collective-permute-done.9.refs_2_, f32[72,128]{1,0:T(8,128)S(1)} %collective-permute-done.10.refs_3_, ...), custom_call_target="tpu_custom_call" | custom-call | tf_op jit(solution)/shard_map/pallas_call | solution.py:304
  42.9 0.5 %slice_bitcast_fusion = f32[3]{0:T(128)} fusion(f32[8,128]{1,0:T(8,128)S(1)} %get-tuple-element.21), kind=kLoop, calls=%fused_computation.2 | loop fusion | bytes 24 | tf_op jit(solution)/shard_map/squeeze | solution.py:308
  (2 shorter events, 0.0 us)
Async XLA Ops:
  3.5 7.6 %collective-permute-start.2 = (f32[72,256]{1,0:T(8,128)S(1)}, f32[72,256]{1,0:T(8,128)S(1)}, u32[]{:S(2)}, u32[]{:S(2)}) collective-permute-start(f32[72,256]{1,0:T(8,128)S(1)} %concatenate.3.refs_0_), channel_id=1, source_target_pairs={{0,4},{4,0},{8,12},{12,8},{1,5},{5,1},{9,13},{13,9},{2,6},{6,2},{1... | collective-permute-start | bytes 221192 | tf_op jit(solution)/shard_map/ppermute | solution.py:253
  5.2 6.0 %collective-permute-start.3 = (f32[72,256]{1,0:T(8,128)S(1)}, f32[72,256]{1,0:T(8,128)S(1)}, u32[]{:S(2)}, u32[]{:S(2)}) collective-permute-start(f32[72,256]{1,0:T(8,128)S(1)} %concatenate.3.refs_0_), channel_id=1, source_target_pairs={{0,8},{4,12},{8,0},{12,4},{1,9},{5,13},{9,1},{13,5},{2,10},{6,14},... | collective-permute-start | bytes 221192 | tf_op jit(solution)/shard_map/ppermute | solution.py:253
  5.5 13.4 %collective-permute-start.4 = (f32[72,256]{1,0:T(8,128)S(1)}, f32[72,256]{1,0:T(8,128)S(1)}, u32[]{:S(2)}, u32[]{:S(2)}) collective-permute-start(f32[72,256]{1,0:T(8,128)S(1)} %concatenate.3.refs_0_), channel_id=1, source_target_pairs={{0,12},{4,8},{8,4},{12,0},{1,13},{5,9},{9,5},{13,1},{2,14},{6,10},... | collective-permute-start | bytes 221192 | tf_op jit(solution)/shard_map/ppermute | solution.py:253
  7.1 16.4 %collective-permute-start = (f32[3,128,128]{2,1,0:T(8,128)}, f32[3,128,128]{2,1,0:T(8,128)S(1)}, u32[]{:S(2)}, u32[]{:S(2)}) collective-permute-start(f32[3,128,128]{2,1,0:T(8,128)} %param.12), channel_id=1, source_target_pairs={{0,0},{9,1},{4,4},{13,5},{8,8},{1,9},{12,12},{5,13},{2,2},{11,3},{... | collective-permute-start | bytes 589832 | tf_op jit(solution)/shard_map/ppermute | solution.py:278
  8.6 14.8 %collective-permute-start.1 = (f32[3,128,128]{2,1,0:T(8,128)}, f32[3,128,128]{2,1,0:T(8,128)S(1)}, u32[]{:S(2)}, u32[]{:S(2)}) collective-permute-start(f32[3,128,128]{2,1,0:T(8,128)} %param.12), channel_id=1, source_target_pairs={{4,0},{13,1},{0,4},{9,5},{12,8},{5,9},{8,12},{1,13},{6,2},{15,3},{... | collective-permute-start | bytes 589832 | tf_op jit(solution)/shard_map/ppermute | solution.py:278
  18.9 1.0 %copy-start = (bf16[256,512]{1,0:T(8,128)(2,1)S(1)}, bf16[256,512]{1,0:T(8,128)(2,1)}, u32[]{:S(2)}) copy-start(bf16[256,512]{1,0:T(8,128)(2,1)} %constant.12.clone.refs_4_.refs_5_.refs_7_) | copy-start | bytes 786436
  19.8 0.9 %copy-start.2 = (bf16[256,512]{1,0:T(8,128)(2,1)S(1)}, bf16[256,512]{1,0:T(8,128)(2,1)}, u32[]{:S(2)}) copy-start(bf16[256,512]{1,0:T(8,128)(2,1)} %constant.13.clone.refs_5_.refs_6_.refs_8_) | copy-start | bytes 786436
  20.8 0.9 %copy-start.4 = (bf16[512,256]{1,0:T(8,128)(2,1)S(1)}, bf16[512,256]{1,0:T(8,128)(2,1)}, u32[]{:S(2)}) copy-start(bf16[512,256]{1,0:T(8,128)(2,1)} %constant.14.clone.refs_6_.refs_7_.refs_9_) | copy-start | bytes 786436
  21.7 0.9 %copy-start.6 = (bf16[512,256]{1,0:T(8,128)(2,1)S(1)}, bf16[512,256]{1,0:T(8,128)(2,1)}, u32[]{:S(2)}) copy-start(bf16[512,256]{1,0:T(8,128)(2,1)} %constant.15.clone.refs_7_.refs_8_.refs_10_) | copy-start | bytes 786436
  23.4 1.4 %collective-permute-start.5 = (f32[256,128]{1,0:T(8,128)S(1)}, f32[256,128]{1,0:T(8,128)S(1)}, u32[]{:S(2)}, u32[]{:S(2)}) collective-permute-start(f32[256,128]{1,0:T(8,128)S(1)} %get-tuple-element.12.refs_2_), channel_id=1, source_target_pairs={{0,1},{1,0},{2,3},{3,2},{4,5},{5,4},{6,7},{7,6},{8,9},{9,8},{10,11... | collective-permute-start | bytes 393224 | tf_op jit(solution)/shard_map/ppermute | solution.py:253
  24.8 1.0 %copy-start.1 = (bf16[256,512]{1,0:T(8,128)(2,1)S(1)}, bf16[256,512]{1,0:T(8,128)(2,1)}, u32[]{:S(2)}) copy-start(bf16[256,512]{1,0:T(8,128)(2,1)} %constant.12.clone.refs_4_.refs_5_.refs_7_) | copy-start | bytes 786436
  25.7 0.9 %copy-start.3 = (bf16[256,512]{1,0:T(8,128)(2,1)S(1)}, bf16[256,512]{1,0:T(8,128)(2,1)}, u32[]{:S(2)}) copy-start(bf16[256,512]{1,0:T(8,128)(2,1)} %constant.13.clone.refs_5_.refs_6_.refs_8_) | copy-start | bytes 786436
  26.7 0.9 %copy-start.5 = (bf16[512,256]{1,0:T(8,128)(2,1)S(1)}, bf16[512,256]{1,0:T(8,128)(2,1)}, u32[]{:S(2)}) copy-start(bf16[512,256]{1,0:T(8,128)(2,1)} %constant.14.clone.refs_6_.refs_7_.refs_9_) | copy-start | bytes 786436
  27.6 0.9 %copy-start.7 = (bf16[512,256]{1,0:T(8,128)(2,1)S(1)}, bf16[512,256]{1,0:T(8,128)(2,1)}, u32[]{:S(2)}) copy-start(bf16[512,256]{1,0:T(8,128)(2,1)} %constant.15.clone.refs_7_.refs_8_.refs_10_) | copy-start | bytes 786436
  31.7 1.8 %collective-permute-start.6 = (f32[256,256]{1,0:T(8,128)S(1)}, f32[256,256]{1,0:T(8,128)S(1)}, u32[]{:S(2)}, u32[]{:S(2)}) collective-permute-start(f32[256,256]{1,0:T(8,128)S(1)} %get-tuple-element.16.refs_2_), channel_id=1, source_target_pairs={{0,1},{1,0},{2,3},{3,2},{4,5},{5,4},{6,7},{7,6},{8,9},{9,8},{10,11... | collective-permute-start | bytes 786440 | tf_op jit(solution)/shard_map/ppermute | solution.py:253
  32.0 1.6 %collective-permute-start.7 = (f32[4,32,256]{2,1,0:T(8,128)S(1)}, f32[4,32,256]{2,1,0:T(8,128)S(1)}, u32[]{:S(2)}, u32[]{:S(2)}) collective-permute-start(f32[4,32,256]{2,1,0:T(8,128)S(1)} %get-tuple-element.17.refs_4_), channel_id=1, source_target_pairs={{0,1},{1,0},{2,3},{3,2},{4,5},{5,4},{6,7},{7,6},{8,9},{9,8},{10,11... | collective-permute-start | bytes 393224 | tf_op jit(solution)/shard_map/ppermute | solution.py:253
  36.2 5.6 %collective-permute-start.8 = (f32[264,128]{1,0:T(8,128)S(1)}, f32[264,128]{1,0:T(8,128)S(1)}, u32[]{:S(2)}, u32[]{:S(2)}) collective-permute-start(f32[264,128]{1,0:T(8,128)S(1)} %get-tuple-element.18.refs_0_), channel_id=1, source_target_pairs={{0,1},{1,0},{2,3},{3,2},{4,5},{5,4},{6,7},{7,6},{8,9},{9,8},{10,11... | collective-permute-start | bytes 405512 | tf_op jit(solution)/shard_map/ppermute | solution.py:253
  36.4 3.4 %collective-permute-start.10 = (f32[72,128]{1,0:T(8,128)S(1)}, f32[72,128]{1,0:T(8,128)S(1)}, u32[]{:S(2)}, u32[]{:S(2)}) collective-permute-start(f32[72,128]{1,0:T(8,128)S(1)} %get-tuple-element.19), channel_id=1, source_target_pairs={{0,3},{1,2},{2,1},{3,0},{4,7},{5,6},{6,5},{7,4},{8,11},{9,10},{10,... | collective-permute-start | bytes 110600 | tf_op jit(solution)/shard_map/ppermute | solution.py:253
  37.8 4.0 %collective-permute-start.9 = (f32[72,128]{1,0:T(8,128)S(1)}, f32[72,128]{1,0:T(8,128)S(1)}, u32[]{:S(2)}, u32[]{:S(2)}) collective-permute-start(f32[72,128]{1,0:T(8,128)S(1)} %get-tuple-element.19), channel_id=1, source_target_pairs={{0,2},{2,0},{1,3},{3,1},{4,6},{6,4},{5,7},{7,5},{8,10},{10,8},{9,1... | collective-permute-start | bytes 110600 | tf_op jit(solution)/shard_map/ppermute | solution.py:253

commit v2 on v1

--- a/solution.py
+++ b/solution.py
@@ -3,8 +3,6 @@
 
 import jax
 import jax.numpy as jnp
-import ml_dtypes
-import numpy as np
 from jax import lax
 from jax.experimental import pallas as pl
 from jax.experimental.pallas import tpu as pltpu
@@ -18,20 +16,6 @@
 F32 = jnp.float32
 BF16 = jnp.bfloat16
 VMEM_BUDGET = 24 * 1024 * 1024
-
-
-def wave_blocks(pixels, freqs):
-    freq = np.arange(freqs) - freqs // 2
-    angle = 2.0 * np.pi / pixels * ((freq[:, None] * np.arange(pixels)[None, :]) % pixels)
-    c, s = np.cos(angle), np.sin(angle)
-    fwd = np.block([[c, s], [-s, c]]).astype(np.float32)
-
-    def pair(a):
-        high = a.astype(ml_dtypes.bfloat16)
-        low = (a - high.astype(np.float32)).astype(ml_dtypes.bfloat16)
-        return high, low
-
-    return pair(fwd), pair(np.ascontiguousarray(fwd.T))
 
 
 def split(a):
@@ -66,44 +50,77 @@
     return two_s * c, 1.0 - two_s * s
 
 
-def offset_of(index, offset, count):
-    return index ^ offset if count & (count - 1) == 0 else lax.rem(index + offset, count)
-
-
-def pick(values):
-    row = lax.axis_index("row")
-    out = values[0]
-    for r in range(1, len(values)):
-        out = jnp.where(row == r, values[r], out)
-    return out
-
-
-def spectrum_kernel(src_count, row_count, *refs):
-    blocks = refs[:src_count]
-    fwd_h, fwd_l, adj_h, adj_l, spec, goal, meta, part = refs[src_count:]
+def block_of(src, side, steps, half):
+    same = half - 1 - steps
+    other = half + steps
+    low = src < half
+    return jnp.where(low, same if side == 0 else other, other if side == 0 else same)
+
+
+def message_kernel(mask, goal, bands, weight, message):
+    rows = mask.shape[1]
+    per_device, _, freqs = bands.shape
+    message[:rows] = mask[0]
+    message[rows : 2 * rows] = goal[0]
+    message[2 * rows :] = jnp.zeros_like(message[2 * rows :])
+    for i in range(per_device):
+        for n in range(2):
+            message[2 * rows + i : 2 * rows + i + 1, n * freqs : (n + 1) * freqs] = bands[
+                i, n : n + 1, :
+            ].astype(F32)
+    message[2 * rows + per_device : 2 * rows + per_device + 1, :per_device] = weight[...]
+
+
+def tables_kernel(fwd_h, fwd_l, adj_h, adj_l):
+    freqs, pixels = fwd_h.shape[0] // 2, fwd_h.shape[1] // 2
+
+    def waves(shape, freq_dim):
+        freq = lax.broadcasted_iota(jnp.int32, shape, freq_dim) - freqs // 2
+        turn = freq * lax.broadcasted_iota(jnp.int32, shape, 1 - freq_dim)
+        turn = ((turn + pixels // 2) & (pixels - 1)) - pixels // 2
+        sin, cos = sincos((2.0 * math.pi / pixels) * turn.astype(F32))
+        return split(cos), split(sin)
+
+    (cos_h, cos_l), (sin_h, sin_l) = waves((freqs, pixels), 0)
+    for table, cos, sin in ((fwd_h, cos_h, sin_h), (fwd_l, cos_l, sin_l)):
+        table[:freqs, :pixels] = cos
+        table[:freqs, pixels:] = sin
+        table[freqs:, :pixels] = -sin
+        table[freqs:, pixels:] = cos
+    (cos_h, cos_l), (sin_h, sin_l) = waves((pixels, freqs), 1)
+    for table, cos, sin in ((adj_h, cos_h, sin_h), (adj_l, cos_l, sin_l)):
+        table[:pixels, :freqs] = cos
+        table[:pixels, freqs:] = -sin
+        table[pixels:, :freqs] = sin
+        table[pixels:, freqs:] = cos
+
+
+def spectrum_kernel(half, *refs):
+    blocks = refs[: 2 * half]
+    fwd_h, fwd_l, adj_h, adj_l, spec, goal, meta, part = refs[2 * half :]
     rows, pixels = goal.shape[1], goal.shape[2]
     freqs = spec.shape[1]
     src, row = lax.axis_index("src"), lax.axis_index("row")
-    slots = meta.shape[0]
     own = jnp.concatenate([b[:rows] for b in blocks], axis=0)
     waves = mm3(split(own), (adj_h[:pixels], adj_l[:pixels]))
     part[...] = jnp.zeros_like(part)
-    for d in range(src_count):
-        block = offset_of(src, d, src_count)
-        start = pl.multiple_of((block * row_count + row) * rows, rows)
+    for d in range(2 * half):
+        block = block_of(src, d // half, d % half, half)
+        start = pl.multiple_of((block * 2 + row) * rows, rows)
         mine = waves[d * rows : (d + 1) * rows]
         part[pl.ds(start, rows), :] = mine[:, :freqs]
         part[pl.ds(pl.multiple_of(pixels + start, rows), rows), :] = mine[:, freqs:]
         goal[block] = blocks[d][rows : 2 * rows]
-    for j in range(slots):
-        meta[j] = pick([blocks[r * slots + j][2 * rows :] for r in range(row_count)])
+    for j in range(half):
+        meta[j] = jnp.where(row == 0, blocks[j][2 * rows :], blocks[half + j][2 * rows :])
     spec[...] = mm3((fwd_h[...], fwd_l[...]), split(part[...]))
 
 
 def fields_kernel(per_device, sources, slots, *refs):
-    phases = refs[:slots]
-    spec_a, spec_b, meta, fwd_h, fwd_l, adj_h, adj_l = refs[slots : slots + 7]
-    field, pupil, intensity, amp_h, amp_l = refs[slots + 7 :]
+    phase_own, *phases = refs[: slots + 1]
+    spec_a, spec_b, meta, fwd_h, fwd_l, adj_h, adj_l = refs[slots + 1 : slots + 8]
+    field, pupil, intensity, amp_h, amp_l = refs[slots + 8 :]
+    row = lax.axis_index("row")
     pixels = intensity.shape[1]
     freqs = spec_a.shape[1]
     spec = (spec_a[...] + spec_b[...]) * (1.0 / (pixels * freqs))
@@ -119,7 +136,10 @@
             inside = (column >= bounds[:freqs, i : i + 1]) & (
                 column < bounds[freqs : 2 * freqs, i : i + 1]
             )
-            sin_p, cos_p = sincos(phases[j][i])
+            phase = phases[j][i]
+            if j == 0:
+                phase = jnp.where(row == 0, phase_own[i], phase)
+            sin_p, cos_p = sincos(phase)
             pass_r = jnp.where(inside, cos_p, 0.0)
             pass_i = jnp.where(inside, sin_p, 0.0)
             pupil[s, :freqs] = pass_r
@@ -149,12 +169,11 @@
 
 def adjoint_kernel(per_device, sources, *refs):
     (field, pupil, inten_a, inten_b, goal_a, goal_b, meta, fwd_h, fwd_l, adj_h, adj_l) = refs[:11]
-    grad, strip, cot_ref, back_h, back_l = refs[11:]
+    grad, cot_ref, back_h, back_l = refs[11:]
     src_count, rows = goal_a.shape[0], goal_a.shape[1]
     pixels = inten_a.shape[1]
     freqs = grad.shape[1]
     row = lax.axis_index("row")
-    tile = lax.axis_index("tile")
     for z in range(src_count):
         for r in range(2):
             here = slice((2 * z + r) * rows, (2 * z + r + 1) * rows)
@@ -164,6 +183,7 @@
             cot_ref[here] = (LOSS_SCALE * STEEPNESS) * (resist - goal) * resist * (1.0 - resist)
     cot = cot_ref[...]
     count = field.shape[0]
+    line = lax.broadcasted_iota(jnp.int32, (PAD, freqs), 0)
     lane = lax.broadcasted_iota(jnp.int32, (PAD, freqs), 1)
     terms = jnp.zeros((PAD, freqs), F32)
     for s in range(count):
@@ -171,7 +191,8 @@
         back_r, back_i = cot * value[:, :pixels], cot * value[:, pixels:]
         power = back_r * value[:, :pixels] + back_i * value[:, pixels:]
         power = jnp.sum(jnp.sum(power, axis=0, keepdims=True), axis=1, keepdims=True)
-        terms = terms + jnp.where(lane == s, power, 0.0)
+        j, i = divmod(s, per_device)
+        terms = terms + jnp.where((lane == i) & (line == j), power, 0.0)
         back = jnp.concatenate([back_r, back_i], axis=1)
         half = mm3(split(back), (adj_h[...], adj_l[...]))
         lanes = slice(s * freqs, (s + 1) * freqs)
@@ -199,113 +220,151 @@
     grad[:freqs] = grad_r
     grad[freqs : 2 * freqs] = grad_i
     grad[2 * freqs :] = terms
-    flat = split(jnp.concatenate([grad_r, grad_i], axis=1))
-
-    def edge(start):
-        def part(table):
-            return jnp.concatenate(
-                [table[start : start + OV], table[pixels + start : pixels + start + OV]], axis=0
-            )
-
-        return part(adj_h), part(adj_l)
-
-    high_h, high_l = edge(pixels - OV)
-    low_h, low_l = edge(0)
-    table = (jnp.where(tile == 0, high_h, low_h), jnp.where(tile == 0, high_l, low_l))
-    strip[: 2 * OV] = mm3(table, flat, dot_nt)
-    strip[2 * OV :] = terms
-
-
-def window_kernel(per_device, term_scale, *refs):
-    grad_a, grad_b, strip_a, strip_b, fwd_h, fwd_l, adj_h, adj_l, out, source = refs
-    rows, pixels = out.shape
+
+
+def window_kernel(half, grad_a, grad_b, fwd_h, fwd_l, adj_h, adj_l, *outs):
+    bodies, edges = outs[:half], outs[half:]
+    rows, pixels = bodies[0].shape[0] - PAD, bodies[0].shape[1]
     freqs = grad_a.shape[1]
     src, row, tile = lax.axis_index("src"), lax.axis_index("row"), lax.axis_index("tile")
     total = grad_a[: 2 * freqs] + grad_b[: 2 * freqs]
     flat = split(jnp.concatenate([total[:freqs], total[freqs:]], axis=1))
     waves = mm3(flat, (fwd_h[...], fwd_l[...]))
     waves = jnp.concatenate([waves[:, :pixels], waves[:, pixels:]], axis=0)
-    start = pl.multiple_of((src * 2 + row) * rows, rows)
-    table = (adj_h[pl.ds(start, rows), :], adj_l[pl.ds(start, rows), :])
-    window = mm3(table, split(waves))
-    edge = strip_a[: 2 * OV] + strip_b[: 2 * OV]
-    edge = mm3(table, split(jnp.concatenate([edge[:OV], edge[OV:]], axis=1)), dot_nt)
+    tables = []
+    for table in (adj_h, adj_l):
+        parts = []
+        for steps in range(half):
+            start = (block_of(src, 0, steps, half) * 2 + row) * rows
+            parts.append(table[pl.ds(pl.multiple_of(start, rows), rows), :])
+        tables.append(jnp.concatenate(parts, axis=0))
+    window = mm3(tables, split(waves))
+    terms = jnp.where(row == 0, grad_a[2 * freqs :], grad_b[2 * freqs :])
+    for steps in range(half):
+        block = window[steps * rows : (steps + 1) * rows]
+        term = terms[steps : steps + 1]
+        bodies[steps][:rows] = block
+        bodies[steps][rows : rows + 1, :freqs] = term
+        edge = jnp.where(tile == 0, block[:, pixels - OV :], block[:, :OV])
+        edges[steps][:rows, :OV] = edge
+        edges[steps][rows : rows + 1, :] = term
+
+
+def place_kernel(half, term_scale, *refs):
+    bodies, edges = refs[:half], refs[half : 2 * half]
+    out, source = refs[2 * half :]
+    rows, pixels = out.shape[1:]
+    per_device = source.shape[1]
+    src, tile = lax.axis_index("src"), lax.axis_index("tile")
+    steps = jnp.where(src < half, half - 1 - src, src - half)
+
+    def mine(refs, *index):
+        value = refs[0][index]
+        for n in range(1, half):
+            value = jnp.where(steps == n, refs[n][index], value)
+        return value
+
+    body = mine(bodies, slice(0, rows), slice(None))
+    edge = mine(edges, slice(0, rows), slice(0, OV))
     zero = jnp.zeros_like(edge)
     middle = jnp.zeros((rows, pixels - 2 * OV), F32)
     low, high = jnp.where(tile == 1, edge, zero), jnp.where(tile == 0, edge, zero)
-    out[...] = window + jnp.concatenate([low, middle, high], axis=1)
-    first = jnp.where(row == 0, grad_a[2 * freqs :], grad_b[2 * freqs :])
-    second = jnp.where(row == 0, strip_a[2 * OV :], strip_b[2 * OV :])
-    source[...] = (first + second) * term_scale
-
-
-def call(kernel, outs, scratch=()):
+    out[0] = body + jnp.concatenate([low, middle, high], axis=1)
+    term = slice(rows, rows + 1), slice(0, per_device)
+    source[...] = (mine(bodies, *term) + mine(edges, *term)) * term_scale
+
+
+def call(kernel, outs, scratch=(), kind=F32):
     return pl.pallas_call(
         kernel,
-        out_shape=[jax.ShapeDtypeStruct(shape, F32) for shape in outs],
+        out_shape=[jax.ShapeDtypeStruct(shape, kind) for shape in outs],
         out_specs=[pl.BlockSpec(memory_space=pltpu.VMEM) for _ in outs],
-        scratch_shapes=[pltpu.VMEM(shape, kind) for shape, kind in scratch],
+        scratch_shapes=[pltpu.VMEM(shape, scratch_kind) for shape, scratch_kind in scratch],
         compiler_params=pltpu.CompilerParams(vmem_limit_bytes=VMEM_BUDGET),
     )
 
 
-def swap(x, axis, count, offset):
-    return lax.ppermute(x, axis, [(i, i ^ offset) for i in range(count)])
-
-
-def shards_full(mask_windows, target_windows, pupil_bands, pupil_phase, source_weight):
-    src_count, tile_count, row_count = (lax.axis_size(a) for a in ("src", "tile", "row"))
+def swap_rows(x):
+    return lax.ppermute(x, "row", [(0, 1), (1, 0)])
+
+
+def hub_shards(mask_windows, target_windows, pupil_bands, pupil_phase, source_weight):
+    src_count, tile_count = lax.axis_size("src"), lax.axis_size("tile")
     rows, pixels = mask_windows.shape[1:]
     per_device, freqs = pupil_phase.shape[:2]
     sources = per_device * src_count
-    slots = src_count // row_count
-    count = slots * per_device
-    (fwd_h, fwd_l), (adj_h, adj_l) = wave_blocks(pixels, freqs)
-    tables = [jnp.asarray(t) for t in (fwd_h, fwd_l, adj_h, adj_l)]
-
-    bands = pupil_bands.astype(F32).transpose(0, 2, 1).reshape(per_device, 2 * freqs)
-    weights = jnp.pad(source_weight[None, :], ((0, 0), (0, pixels - per_device)))
-    meta = jnp.concatenate([bands, weights, jnp.zeros((PAD - per_device - 1, pixels), F32)])
-    message = jnp.concatenate([mask_windows[0], target_windows[0], meta], axis=0)
-
-    blocks = [message] + [swap(message, "src", src_count, d) for d in range(1, src_count)]
-    phases = []
-    for j in range(slots):
+    half = src_count // 2
+    count = half * per_device
+
+    def chip(low, steps):
+        return half - 1 - steps if low else half + steps
+
+    def to_hub(x, side, steps, cores=(0, 1)):
+        sides = dict.fromkeys(cores, side) if side is not None else {0: 0, 1: 1}
         pairs = []
-        for z in range(src_count):
-            for r in range(row_count):
-                pairs.append(((z ^ (r * slots + j)) * row_count + r, z * row_count + r))
-        phases.append(lax.ppermute(pupil_phase, ("src", "row"), pairs))
+        for low in (True, False):
+            for core, across in sides.items():
+                source, hub = chip(low, steps), chip(low != (across == 1), 0)
+                if source != hub:
+                    pairs.append((source * 2 + core, hub * 2 + core))
+        return lax.ppermute(x, ("src", "row"), pairs)
+
+    (message,) = call(message_kernel, [(2 * rows + PAD, pixels)])(
+        mask_windows,
+        target_windows,
+        pupil_bands.transpose(0, 2, 1),
+        source_weight.reshape(1, per_device),
+    )
+    blocks = [message] + [to_hub(message, 0, n) for n in range(1, half)]
+    blocks += [to_hub(message, 1, n) for n in range(half)]
+    phases = [to_hub(pupil_phase, None, n) for n in range(half)]
+    tables = call(
+        tables_kernel, [(2 * freqs, 2 * pixels)] * 2 + [(2 * pixels, 2 * freqs)] * 2, kind=BF16
+    )()
 
     spec, goal, meta = call(
-        functools.partial(spectrum_kernel, src_count, row_count),
-        [(2 * freqs, freqs), (src_count, rows, pixels), (slots, PAD, pixels)],
+        functools.partial(spectrum_kernel, half),
+        [(2 * freqs, freqs), (src_count, rows, pixels), (half, PAD, pixels)],
         [((2 * pixels, freqs), F32)],
     )(*blocks, *tables)
-    spec_other = swap(spec, "row", row_count, 1)
-    goal_other = swap(goal, "row", row_count, 1)
+    spec_other = swap_rows(spec)
+    goal_other = swap_rows(goal)
 
     field, pupil, inten = call(
-        functools.partial(fields_kernel, per_device, sources, slots),
+        functools.partial(fields_kernel, per_device, sources, half),
         [(count, pixels, 2 * pixels), (count, 2 * freqs, freqs), (pixels, pixels)],
         [((2 * freqs, count * freqs), BF16)] * 2,
-    )(*phases, spec, spec_other, meta, *tables)
-    inten_other = swap(inten, "row", row_count, 1)
-
-    grad, strip = call(
+    )(pupil_phase, *phases, spec, spec_other, meta, *tables)
+    inten_other = swap_rows(inten)
+
+    (grad,) = call(
         functools.partial(adjoint_kernel, per_device, sources),
-        [(2 * freqs + PAD, freqs), (2 * OV + PAD, freqs)],
+        [(2 * freqs + PAD, freqs)],
         [((pixels, pixels), F32)] + [((2 * pixels, count * freqs), BF16)] * 2,
     )(field, pupil, inten, inten_other, goal, goal_other, meta, *tables)
-    grad_other = swap(grad, "row", row_count, 1)
-    strip_a = swap(strip, "tile", tile_count, 1)
-    strip_b = swap(strip, ("tile", "row"), tile_count * row_count, 3)
-
+    grad_other = swap_rows(grad)
+
+    outs = call(
+        functools.partial(window_kernel, half),
+        [(rows + PAD, pixels)] * half + [(rows + PAD, freqs)] * half,
+    )(grad, grad_other, *tables)
+    bodies, edges = outs[:half], outs[half:]
+
+    def from_hub(x, steps, flip):
+        pairs = []
+        for low in (True, False):
+            for tile in range(2):
+                target = tile ^ 1 if flip else tile
+                pairs.append((chip(low, 0) * 2 + tile, chip(low, steps) * 2 + target))
+        return lax.ppermute(x, ("src", "tile"), pairs)
+
+    bodies = [bodies[0]] + [from_hub(bodies[n], n, False) for n in range(1, half)]
+    edges = [from_hub(edges[n], n, True) for n in range(half)]
     out, source = call(
-        functools.partial(window_kernel, per_device, 1.0 / (sources * pixels * tile_count)),
-        [(rows, pixels), (PAD, freqs)],
-    )(grad, grad_other, strip_a, strip_b, *tables)
-    return out[None], source[0, :per_device]
+        functools.partial(place_kernel, half, 1.0 / (sources * pixels * tile_count)),
+        [(1, rows, pixels), (1, per_device)],
+    )(*bodies, *edges)
+    return out, source[0]
 
 
 M = 256
@@ -457,18 +516,40 @@
     return (grad_block[None], source_grad)
 
 
+def hubs_serve(mesh, mask_windows, pupil_phase):
+    src_count = mesh.shape["src"]
+    pixels = mask_windows.shape[2]
+    sources, freqs = pupil_phase.shape[0] // mesh.shape["parts"], pupil_phase.shape[1]
+    per_device = sources // src_count
+    held = sources // 2 * (2 * pixels * pixels + 4 * freqs * freqs) * 4
+    return (
+        mesh.shape["row"] == 2
+        and mesh.shape["tile"] == 2
+        and src_count % 2 == 0
+        and src_count // 2 <= PAD
+        and per_device < PAD
+        and mask_windows.shape[1] // (2 * src_count) % 16 == 0
+        and pixels & (pixels - 1) == 0
+        and pixels >= 2 * freqs
+        and held <= VMEM_BUDGET // 2
+    )
+
+
 def solution(mesh):
-    small = mesh.shape["src"] == 4 and mesh.shape["tile"] == 2 and mesh.shape["row"] == 2
-    return jax.shard_map(
-        shards_full if small else shards,
-        mesh=mesh,
-        in_specs=(
-            P(("parts", "tile"), ("src", "row"), None),
-            P(("parts", "tile"), ("src", "row"), None),
-            P(("parts", "src"), None, None),
-            P(("parts", "src"), None, None),
-            P(("parts", "src")),
-        ),
-        out_specs=(P(("parts", "tile"), ("src", "row"), None), P(("parts", "src"))),
-        check_vma=False,
-    )
+    def run(mask_windows, target_windows, pupil_bands, pupil_phase, source_weight):
+        hubs = hubs_serve(mesh, mask_windows, pupil_phase)
+        return jax.shard_map(
+            hub_shards if hubs else shards,
+            mesh=mesh,
+            in_specs=(
+                P(("parts", "tile"), ("src", "row"), None),
+                P(("parts", "tile"), ("src", "row"), None),
+                P(("parts", "src"), None, None),
+                P(("parts", "src"), None, None),
+                P(("parts", "src")),
+            ),
+            out_specs=(P(("parts", "tile"), ("src", "row"), None), P(("parts", "src"))),
+            check_vma=False,
+        )(mask_windows, target_windows, pupil_bands, pupil_phase, source_weight)
+
+    return run

time: 44 us -> 43 us (0.977)
  the two profiles are of different devices: /device:TPU:16 before, /device:TPU:0 now
where the time goes in v2:
time: 43 us; the launch traced here: 42.6 us
  starting transfers between devices  18.4 us (43%)
  waiting for transfers between devices  11.3 us (26%)
  Pallas kernels  8.28 us (19%)
  local copies, waits for them, and re-layouts  3.77 us (9%)
  between operations  0.78 us (2%)
    ppermute x5, starting transfers between devices, to_hub(): return lax.ppermute(x, ('src', 'row'), pairs)  11.7 us
    ppermute x3, waiting for transfers between devices, from_hub(): return lax.ppermute(x, ('src', 'tile'), pairs)  7.41 us
    unnamed x10, local copies, waits for them, and re-layouts  3.77 us
    ppermute x4, starting transfers between devices, swap_rows(): return lax.ppermute(x, 'row', [(0, 1), (1, 0)])  3.46 us
    ppermute x3, starting transfers between devices, from_hub(): return lax.ppermute(x, ('src', 'tile'), pairs)  3.26 us
    pallas_call x1, Pallas kernels, hub_shards(): call(functools.partial(fields_kernel, per_device, sources, half), [(count...  3.18 us
    pallas_call x1, Pallas kernels, hub_shards(): call(functools.partial(adjoint_kernel, per_device, sources), [(2 * freqs...  2.62 us
    ppermute x4, waiting for transfers between devices, swap_rows(): return lax.ppermute(x, 'row', [(0, 1), (1, 0)])  2.27 us
  transfers between devices with their start and end apart: 12, of which 4 were waited for; matrix products, arithmetic and copies ran while one was open for 0% of the time, Pallas kernels for 3%

profile of v2, /device:TPU:0, one launch (start us, length us, event | category | flops | bytes accessed | tf_op | source)
XLA Modules:
  0.0 42.6 jit_solution(9254286855880904051)
XLA Ops:
  0.6 0.0 copy-start.1
  0.6 0.7 %copy-done.1 = f32[1,32,256]{2,1,0:T(8,128)S(1)} copy-done((f32[1,32,256]{2,1,0:T(8,128)S(1)}, f32[1,32,256]{2,1,0:T(8,128)}, u32[]{:S(2)}) %copy-start.1) | copy-done | bytes 32792
  1.4 0.0 copy-start.2
  1.4 0.8 %copy-done.2 = f32[1,32,256]{2,1,0:T(8,128)S(1)} copy-done((f32[1,32,256]{2,1,0:T(8,128)S(1)}, f32[1,32,256]{2,1,0:T(8,128)}, u32[]{:S(2)}) %copy-start.2) | copy-done | bytes 32792
  2.1 0.0 copy-start.3
  2.1 0.7 %copy-done.3 = s32[3,128,2]{1,2,0:T(2,128)S(1)} copy-done((s32[3,128,2]{1,2,0:T(2,128)S(1)}, s32[3,128,2]{1,2,0:T(2,128)}, u32[]{:S(2)}) %copy-start.3) | copy-done | bytes 3096
  2.8 0.0 copy-start.4
  2.8 0.7 %copy-done.4 = f32[3]{0:T(128)S(1)} copy-done((f32[3]{0:T(128)S(1)}, f32[3]{0:T(128)}, u32[]{:S(2)}) %copy-start.4) | copy-done | bytes 36
  3.5 4.9 %collective-permute-start.2 = (f32[72,256]{1,0:T(8,128)S(1)}, f32[72,256]{1,0:T(8,128)S(1)}, u32[]{:S(2)}, u32[]{:S(2)}) collective-permute-start(f32[72,256]{1,0:T(8,128)S(1)} %shard_map.68.refs_0_), channel_id=1, source_target_pairs={{0,4},{1,5},{12,8},{13,9},{2,6},{3,7},{14,10},{15,11},{16,20},{17,... | collective-permute-start | bytes 221192 | tf_op jit(solution)/shard_map/ppermute | solution.py:310
  8.4 0.7 %collective-permute-start.3 = (f32[72,256]{1,0:T(8,128)S(1)}, f32[72,256]{1,0:T(8,128)S(1)}, u32[]{:S(2)}, u32[]{:S(2)}) collective-permute-start(f32[72,256]{1,0:T(8,128)S(1)} %shard_map.68.refs_0_), channel_id=1, source_target_pairs={{4,8},{5,9},{8,4},{9,5},{6,10},{7,11},{10,6},{11,7},{20,24},{21,25... | collective-permute-start | bytes 221192 | tf_op jit(solution)/shard_map/ppermute | solution.py:310
  9.1 4.0 %collective-permute-start.4 = (f32[72,256]{1,0:T(8,128)S(1)}, f32[72,256]{1,0:T(8,128)S(1)}, u32[]{:S(2)}, u32[]{:S(2)}) collective-permute-start(f32[72,256]{1,0:T(8,128)S(1)} %shard_map.68.refs_0_), channel_id=1, source_target_pairs={{0,8},{1,9},{12,4},{13,5},{2,10},{3,11},{14,6},{15,7},{16,24},{17,... | collective-permute-start | bytes 221192 | tf_op jit(solution)/shard_map/ppermute | solution.py:310
  13.1 0.7 %collective-permute-start = (f32[3,128,128]{2,1,0:T(8,128)}, f32[3,128,128]{2,1,0:T(8,128)S(1)}, u32[]{:S(2)}, u32[]{:S(2)}) collective-permute-start(f32[3,128,128]{2,1,0:T(8,128)} %refs_0_.1), channel_id=1, source_target_pairs={{5,9},{9,5},{7,11},{11,7},{21,25},{25,21},{23,27},{27,23}} | collective-permute-start | bytes 589832 | tf_op jit(solution)/shard_map/ppermute | solution.py:310
  13.8 1.4 %collective-permute-start.1 = (f32[3,128,128]{2,1,0:T(8,128)}, f32[3,128,128]{2,1,0:T(8,128)S(1)}, u32[]{:S(2)}, u32[]{:S(2)}) collective-permute-start(f32[3,128,128]{2,1,0:T(8,128)} %refs_0_.1), channel_id=1, source_target_pairs={{0,4},{1,9},{12,8},{13,5},{2,6},{3,11},{14,10},{15,7},{16,20},{17,... | collective-permute-start | bytes 589832 | tf_op jit(solution)/shard_map/ppermute | solution.py:310
  15.2 0.4 %shard_map.69 = (bf16[256,512]{1,0:T(8,128)(2,1)S(1)}, bf16[256,512]{1,0:T(8,128)(2,1)S(1)}, bf16[512,256]{1,0:T(8,128)(2,1)S(1)}, bf16[512,256]{1,0:T(8,128)(2,1)S(1)}) custom-call(), custom_call_target="tpu_custom_call" | custom-call | tf_op jit(solution)/shard_map/pallas_call | solution.py:321
  15.7 0.0 collective-permute-done.2.refs_1_
  15.7 0.0 collective-permute-done.3.refs_2_
  15.7 0.0 collective-permute-done.4.refs_3_
  15.7 0.7 %shard_map.70 = (f32[256,128]{1,0:T(8,128)S(1)}, f32[4,32,256]{2,1,0:T(8,128)S(1)}, f32[2,8,256]{2,1,0:T(8,128)S(1)}) custom-call(f32[72,256]{1,0:T(8,128)S(1)} %shard_map.68.refs_0_, f32[72,256]{1,0:T(8,128)S(1)} %collective-permute-done.2.refs_1_, f32[72,256]{1,0:T(8,128)S(1)} %collective-permute-done.3.refs_2_, ...), custom_call_target="tpu_custom_call" | custom-call | tf_op jit(solution)/shard_map/pallas_call | solution.py:325
  16.4 1.8 %collective-permute-start.5 = (f32[256,128]{1,0:T(8,128)S(1)}, f32[256,128]{1,0:T(8,128)S(1)}, u32[]{:S(2)}, u32[]{:S(2)}) collective-permute-start(f32[256,128]{1,0:T(8,128)S(1)} %get-tuple-element.22.refs_3_), channel_id=1, source_target_pairs={{0,1},{1,0},{2,3},{3,2},{4,5},{5,4},{6,7},{7,6},{8,9},{9,8},{10,11... | collective-permute-start | bytes 393224 | tf_op jit(solution)/shard_map/ppermute | solution.py:288
  18.2 0.0 collective-permute-done.refs_1_
  18.2 1.6 %collective-permute-done.1.refs_2_ = f32[3,128,128]{2,1,0:T(8,128)S(1)} collective-permute-done((f32[3,128,128]{2,1,0:T(8,128)}, f32[3,128,128]{2,1,0:T(8,128)S(1)}, u32[]{:S(2)}, u32[]{:S(2)}) %collective-permute-start.1) | collective-permute-done | bytes 196640 | tf_op jit(solution)/shard_map/ppermute | solution.py:310
  19.8 0.0 collective-permute-done.5.refs_4_
  19.8 0.0 copy-start
  19.8 0.9 %copy-done = f32[3,128,128]{2,1,0:T(8,128)S(1)} copy-done((f32[3,128,128]{2,1,0:T(8,128)S(1)}, f32[3,128,128]{2,1,0:T(8,128)}, u32[]{:S(2)}) %copy-start) | copy-done | bytes 196632
  20.7 3.2 %shard_map.71 = (f32[6,256,512]{2,1,0:T(8,128)S(1)}, f32[6,256,128]{2,1,0:T(8,128)S(1)}, f32[256,256]{1,0:T(8,128)S(1)}) custom-call(f32[3,128,128]{2,1,0:T(8,128)S(1)} %copy-done, f32[3,128,128]{2,1,0:T(8,128)S(1)} %collective-permute-done.refs_1_, f32[3,128,128]{2,1,0:T(8,128)S(1)} %collective-permute-done.1.refs_2_, ...), custom_call_target="tpu_custom_call" | custom-call | tf_op jit(solution)/shard_map/pallas_call | solution.py:333
  23.9 1.2 %collective-permute-start.6 = (f32[256,256]{1,0:T(8,128)S(1)}, f32[256,256]{1,0:T(8,128)S(1)}, u32[]{:S(2)}, u32[]{:S(2)}) collective-permute-start(f32[256,256]{1,0:T(8,128)S(1)} %get-tuple-element.26.refs_2_), channel_id=1, source_target_pairs={{0,1},{1,0},{2,3},{3,2},{4,5},{5,4},{6,7},{7,6},{8,9},{9,8},{10,11... | collective-permute-start | bytes 786440 | tf_op jit(solution)/shard_map/ppermute | solution.py:288
  25.1 0.1 collective-permute-start.7
  25.2 1.3 %collective-permute-done.7.refs_5_ = f32[4,32,256]{2,1,0:T(8,128)S(1)} collective-permute-done((f32[4,32,256]{2,1,0:T(8,128)S(1)}, f32[4,32,256]{2,1,0:T(8,128)S(1)}, u32[]{:S(2)}, u32[]{:S(2)}) %collective-permute-start.7) | collective-permute-done | bytes 131104 | tf_op jit(solution)/shard_map/ppermute | solution.py:288
  26.5 0.0 collective-permute-done.6.refs_3_
  26.5 2.6 %shard_map.72.grad_a = f32[264,128]{1,0:T(8,128)S(1)} custom-call(f32[6,256,512]{2,1,0:T(8,128)S(1)} %get-tuple-element.24.refs_0_, f32[6,256,128]{2,1,0:T(8,128)S(1)} %get-tuple-element.25.refs_1_, f32[256,256]{1,0:T(8,128)S(1)} %get-tuple-element.26.refs_2_, f32[256,256]{1,0:T(8,128)S(1)} %collective-permute-done.6.refs_3_, ...), custom_call_target="tpu_custom_call" | custom-call | tf_op jit(solution)/shard_map/pallas_call | solution.py:340
  29.1 0.4 %collective-permute-start.8 = (f32[264,128]{1,0:T(8,128)S(1)}, f32[264,128]{1,0:T(8,128)S(1)}, u32[]{:S(2)}, u32[]{:S(2)}) collective-permute-start(f32[264,128]{1,0:T(8,128)S(1)} %shard_map.72.grad_a), channel_id=1, source_target_pairs={{0,1},{1,0},{2,3},{3,2},{4,5},{5,4},{6,7},{7,6},{8,9},{9,8},{10,11... | collective-permute-start | bytes 405512 | tf_op jit(solution)/shard_map/ppermute | solution.py:288
  29.5 1.0 %collective-permute-done.8.grad_b = f32[264,128]{1,0:T(8,128)S(1)} collective-permute-done((f32[264,128]{1,0:T(8,128)S(1)}, f32[264,128]{1,0:T(8,128)S(1)}, u32[]{:S(2)}, u32[]{:S(2)}) %collective-permute-start.8) | collective-permute-done | bytes 135200 | tf_op jit(solution)/shard_map/ppermute | solution.py:288
  30.5 0.6 %shard_map.73 = (f32[40,256]{1,0:T(8,128)S(1)}, f32[40,256]{1,0:T(8,128)S(1)}, f32[40,128]{1,0:T(8,128)S(1)}, f32[40,128]{1,0:T(8,128)S(1)}) custom-call(f32[264,128]{1,0:T(8,128)S(1)} %shard_map.72.grad_a, f32[264,128]{1,0:T(8,128)S(1)} %collective-permute-done.8.grad_b, bf16[256,512]{1,0:T(8,128)(2,1)S(1)} %get-tuple-element.18.refs_4_.refs_6_.refs_7_.fwd_h, ...), custom_call_target="tpu_custom_call" | custom-call | tf_op jit(solution)/shard_map/pallas_call | solution.py:347
  31.2 1.3 %collective-permute-start.9 = (f32[40,256]{1,0:T(8,128)S(1)}, f32[40,256]{1,0:T(8,128)S(1)}, u32[]{:S(2)}, u32[]{:S(2)}) collective-permute-start(f32[40,256]{1,0:T(8,128)S(1)} %get-tuple-element.29), channel_id=1, source_target_pairs={{4,0},{6,2},{8,12},{10,14},{5,1},{7,3},{9,13},{11,15},{20,16},{22,... | collective-permute-start | bytes 122888 | tf_op jit(solution)/shard_map/ppermute | solution.py:359
  32.5 0.7 %collective-permute-start.10 = (f32[40,128]{1,0:T(8,128)S(1)}, f32[40,128]{1,0:T(8,128)S(1)}, u32[]{:S(2)}, u32[]{:S(2)}) collective-permute-start(f32[40,128]{1,0:T(8,128)S(1)} %get-tuple-element.30), channel_id=1, source_target_pairs={{4,6},{6,4},{8,10},{10,8},{5,7},{7,5},{9,11},{11,9},{20,22},{22,20... | collective-permute-start | bytes 61448 | tf_op jit(solution)/shard_map/ppermute | solution.py:359
  33.1 1.3 %collective-permute-start.11 = (f32[40,128]{1,0:T(8,128)S(1)}, f32[40,128]{1,0:T(8,128)S(1)}, u32[]{:S(2)}, u32[]{:S(2)}) collective-permute-start(f32[40,128]{1,0:T(8,128)S(1)} %get-tuple-element.31), channel_id=1, source_target_pairs={{4,2},{6,0},{8,14},{10,12},{5,3},{7,1},{9,15},{11,13},{20,18},{22,... | collective-permute-start | bytes 61448 | tf_op jit(solution)/shard_map/ppermute | solution.py:359
  34.4 0.0 collective-permute-done.10.refs_2_
  34.5 7.4 %collective-permute-done.11.refs_3_ = f32[40,128]{1,0:T(8,128)S(1)} collective-permute-done((f32[40,128]{1,0:T(8,128)S(1)}, f32[40,128]{1,0:T(8,128)S(1)}, u32[]{:S(2)}, u32[]{:S(2)}) %collective-permute-start.11) | collective-permute-done | bytes 20512 | tf_op jit(solution)/shard_map/ppermute | solution.py:359
  41.9 0.0 collective-permute-done.9.refs_1_
  41.9 0.7 %shard_map.74 = (f32[1,32,256]{2,1,0:T(8,128)}, f32[1,3]{1,0:T(1,128)}) custom-call(f32[40,256]{1,0:T(8,128)S(1)} %get-tuple-element.28.refs_0_, f32[40,256]{1,0:T(8,128)S(1)} %collective-permute-done.9.refs_1_, f32[40,128]{1,0:T(8,128)S(1)} %collective-permute-done.10.refs_2_, f32[40,128]{1,0:T(8,128)S(1)} %collective-permute-done.11.refs_3_), custom_call_target="tpu_custom_call" | custom-call | tf_op jit(solution)/shard_map/pallas_call | solution.py:363
  (1 shorter events, 0.0 us)
Async XLA Ops:
  0.6 0.8 %copy-start.1 = (f32[1,32,256]{2,1,0:T(8,128)S(1)}, f32[1,32,256]{2,1,0:T(8,128)}, u32[]{:S(2)}) copy-start(f32[1,32,256]{2,1,0:T(8,128)} %mask.1) | copy-start | bytes 98308
  1.4 0.8 %copy-start.2 = (f32[1,32,256]{2,1,0:T(8,128)S(1)}, f32[1,32,256]{2,1,0:T(8,128)}, u32[]{:S(2)}) copy-start(f32[1,32,256]{2,1,0:T(8,128)} %goal.1) | copy-start | bytes 98308
  2.1 0.7 %copy-start.3 = (s32[3,128,2]{1,2,0:T(2,128)S(1)}, s32[3,128,2]{1,2,0:T(2,128)}, u32[]{:S(2)}) copy-start(s32[3,128,2]{1,2,0:T(2,128)} %param.7) | copy-start | bytes 9220
  2.8 0.7 %copy-start.4 = (f32[3]{0:T(128)S(1)}, f32[3]{0:T(128)}, u32[]{:S(2)}) copy-start(f32[3]{0:T(128)} %param.9) | copy-start | bytes 40
  3.5 12.2 %collective-permute-start.2 = (f32[72,256]{1,0:T(8,128)S(1)}, f32[72,256]{1,0:T(8,128)S(1)}, u32[]{:S(2)}, u32[]{:S(2)}) collective-permute-start(f32[72,256]{1,0:T(8,128)S(1)} %shard_map.68.refs_0_), channel_id=1, source_target_pairs={{0,4},{1,5},{12,8},{13,9},{2,6},{3,7},{14,10},{15,11},{16,20},{17,... | collective-permute-start | bytes 221192 | tf_op jit(solution)/shard_map/ppermute | solution.py:310
  8.4 7.2 %collective-permute-start.3 = (f32[72,256]{1,0:T(8,128)S(1)}, f32[72,256]{1,0:T(8,128)S(1)}, u32[]{:S(2)}, u32[]{:S(2)}) collective-permute-start(f32[72,256]{1,0:T(8,128)S(1)} %shard_map.68.refs_0_), channel_id=1, source_target_pairs={{4,8},{5,9},{8,4},{9,5},{6,10},{7,11},{10,6},{11,7},{20,24},{21,25... | collective-permute-start | bytes 221192 | tf_op jit(solution)/shard_map/ppermute | solution.py:310
  9.1 6.6 %collective-permute-start.4 = (f32[72,256]{1,0:T(8,128)S(1)}, f32[72,256]{1,0:T(8,128)S(1)}, u32[]{:S(2)}, u32[]{:S(2)}) collective-permute-start(f32[72,256]{1,0:T(8,128)S(1)} %shard_map.68.refs_0_), channel_id=1, source_target_pairs={{0,8},{1,9},{12,4},{13,5},{2,10},{3,11},{14,6},{15,7},{16,24},{17,... | collective-permute-start | bytes 221192 | tf_op jit(solution)/shard_map/ppermute | solution.py:310
  13.1 5.0 %collective-permute-start = (f32[3,128,128]{2,1,0:T(8,128)}, f32[3,128,128]{2,1,0:T(8,128)S(1)}, u32[]{:S(2)}, u32[]{:S(2)}) collective-permute-start(f32[3,128,128]{2,1,0:T(8,128)} %refs_0_.1), channel_id=1, source_target_pairs={{5,9},{9,5},{7,11},{11,7},{21,25},{25,21},{23,27},{27,23}} | collective-permute-start | bytes 589832 | tf_op jit(solution)/shard_map/ppermute | solution.py:310
  13.8 6.0 %collective-permute-start.1 = (f32[3,128,128]{2,1,0:T(8,128)}, f32[3,128,128]{2,1,0:T(8,128)S(1)}, u32[]{:S(2)}, u32[]{:S(2)}) collective-permute-start(f32[3,128,128]{2,1,0:T(8,128)} %refs_0_.1), channel_id=1, source_target_pairs={{0,4},{1,9},{12,8},{13,5},{2,6},{3,11},{14,10},{15,7},{16,20},{17,... | collective-permute-start | bytes 589832 | tf_op jit(solution)/shard_map/ppermute | solution.py:310
  16.4 3.4 %collective-permute-start.5 = (f32[256,128]{1,0:T(8,128)S(1)}, f32[256,128]{1,0:T(8,128)S(1)}, u32[]{:S(2)}, u32[]{:S(2)}) collective-permute-start(f32[256,128]{1,0:T(8,128)S(1)} %get-tuple-element.22.refs_3_), channel_id=1, source_target_pairs={{0,1},{1,0},{2,3},{3,2},{4,5},{5,4},{6,7},{7,6},{8,9},{9,8},{10,11... | collective-permute-start | bytes 393224 | tf_op jit(solution)/shard_map/ppermute | solution.py:288
  19.8 0.9 %copy-start = (f32[3,128,128]{2,1,0:T(8,128)S(1)}, f32[3,128,128]{2,1,0:T(8,128)}, u32[]{:S(2)}) copy-start(f32[3,128,128]{2,1,0:T(8,128)} %refs_0_.1) | copy-start | bytes 589828
  23.9 2.5 %collective-permute-start.6 = (f32[256,256]{1,0:T(8,128)S(1)}, f32[256,256]{1,0:T(8,128)S(1)}, u32[]{:S(2)}, u32[]{:S(2)}) collective-permute-start(f32[256,256]{1,0:T(8,128)S(1)} %get-tuple-element.26.refs_2_), channel_id=1, source_target_pairs={{0,1},{1,0},{2,3},{3,2},{4,5},{5,4},{6,7},{7,6},{8,9},{9,8},{10,11... | collective-permute-start | bytes 786440 | tf_op jit(solution)/shard_map/ppermute | solution.py:288
  25.1 1.3 %collective-permute-start.7 = (f32[4,32,256]{2,1,0:T(8,128)S(1)}, f32[4,32,256]{2,1,0:T(8,128)S(1)}, u32[]{:S(2)}, u32[]{:S(2)}) collective-permute-start(f32[4,32,256]{2,1,0:T(8,128)S(1)} %get-tuple-element.27.refs_4_), channel_id=1, source_target_pairs={{0,1},{1,0},{2,3},{3,2},{4,5},{5,4},{6,7},{7,6},{8,9},{9,8},{10,11... | collective-permute-start | bytes 393224 | tf_op jit(solution)/shard_map/ppermute | solution.py:288
  29.1 1.4 %collective-permute-start.8 = (f32[264,128]{1,0:T(8,128)S(1)}, f32[264,128]{1,0:T(8,128)S(1)}, u32[]{:S(2)}, u32[]{:S(2)}) collective-permute-start(f32[264,128]{1,0:T(8,128)S(1)} %shard_map.72.grad_a), channel_id=1, source_target_pairs={{0,1},{1,0},{2,3},{3,2},{4,5},{5,4},{6,7},{7,6},{8,9},{9,8},{10,11... | collective-permute-start | bytes 405512 | tf_op jit(solution)/shard_map/ppermute | solution.py:288
  31.2 10.7 %collective-permute-start.9 = (f32[40,256]{1,0:T(8,128)S(1)}, f32[40,256]{1,0:T(8,128)S(1)}, u32[]{:S(2)}, u32[]{:S(2)}) collective-permute-start(f32[40,256]{1,0:T(8,128)S(1)} %get-tuple-element.29), channel_id=1, source_target_pairs={{4,0},{6,2},{8,12},{10,14},{5,1},{7,3},{9,13},{11,15},{20,16},{22,... | collective-permute-start | bytes 122888 | tf_op jit(solution)/shard_map/ppermute | solution.py:359
  32.5 2.0 %collective-permute-start.10 = (f32[40,128]{1,0:T(8,128)S(1)}, f32[40,128]{1,0:T(8,128)S(1)}, u32[]{:S(2)}, u32[]{:S(2)}) collective-permute-start(f32[40,128]{1,0:T(8,128)S(1)} %get-tuple-element.30), channel_id=1, source_target_pairs={{4,6},{6,4},{8,10},{10,8},{5,7},{7,5},{9,11},{11,9},{20,22},{22,20... | collective-permute-start | bytes 61448 | tf_op jit(solution)/shard_map/ppermute | solution.py:359
  33.1 8.7 %collective-permute-start.11 = (f32[40,128]{1,0:T(8,128)S(1)}, f32[40,128]{1,0:T(8,128)S(1)}, u32[]{:S(2)}, u32[]{:S(2)}) collective-permute-start(f32[40,128]{1,0:T(8,128)S(1)} %get-tuple-element.31), channel_id=1, source_target_pairs={{4,2},{6,0},{8,14},{10,12},{5,3},{7,1},{9,15},{11,13},{20,18},{22,... | collective-permute-start | bytes 61448 | tf_op jit(solution)/shard_map/ppermute | solution.py:359

commit v3 on v2

--- a/solution.py
+++ b/solution.py
@@ -1,4 +1,5 @@
 import functools
+import itertools
 import math
 
 import jax
@@ -57,18 +58,33 @@
     return jnp.where(low, same if side == 0 else other, other if side == 0 else same)
 
 
-def message_kernel(mask, goal, bands, weight, message):
+def fetch_kernel(mask, goal, bands, weight, phase, message, held, bands_in, weight_in, sems):
     rows = mask.shape[1]
     per_device, _, freqs = bands.shape
-    message[:rows] = mask[0]
-    message[rows : 2 * rows] = goal[0]
     message[2 * rows :] = jnp.zeros_like(message[2 * rows :])
+    copies = [
+        pltpu.make_async_copy(source, target, sems.at[n])
+        for n, (source, target) in enumerate(
+            (
+                (mask.at[0], message.at[pl.ds(0, rows)]),
+                (goal.at[0], message.at[pl.ds(rows, rows)]),
+                (bands, bands_in),
+                (weight, weight_in),
+                (phase, held),
+            )
+        )
+    ]
+    for copy in copies:
+        copy.start()
+    for copy in copies:
+        copy.wait()
     for i in range(per_device):
         for n in range(2):
-            message[2 * rows + i : 2 * rows + i + 1, n * freqs : (n + 1) * freqs] = bands[
+            message[2 * rows + i : 2 * rows + i + 1, n * freqs : (n + 1) * freqs] = bands_in[
                 i, n : n + 1, :
             ].astype(F32)
-    message[2 * rows + per_device : 2 * rows + per_device + 1, :per_device] = weight[...]
+    line = 2 * rows + per_device
+    message[line : line + 1, :per_device] = weight_in[...]
 
 
 def tables_kernel(fwd_h, fwd_l, adj_h, adj_l):
@@ -274,14 +290,35 @@
     source[...] = (mine(bodies, *term) + mine(edges, *term)) * term_scale
 
 
-def call(kernel, outs, scratch=(), kind=F32):
+def call(kernel, outs, scratch=(), kind=F32, hbm=False):
+    held = {"in_specs": [pl.BlockSpec(memory_space=pltpu.HBM)] * 5} if hbm else {}
     return pl.pallas_call(
         kernel,
         out_shape=[jax.ShapeDtypeStruct(shape, kind) for shape in outs],
         out_specs=[pl.BlockSpec(memory_space=pltpu.VMEM) for _ in outs],
-        scratch_shapes=[pltpu.VMEM(shape, scratch_kind) for shape, scratch_kind in scratch],
+        scratch_shapes=list(scratch),
         compiler_params=pltpu.CompilerParams(vmem_limit_bytes=VMEM_BUDGET),
-    )
+        **held,
+    )
+
+
+def permute(x, wanted):
+    shape = tuple(lax.axis_size(a) for a in ("src", "tile", "row"))
+    devices = list(itertools.product(*(range(n) for n in shape)))
+    pairs = dict(wanted)
+    sources = [d for d in devices if d not in pairs]
+    targets = [d for d in devices if d not in pairs.values()]
+
+    def cost(pair):
+        source, target = pair
+        hops = abs(source[0] - target[0]) + abs(source[1] - target[1])
+        return (source == target, hops, source, target)
+
+    for source, target in sorted(itertools.product(sources, targets), key=cost):
+        if source not in pairs and target not in pairs.values():
+            pairs[source] = target
+    flat = {d: n for n, d in enumerate(devices)}
+    return lax.ppermute(x, ("src", "tile", "row"), [(flat[a], flat[b]) for a, b in pairs.items()])
 
 
 def swap_rows(x):
@@ -299,25 +336,47 @@
     def chip(low, steps):
         return half - 1 - steps if low else half + steps
 
-    def to_hub(x, side, steps, cores=(0, 1)):
-        sides = dict.fromkeys(cores, side) if side is not None else {0: 0, 1: 1}
-        pairs = []
-        for low in (True, False):
-            for core, across in sides.items():
-                source, hub = chip(low, steps), chip(low != (across == 1), 0)
-                if source != hub:
-                    pairs.append((source * 2 + core, hub * 2 + core))
-        return lax.ppermute(x, ("src", "row"), pairs)
-
-    (message,) = call(message_kernel, [(2 * rows + PAD, pixels)])(
-        mask_windows,
-        target_windows,
-        pupil_bands.transpose(0, 2, 1),
-        source_weight.reshape(1, per_device),
+    cores = list(itertools.product(range(tile_count), range(2)))
+    halves = (True, False)
+
+    def to_hub(x, side, steps):
+        return permute(
+            x,
+            {
+                (chip(low, steps), t, c): (chip(low != (side == 1), 0), t, c)
+                for low in halves
+                for t, c in cores
+            },
+        )
+
+    def phases_to_hub(x, steps):
+        pairs = {}
+        for low, tile in itertools.product(halves, range(tile_count)):
+            if steps:
+                pairs[chip(low, steps), tile, 0] = chip(low, 0), tile, 0
+            pairs[chip(low, steps), tile, 1 if steps else 0] = chip(not low, 0), tile, 1
+        return permute(x, pairs)
+
+    pin = functools.partial(pltpu.with_memory_space_constraint, memory_space=pltpu.HBM)
+    message, phase = call(
+        fetch_kernel,
+        [(2 * rows + PAD, pixels), pupil_phase.shape],
+        [
+            pltpu.VMEM((per_device, 2, freqs), jnp.int32),
+            pltpu.VMEM((1, per_device), F32),
+            pltpu.SemaphoreType.DMA((5,)),
+        ],
+        hbm=True,
+    )(
+        pin(mask_windows),
+        pin(target_windows),
+        pin(pupil_bands.transpose(0, 2, 1)),
+        pin(source_weight.reshape(1, per_device)),
+        pin(pupil_phase),
     )
     blocks = [message] + [to_hub(message, 0, n) for n in range(1, half)]
-    blocks += [to_hub(message, 1, n) for n in range(half)]
-    phases = [to_hub(pupil_phase, None, n) for n in range(half)]
+    blocks += [to_hub(message, 1, n) for n in reversed(range(half))][::-1]
+    phases = [phases_to_hub(phase, n) for n in reversed(range(half))][::-1]
     tables = call(
         tables_kernel, [(2 * freqs, 2 * pixels)] * 2 + [(2 * pixels, 2 * freqs)] * 2, kind=BF16
     )()
@@ -325,7 +384,7 @@
     spec, goal, meta = call(
         functools.partial(spectrum_kernel, half),
         [(2 * freqs, freqs), (src_count, rows, pixels), (half, PAD, pixels)],
-        [((2 * pixels, freqs), F32)],
+        [pltpu.VMEM((2 * pixels, freqs), F32)],
     )(*blocks, *tables)
     spec_other = swap_rows(spec)
     goal_other = swap_rows(goal)
@@ -333,14 +392,15 @@
     field, pupil, inten = call(
         functools.partial(fields_kernel, per_device, sources, half),
         [(count, pixels, 2 * pixels), (count, 2 * freqs, freqs), (pixels, pixels)],
-        [((2 * freqs, count * freqs), BF16)] * 2,
-    )(pupil_phase, *phases, spec, spec_other, meta, *tables)
+        [pltpu.VMEM((2 * freqs, count * freqs), BF16)] * 2,
+    )(phase, *phases, spec, spec_other, meta, *tables)
     inten_other = swap_rows(inten)
 
     (grad,) = call(
         functools.partial(adjoint_kernel, per_device, sources),
         [(2 * freqs + PAD, freqs)],
-        [((pixels, pixels), F32)] + [((2 * pixels, count * freqs), BF16)] * 2,
+        [pltpu.VMEM((pixels, pixels), F32)]
+        + [pltpu.VMEM((2 * pixels, count * freqs), BF16)] * 2,
     )(field, pupil, inten, inten_other, goal, goal_other, meta, *tables)
     grad_other = swap_rows(grad)
 
@@ -351,12 +411,14 @@
     bodies, edges = outs[:half], outs[half:]
 
     def from_hub(x, steps, flip):
-        pairs = []
-        for low in (True, False):
-            for tile in range(2):
-                target = tile ^ 1 if flip else tile
-                pairs.append((chip(low, 0) * 2 + tile, chip(low, steps) * 2 + target))
-        return lax.ppermute(x, ("src", "tile"), pairs)
+        return permute(
+            x,
+            {
+                (chip(low, 0), t, c): (chip(low, steps), 1 - t if flip else t, c)
+                for low in halves
+                for t, c in cores
+            },
+        )
 
     bodies = [bodies[0]] + [from_hub(bodies[n], n, False) for n in range(1, half)]
     edges = [from_hub(edges[n], n, True) for n in range(half)]

time: 43 us -> 31.3 us (0.73)
  starting transfers between devices: 18.4 us -> 10.9 us
  local copies, waits for them, and re-layouts: 3.77 us -> 0 us
  waiting for transfers between devices: 11.3 us -> 10.3 us
  Pallas kernels: 8.28 us -> 9.17 us
    ppermute x8, starting transfers between devices: 14.9 us -> 10.1 us  [permute(): lax.ppermute(x, ('src', 'tile', 'row'), [(flat[a], flat[b]) for a, b in p...]
    unnamed x10 -> x0, local copies, waits for them, and re-layouts: 3.77 us -> none
    ppermute x4, starting transfers between devices: 3.46 us -> 0.85 us  [swap_rows(): return lax.ppermute(x, 'row', [(0, 1), (1, 0)])]
    ppermute x8, waiting for transfers between devices: 9.06 us -> 7.89 us  [permute(): lax.ppermute(x, ('src', 'tile', 'row'), [(flat[a], flat[b]) for a, b in p...]
    pallas_call x1, Pallas kernels: 0.01 us -> 1.05 us  [hub_shards(): call(fetch_kernel, [(2 * rows + PAD, pixels), pupil_phase.shape], [pltpu....]
  transfers between devices with their start and end apart: 12 -> 12, of which waited for: 4 -> 5; matrix products, arithmetic and copies ran while one was open for 0% -> 0% of each run, Pallas kernels for 3% -> 4%
where the time goes in v3:
time: 31.3 us; the launch traced here: 31.1 us
  starting transfers between devices  10.9 us (35%)
  waiting for transfers between devices  10.3 us (33%)
  Pallas kernels  9.17 us (29%)
  between operations  0.71 us (2%)
    ppermute x8, starting transfers between devices, permute(): lax.ppermute(x, ('src', 'tile', 'row'), [(flat[a], flat[b]) for a, b in p...  10.1 us
    ppermute x8, waiting for transfers between devices, permute(): lax.ppermute(x, ('src', 'tile', 'row'), [(flat[a], flat[b]) for a, b in p...  7.89 us
    pallas_call x1, Pallas kernels, hub_shards(): call(functools.partial(fields_kernel, per_device, sources, half), [(count...  3.15 us
    pallas_call x1, Pallas kernels, hub_shards(): call(functools.partial(adjoint_kernel, per_device, sources), [(2 * freqs...  2.52 us
    ppermute x4, waiting for transfers between devices, swap_rows(): return lax.ppermute(x, 'row', [(0, 1), (1, 0)])  2.43 us
    pallas_call x1, Pallas kernels, hub_shards(): call(fetch_kernel, [(2 * rows + PAD, pixels), pupil_phase.shape], [pltpu....  1.05 us
    ppermute x4, starting transfers between devices, swap_rows(): return lax.ppermute(x, 'row', [(0, 1), (1, 0)])  0.85 us
    pallas_call x1, Pallas kernels, hub_shards(): call(functools.partial(place_kernel, half, 1.0 / (sources * pixels * tile...  0.7 us
  transfers between devices with their start and end apart: 12, of which 5 were waited for; matrix products, arithmetic and copies ran while one was open for 0% of the time, Pallas kernels for 4%

profile of v3, /device:TPU:0, one launch (start us, length us, event | category | flops | bytes accessed | tf_op | source)
XLA Modules:
  0.0 31.1 jit_solution(1026156643706167664)
XLA Ops:
  0.6 1.0 %shard_map.68 = (f32[72,256]{1,0:T(8,128)S(1)}, f32[3,128,128]{2,1,0:T(8,128)S(1)}) custom-call(f32[1,32,256]{2,1,0:T(8,128)} %mask.1, f32[1,32,256]{2,1,0:T(8,128)} %goal.1, s32[3,2,128]{2,1,0:T(2,128)} %bitcast.3, f32[1,3]{1,0:T(1,128)} %bitcast.4, f32[3,128,128]{2,1,0:T(8,128)} %phase.1), custom_call_target="tpu_custom_call" | custom-call | tf_op jit(solution)/shard_map/pallas_call | solution.py:361
  1.7 3.1 %collective-permute-start.2 = (f32[72,256]{1,0:T(8,128)S(1)}, f32[72,256]{1,0:T(8,128)S(1)}, u32[]{:S(2)}, u32[]{:S(2)}) collective-permute-start(f32[72,256]{1,0:T(8,128)S(1)} %get-tuple-element.21.refs_0_), channel_id=1, source_target_pairs={{0,4},{1,5},{2,6},{3,7},{12,8},{13,9},{14,10},{15,11},{4,0},{5,1},... | collective-permute-start | bytes 221192 | tf_op jit(solution)/shard_map/ppermute | solution.py:321
  4.8 0.0 collective-permute-start.3
  4.8 2.6 %collective-permute-start.4 = (f32[72,256]{1,0:T(8,128)S(1)}, f32[72,256]{1,0:T(8,128)S(1)}, u32[]{:S(2)}, u32[]{:S(2)}) collective-permute-start(f32[72,256]{1,0:T(8,128)S(1)} %get-tuple-element.21.refs_0_), channel_id=1, source_target_pairs={{0,8},{1,9},{2,10},{3,11},{12,4},{13,5},{14,6},{15,7},{4,0},{5,1},... | collective-permute-start | bytes 221192 | tf_op jit(solution)/shard_map/ppermute | solution.py:321
  7.4 0.0 collective-permute-start
  7.4 0.8 %collective-permute-start.1 = (f32[3,128,128]{2,1,0:T(8,128)S(1)}, f32[3,128,128]{2,1,0:T(8,128)S(1)}, u32[]{:S(2)}, u32[]{:S(2)}) collective-permute-start(f32[3,128,128]{2,1,0:T(8,128)S(1)} %get-tuple-element.20.refs_0_), channel_id=1, source_target_pairs={{0,4},{1,9},{2,6},{3,11},{12,8},{13,5},{14,10},{15,7},{4,0},{5,1},... | collective-permute-start | bytes 589832 | tf_op jit(solution)/shard_map/ppermute | solution.py:321
  8.2 0.4 %shard_map.69 = (bf16[256,512]{1,0:T(8,128)(2,1)S(1)}, bf16[256,512]{1,0:T(8,128)(2,1)S(1)}, bf16[512,256]{1,0:T(8,128)(2,1)S(1)}, bf16[512,256]{1,0:T(8,128)(2,1)S(1)}) custom-call(), custom_call_target="tpu_custom_call" | custom-call | tf_op jit(solution)/shard_map/pallas_call | solution.py:380
  8.7 0.0 collective-permute-done.2.refs_1_
  8.7 0.0 collective-permute-done.3.refs_2_
  8.7 1.6 %collective-permute-done.4.refs_3_ = f32[72,256]{1,0:T(8,128)S(1)} collective-permute-done((f32[72,256]{1,0:T(8,128)S(1)}, f32[72,256]{1,0:T(8,128)S(1)}, u32[]{:S(2)}, u32[]{:S(2)}) %collective-permute-start.4) | collective-permute-done | bytes 73760 | tf_op jit(solution)/shard_map/ppermute | solution.py:321
  10.3 0.7 %shard_map.70 = (f32[256,128]{1,0:T(8,128)S(1)}, f32[4,32,256]{2,1,0:T(8,128)S(1)}, f32[2,8,256]{2,1,0:T(8,128)S(1)}) custom-call(f32[72,256]{1,0:T(8,128)S(1)} %get-tuple-element.21.refs_0_, f32[72,256]{1,0:T(8,128)S(1)} %collective-permute-done.2.refs_1_, f32[72,256]{1,0:T(8,128)S(1)} %collective-permute-done.3.refs_2_, ...), custom_call_target="tpu_custom_call" | custom-call | tf_op jit(solution)/shard_map/pallas_call | solution.py:384
  11.0 0.1 collective-permute-start.5
  11.0 0.0 collective-permute-done.refs_1_
  11.0 3.6 %collective-permute-done.1.refs_2_ = f32[3,128,128]{2,1,0:T(8,128)S(1)} collective-permute-done((f32[3,128,128]{2,1,0:T(8,128)S(1)}, f32[3,128,128]{2,1,0:T(8,128)S(1)}, u32[]{:S(2)}, u32[]{:S(2)}) %collective-permute-start.1) | collective-permute-done | bytes 196640 | tf_op jit(solution)/shard_map/ppermute | solution.py:321
  14.7 0.0 collective-permute-done.5.refs_4_
  14.7 3.2 %shard_map.71 = (f32[6,256,512]{2,1,0:T(8,128)S(1)}, f32[6,256,128]{2,1,0:T(8,128)S(1)}, f32[256,256]{1,0:T(8,128)S(1)}) custom-call(f32[3,128,128]{2,1,0:T(8,128)S(1)} %get-tuple-element.20.refs_0_, f32[3,128,128]{2,1,0:T(8,128)S(1)} %collective-permute-done.refs_1_, f32[3,128,128]{2,1,0:T(8,128)S(1)} %collective-permute-done.1.refs_2_, ...), custom_call_target="tpu_custom_call" | custom-call | tf_op jit(solution)/shard_map/pallas_call | solution.py:392
  17.8 0.1 collective-permute-start.6
  17.9 0.5 %collective-permute-start.7 = (f32[4,32,256]{2,1,0:T(8,128)S(1)}, f32[4,32,256]{2,1,0:T(8,128)S(1)}, u32[]{:S(2)}, u32[]{:S(2)}) collective-permute-start(f32[4,32,256]{2,1,0:T(8,128)S(1)} %get-tuple-element.31.refs_4_), channel_id=1, source_target_pairs={{0,1},{1,0},{2,3},{3,2},{4,5},{5,4},{6,7},{7,6},{8,9},{9,8},{10,11... | collective-permute-start | bytes 393224 | tf_op jit(solution)/shard_map/ppermute | solution.py:325
  18.4 1.2 %collective-permute-done.7.refs_5_ = f32[4,32,256]{2,1,0:T(8,128)S(1)} collective-permute-done((f32[4,32,256]{2,1,0:T(8,128)S(1)}, f32[4,32,256]{2,1,0:T(8,128)S(1)}, u32[]{:S(2)}, u32[]{:S(2)}) %collective-permute-start.7) | collective-permute-done | bytes 131104 | tf_op jit(solution)/shard_map/ppermute | solution.py:325
  19.6 0.0 collective-permute-done.6.refs_3_
  19.6 2.5 %shard_map.72.grad_a = f32[264,128]{1,0:T(8,128)S(1)} custom-call(f32[6,256,512]{2,1,0:T(8,128)S(1)} %get-tuple-element.28.refs_0_, f32[6,256,128]{2,1,0:T(8,128)S(1)} %get-tuple-element.29.refs_1_, f32[256,256]{1,0:T(8,128)S(1)} %get-tuple-element.30.refs_2_, f32[256,256]{1,0:T(8,128)S(1)} %collective-permute-done.6.refs_3_, ...), custom_call_target="tpu_custom_call" | custom-call | tf_op jit(solution)/shard_map/pallas_call | solution.py:399
  22.2 0.2 collective-permute-start.8
  22.4 1.2 %collective-permute-done.8.grad_b = f32[264,128]{1,0:T(8,128)S(1)} collective-permute-done((f32[264,128]{1,0:T(8,128)S(1)}, f32[264,128]{1,0:T(8,128)S(1)}, u32[]{:S(2)}, u32[]{:S(2)}) %collective-permute-start.8) | collective-permute-done | bytes 135200 | tf_op jit(solution)/shard_map/ppermute | solution.py:325
  23.6 0.6 %shard_map.73 = (f32[40,256]{1,0:T(8,128)S(1)}, f32[40,256]{1,0:T(8,128)S(1)}, f32[40,128]{1,0:T(8,128)S(1)}, f32[40,128]{1,0:T(8,128)S(1)}) custom-call(f32[264,128]{1,0:T(8,128)S(1)} %shard_map.72.grad_a, f32[264,128]{1,0:T(8,128)S(1)} %collective-permute-done.8.grad_b, bf16[256,512]{1,0:T(8,128)(2,1)S(1)} %get-tuple-element.22.refs_4_.refs_6_.refs_7_.fwd_h, ...), custom_call_target="tpu_custom_call" | custom-call | tf_op jit(solution)/shard_map/pallas_call | solution.py:407
  24.2 1.5 %collective-permute-start.9 = (f32[40,256]{1,0:T(8,128)S(1)}, f32[40,256]{1,0:T(8,128)S(1)}, u32[]{:S(2)}, u32[]{:S(2)}) collective-permute-start(f32[40,256]{1,0:T(8,128)S(1)} %get-tuple-element.33), channel_id=1, source_target_pairs={{4,0},{5,1},{6,2},{7,3},{8,12},{9,13},{10,14},{11,15},{0,4},{1,5},... | collective-permute-start | bytes 122888 | tf_op jit(solution)/shard_map/ppermute | solution.py:321
  25.7 0.0 collective-permute-start.10
  25.7 2.0 %collective-permute-start.11 = (f32[40,128]{1,0:T(8,128)S(1)}, f32[40,128]{1,0:T(8,128)S(1)}, u32[]{:S(2)}, u32[]{:S(2)}) collective-permute-start(f32[40,128]{1,0:T(8,128)S(1)} %get-tuple-element.35), channel_id=1, source_target_pairs={{4,2},{5,3},{6,0},{7,1},{8,14},{9,15},{10,12},{11,13},{0,4},{1,5},... | collective-permute-start | bytes 61448 | tf_op jit(solution)/shard_map/ppermute | solution.py:321
  27.8 0.0 collective-permute-done.10.refs_2_
  27.8 2.7 %collective-permute-done.11.refs_3_ = f32[40,128]{1,0:T(8,128)S(1)} collective-permute-done((f32[40,128]{1,0:T(8,128)S(1)}, f32[40,128]{1,0:T(8,128)S(1)}, u32[]{:S(2)}, u32[]{:S(2)}) %collective-permute-start.11) | collective-permute-done | bytes 20512 | tf_op jit(solution)/shard_map/ppermute | solution.py:321
  30.4 0.0 collective-permute-done.9.refs_1_
  30.4 0.7 %shard_map.74 = (f32[1,32,256]{2,1,0:T(8,128)}, f32[1,3]{1,0:T(1,128)}) custom-call(f32[40,256]{1,0:T(8,128)S(1)} %get-tuple-element.32.refs_0_, f32[40,256]{1,0:T(8,128)S(1)} %collective-permute-done.9.refs_1_, f32[40,128]{1,0:T(8,128)S(1)} %collective-permute-done.10.refs_2_, f32[40,128]{1,0:T(8,128)S(1)} %collective-permute-done.11.refs_3_), custom_call_target="tpu_custom_call" | custom-call | tf_op jit(solution)/shard_map/pallas_call | solution.py:425
Async XLA Ops:
  1.7 7.0 %collective-permute-start.2 = (f32[72,256]{1,0:T(8,128)S(1)}, f32[72,256]{1,0:T(8,128)S(1)}, u32[]{:S(2)}, u32[]{:S(2)}) collective-permute-start(f32[72,256]{1,0:T(8,128)S(1)} %get-tuple-element.21.refs_0_), channel_id=1, source_target_pairs={{0,4},{1,5},{2,6},{3,7},{12,8},{13,9},{14,10},{15,11},{4,0},{5,1},... | collective-permute-start | bytes 221192 | tf_op jit(solution)/shard_map/ppermute | solution.py:321
  4.8 3.9 %collective-permute-start.3 = (f32[72,256]{1,0:T(8,128)S(1)}, f32[72,256]{1,0:T(8,128)S(1)}, u32[]{:S(2)}, u32[]{:S(2)}) collective-permute-start(f32[72,256]{1,0:T(8,128)S(1)} %get-tuple-element.21.refs_0_), channel_id=1, source_target_pairs={{4,8},{5,9},{6,10},{7,11},{8,4},{9,5},{10,6},{11,7},{0,1},{1,0},{2... | collective-permute-start | bytes 221192 | tf_op jit(solution)/shard_map/ppermute | solution.py:321
  4.8 5.5 %collective-permute-start.4 = (f32[72,256]{1,0:T(8,128)S(1)}, f32[72,256]{1,0:T(8,128)S(1)}, u32[]{:S(2)}, u32[]{:S(2)}) collective-permute-start(f32[72,256]{1,0:T(8,128)S(1)} %get-tuple-element.21.refs_0_), channel_id=1, source_target_pairs={{0,8},{1,9},{2,10},{3,11},{12,4},{13,5},{14,6},{15,7},{4,0},{5,1},... | collective-permute-start | bytes 221192 | tf_op jit(solution)/shard_map/ppermute | solution.py:321
  7.4 3.7 %collective-permute-start = (f32[3,128,128]{2,1,0:T(8,128)S(1)}, f32[3,128,128]{2,1,0:T(8,128)S(1)}, u32[]{:S(2)}, u32[]{:S(2)}) collective-permute-start(f32[3,128,128]{2,1,0:T(8,128)S(1)} %get-tuple-element.20.refs_0_), channel_id=1, source_target_pairs={{4,9},{6,11},{8,5},{10,7},{0,1},{1,0},{2,3},{3,2},{5,4},{7,6},{9,8... | collective-permute-start | bytes 589832 | tf_op jit(solution)/shard_map/ppermute | solution.py:321
  7.4 7.3 %collective-permute-start.1 = (f32[3,128,128]{2,1,0:T(8,128)S(1)}, f32[3,128,128]{2,1,0:T(8,128)S(1)}, u32[]{:S(2)}, u32[]{:S(2)}) collective-permute-start(f32[3,128,128]{2,1,0:T(8,128)S(1)} %get-tuple-element.20.refs_0_), channel_id=1, source_target_pairs={{0,4},{1,9},{2,6},{3,11},{12,8},{13,5},{14,10},{15,7},{4,0},{5,1},... | collective-permute-start | bytes 589832 | tf_op jit(solution)/shard_map/ppermute | solution.py:321
  11.0 3.7 %collective-permute-start.5 = (f32[256,128]{1,0:T(8,128)S(1)}, f32[256,128]{1,0:T(8,128)S(1)}, u32[]{:S(2)}, u32[]{:S(2)}) collective-permute-start(f32[256,128]{1,0:T(8,128)S(1)} %get-tuple-element.26.refs_3_), channel_id=1, source_target_pairs={{0,1},{1,0},{2,3},{3,2},{4,5},{5,4},{6,7},{7,6},{8,9},{9,8},{10,11... | collective-permute-start | bytes 393224 | tf_op jit(solution)/shard_map/ppermute | solution.py:325
  17.8 1.8 %collective-permute-start.6 = (f32[256,256]{1,0:T(8,128)S(1)}, f32[256,256]{1,0:T(8,128)S(1)}, u32[]{:S(2)}, u32[]{:S(2)}) collective-permute-start(f32[256,256]{1,0:T(8,128)S(1)} %get-tuple-element.30.refs_2_), channel_id=1, source_target_pairs={{0,1},{1,0},{2,3},{3,2},{4,5},{5,4},{6,7},{7,6},{8,9},{9,8},{10,11... | collective-permute-start | bytes 786440 | tf_op jit(solution)/shard_map/ppermute | solution.py:325
  17.9 1.7 %collective-permute-start.7 = (f32[4,32,256]{2,1,0:T(8,128)S(1)}, f32[4,32,256]{2,1,0:T(8,128)S(1)}, u32[]{:S(2)}, u32[]{:S(2)}) collective-permute-start(f32[4,32,256]{2,1,0:T(8,128)S(1)} %get-tuple-element.31.refs_4_), channel_id=1, source_target_pairs={{0,1},{1,0},{2,3},{3,2},{4,5},{5,4},{6,7},{7,6},{8,9},{9,8},{10,11... | collective-permute-start | bytes 393224 | tf_op jit(solution)/shard_map/ppermute | solution.py:325
  22.2 1.4 %collective-permute-start.8 = (f32[264,128]{1,0:T(8,128)S(1)}, f32[264,128]{1,0:T(8,128)S(1)}, u32[]{:S(2)}, u32[]{:S(2)}) collective-permute-start(f32[264,128]{1,0:T(8,128)S(1)} %shard_map.72.grad_a), channel_id=1, source_target_pairs={{0,1},{1,0},{2,3},{3,2},{4,5},{5,4},{6,7},{7,6},{8,9},{9,8},{10,11... | collective-permute-start | bytes 405512 | tf_op jit(solution)/shard_map/ppermute | solution.py:325
  24.2 6.2 %collective-permute-start.9 = (f32[40,256]{1,0:T(8,128)S(1)}, f32[40,256]{1,0:T(8,128)S(1)}, u32[]{:S(2)}, u32[]{:S(2)}) collective-permute-start(f32[40,256]{1,0:T(8,128)S(1)} %get-tuple-element.33), channel_id=1, source_target_pairs={{4,0},{5,1},{6,2},{7,3},{8,12},{9,13},{10,14},{11,15},{0,4},{1,5},... | collective-permute-start | bytes 122888 | tf_op jit(solution)/shard_map/ppermute | solution.py:321
  25.7 2.0 %collective-permute-start.10 = (f32[40,128]{1,0:T(8,128)S(1)}, f32[40,128]{1,0:T(8,128)S(1)}, u32[]{:S(2)}, u32[]{:S(2)}) collective-permute-start(f32[40,128]{1,0:T(8,128)S(1)} %get-tuple-element.34), channel_id=1, source_target_pairs={{4,6},{5,7},{6,4},{7,5},{8,10},{9,11},{10,8},{11,9},{0,1},{1,0},{2... | collective-permute-start | bytes 61448 | tf_op jit(solution)/shard_map/ppermute | solution.py:321
  25.7 4.7 %collective-permute-start.11 = (f32[40,128]{1,0:T(8,128)S(1)}, f32[40,128]{1,0:T(8,128)S(1)}, u32[]{:S(2)}, u32[]{:S(2)}) collective-permute-start(f32[40,128]{1,0:T(8,128)S(1)} %get-tuple-element.35), channel_id=1, source_target_pairs={{4,2},{5,3},{6,0},{7,1},{8,14},{9,15},{10,12},{11,13},{0,4},{1,5},... | collective-permute-start | bytes 61448 | tf_op jit(solution)/shard_map/ppermute | solution.py:321

commit v4 on v3

--- a/solution.py
+++ b/solution.py
@@ -111,8 +111,8 @@
         table[pixels:, freqs:] = cos
 
 
-def spectrum_kernel(half, *refs):
-    blocks = refs[: 2 * half]
+def spectrum_kernel(half, order, *refs):
+    blocks = [refs[order.index(d)] for d in range(2 * half)]
     fwd_h, fwd_l, adj_h, adj_l, spec, goal, meta, part = refs[2 * half :]
     rows, pixels = goal.shape[1], goal.shape[2]
     freqs = spec.shape[1]
@@ -132,73 +132,92 @@
     spec[...] = mm3((fwd_h[...], fwd_l[...]), split(part[...]))
 
 
-def fields_kernel(per_device, sources, slots, *refs):
-    phase_own, *phases = refs[: slots + 1]
-    spec_a, spec_b, meta, fwd_h, fwd_l, adj_h, adj_l = refs[slots + 1 : slots + 8]
-    field, pupil, intensity, amp_h, amp_l = refs[slots + 8 :]
+def weight_of(meta, source, per_device):
+    j, i = divmod(source, per_device)
+    return meta[j][per_device : per_device + 1, i : i + 1]
+
+
+def fields_kernel(per_device, sources, first_row, slots, *refs):
     row = lax.axis_index("row")
-    pixels = intensity.shape[1]
-    freqs = spec_a.shape[1]
-    spec = (spec_a[...] + spec_b[...]) * (1.0 / (pixels * freqs))
-    spec_r, spec_i = spec[:freqs], spec[freqs:]
-    column = lax.broadcasted_iota(jnp.int32, (freqs, freqs), 1).astype(F32)
-    weight = []
-    for j in range(slots):
-        info = meta[j]
-        bounds = info.T
-        for i in range(per_device):
-            s = j * per_device + i
-            weight.append(info[per_device : per_device + 1, i : i + 1] * (1.0 / sources))
-            inside = (column >= bounds[:freqs, i : i + 1]) & (
-                column < bounds[freqs : 2 * freqs, i : i + 1]
-            )
-            phase = phases[j][i]
-            if j == 0:
-                phase = jnp.where(row == 0, phase_own[i], phase)
-            sin_p, cos_p = sincos(phase)
-            pass_r = jnp.where(inside, cos_p, 0.0)
-            pass_i = jnp.where(inside, sin_p, 0.0)
-            pupil[s, :freqs] = pass_r
-            pupil[s, freqs:] = pass_i
-            lanes = slice(s * freqs, (s + 1) * freqs)
-            for half, value in enumerate(
-                (pass_r * spec_r - pass_i * spec_i, pass_i * spec_r + pass_r * spec_i)
-            ):
-                high, low = split(value)
-                amp_h[half * freqs : (half + 1) * freqs, lanes] = high
-                amp_l[half * freqs : (half + 1) * freqs, lanes] = low
-    total = jnp.zeros_like(intensity)
-    group = 2
-    for first in range(0, slots * per_device, group):
-        members = range(first, min(first + group, slots * per_device))
+    if first_row == 0:
+        phase_own, *phases = refs[: slots + 1]
+        spec_a, spec_b, meta, goal, fwd_h, fwd_l, adj_h, adj_l = refs[slots + 1 : -7]
+        field, intensity, pupil, amp_h, amp_l, half_h, half_l = refs[-7:]
+    else:
+        meta, goal, amp_h, amp_l, fwd_h, fwd_l, adj_h, adj_l, field, intensity, *half_refs = refs
+        half_h, half_l = half_refs
+    rows, pixels = field.shape[1], intensity.shape[1]
+    count, freqs = field.shape[0], amp_h.shape[1] // field.shape[0]
+    if first_row == 0:
+        spec = (spec_a[...] + spec_b[...]) * (1.0 / (pixels * freqs))
+        spec_r, spec_i = spec[:freqs], spec[freqs:]
+        column = lax.broadcasted_iota(jnp.int32, (freqs, freqs), 1).astype(F32)
+        bounds = [meta[j].T for j in range(slots)]
+
+    def amplitude(s):
+        j, i = divmod(s, per_device)
+        inside = (column >= bounds[j][:freqs, i : i + 1]) & (
+            column < bounds[j][freqs : 2 * freqs, i : i + 1]
+        )
+        phase = phases[j][i]
+        if j == 0:
+            phase = jnp.where(row == 0, phase_own[i], phase)
+        sin_p, cos_p = sincos(phase)
+        pass_r = jnp.where(inside, cos_p, 0.0)
+        pass_i = jnp.where(inside, sin_p, 0.0)
+        pupil[s, :freqs] = pass_r
+        pupil[s, freqs:] = pass_i
+        lanes = slice(s * freqs, (s + 1) * freqs)
+        for half, value in enumerate(
+            (pass_r * spec_r - pass_i * spec_i, pass_i * spec_r + pass_r * spec_i)
+        ):
+            high, low = split(value)
+            amp_h[half * freqs : (half + 1) * freqs, lanes] = high
+            amp_l[half * freqs : (half + 1) * freqs, lanes] = low
+
+    here, there = (slice(n, n + rows) for n in (first_row, pixels + first_row))
+    waves = [jnp.concatenate([t[here], t[there]], axis=0) for t in (adj_h, adj_l)]
+    for first in range(0, count, 2):
+        members = range(first, min(first + 2, count))
+        if first_row == 0:
+            for s in members:
+                amplitude(s)
         lanes = slice(first * freqs, (members[-1] + 1) * freqs)
-        half = mm3((adj_h[...], adj_l[...]), (amp_h[:, lanes], amp_l[:, lanes]))
+        half = mm3(waves, (amp_h[:, lanes], amp_l[:, lanes]))
         for n, s in enumerate(members):
-            lanes = slice(n * freqs, (n + 1) * freqs)
-            pair = jnp.concatenate([half[:pixels, lanes], half[pixels:, lanes]], axis=1)
-            out = mm3(split(pair), (fwd_h[...], fwd_l[...]))
-            field[s] = out
-            out_r, out_i = out[:, :pixels], out[:, pixels:]
-            total = total + weight[s] * (out_r * out_r + out_i * out_i)
-    intensity[...] = total
-
-
-def adjoint_kernel(per_device, sources, *refs):
-    (field, pupil, inten_a, inten_b, goal_a, goal_b, meta, fwd_h, fwd_l, adj_h, adj_l) = refs[:11]
-    grad, cot_ref, back_h, back_l = refs[11:]
-    src_count, rows = goal_a.shape[0], goal_a.shape[1]
-    pixels = inten_a.shape[1]
-    freqs = grad.shape[1]
+            for m in range(2):
+                high, low = split(half[m * rows : (m + 1) * rows, n * freqs : (n + 1) * freqs])
+                half_h[s * rows : (s + 1) * rows, m * freqs : (m + 1) * freqs] = high
+                half_l[s * rows : (s + 1) * rows, m * freqs : (m + 1) * freqs] = low
+    out = mm3((half_h[...], half_l[...]), (fwd_h[...], fwd_l[...]))
+    total = jnp.zeros((rows, pixels), F32)
+    for s in range(count):
+        value = out[s * rows : (s + 1) * rows]
+        field[s] = value
+        out_r, out_i = value[:, :pixels], value[:, pixels:]
+        weight = weight_of(meta, s, per_device) * (1.0 / sources)
+        total = total + weight * (out_r * out_r + out_i * out_i)
+    intensity[:rows] = total
+    block = goal.shape[1]
+    for n in range(rows // (2 * block)):
+        place = rows + n * block
+        intensity[place : place + block] = goal[first_row // (2 * block) + n]
+
+
+def adjoint_kernel(per_device, sources, first_row, block, *refs):
+    *before, field, pupil, light_a, light_b, meta = refs[:-8]
+    fwd_h, fwd_l, adj_h, adj_l, grad, cot_ref, back_h, back_l = refs[-8:]
+    rows, pixels = cot_ref.shape
+    count, freqs = field.shape[0], grad.shape[1]
     row = lax.axis_index("row")
-    for z in range(src_count):
-        for r in range(2):
-            here = slice((2 * z + r) * rows, (2 * z + r + 1) * rows)
-            goal = jnp.where(row == r, goal_a[z], goal_b[z])
-            intensity = inten_a[here] + inten_b[here]
-            resist = 1.0 / (1.0 + jnp.exp(-STEEPNESS * (intensity - THRESHOLD)))
-            cot_ref[here] = (LOSS_SCALE * STEEPNESS) * (resist - goal) * resist * (1.0 - resist)
+    for n in range(rows // block):
+        here = slice(n * block, (n + 1) * block)
+        place = slice(rows + n // 2 * block, rows + (n // 2 + 1) * block)
+        goal = jnp.where(row == n % 2, light_a[place], light_b[place])
+        intensity = light_a[here] + light_b[here]
+        resist = 1.0 / (1.0 + jnp.exp(-STEEPNESS * (intensity - THRESHOLD)))
+        cot_ref[here] = (LOSS_SCALE * STEEPNESS) * (resist - goal) * resist * (1.0 - resist)
     cot = cot_ref[...]
-    count = field.shape[0]
     line = lax.broadcasted_iota(jnp.int32, (PAD, freqs), 0)
     lane = lax.broadcasted_iota(jnp.int32, (PAD, freqs), 1)
     terms = jnp.zeros((PAD, freqs), F32)
@@ -214,28 +233,29 @@
         lanes = slice(s * freqs, (s + 1) * freqs)
         for n in range(2):
             high, low = split(half[:, n * freqs : (n + 1) * freqs])
-            back_h[n * pixels : (n + 1) * pixels, lanes] = high
-            back_l[n * pixels : (n + 1) * pixels, lanes] = low
+            back_h[n * rows : (n + 1) * rows, lanes] = high
+            back_l[n * rows : (n + 1) * rows, lanes] = low
     grad_r = jnp.zeros((freqs, freqs), F32)
     grad_i = jnp.zeros((freqs, freqs), F32)
-    group = 2
-    for first in range(0, count, group):
-        members = range(first, min(first + group, count))
+    here, there = (slice(n, n + rows) for n in (first_row, pixels + first_row))
+    waves = [jnp.concatenate([t[:, here], t[:, there]], axis=1) for t in (fwd_h, fwd_l)]
+    for first in range(0, count, 2):
+        members = range(first, min(first + 2, count))
         lanes = slice(first * freqs, (members[-1] + 1) * freqs)
-        out = mm3((fwd_h[...], fwd_l[...]), (back_h[:, lanes], back_l[:, lanes]))
+        out = mm3(waves, (back_h[:, lanes], back_l[:, lanes]))
         for n, s in enumerate(members):
             lanes = slice(n * freqs, (n + 1) * freqs)
-            j, i = divmod(s, per_device)
-            weight = meta[j][per_device : per_device + 1, i : i + 1] * (
-                2.0 / (sources * pixels * freqs)
-            )
+            weight = weight_of(meta, s, per_device) * (2.0 / (sources * pixels * freqs))
             pass_r, pass_i = weight * pupil[s, :freqs], weight * pupil[s, freqs:]
             out_r, out_i = out[:freqs, lanes], out[freqs:, lanes]
             grad_r = grad_r + (pass_r * out_r + pass_i * out_i)
             grad_i = grad_i + (pass_r * out_i - pass_i * out_r)
-    grad[:freqs] = grad_r
-    grad[freqs : 2 * freqs] = grad_i
-    grad[2 * freqs :] = terms
+    for place, value in (
+        (slice(0, freqs), grad_r),
+        (slice(freqs, 2 * freqs), grad_i),
+        (slice(2 * freqs, 2 * freqs + PAD), terms),
+    ):
+        grad[place] = value + before[0][place] if before else value
 
 
 def window_kernel(half, grad_a, grad_b, fwd_h, fwd_l, adj_h, adj_l, *outs):
@@ -266,8 +286,16 @@
         edges[steps][rows : rows + 1, :] = term
 
 
+def last_order(half):
+    far = range(1, half)
+    return [("body", n) for n in far] + [("edge", n) for n in far] + [("edge", 0)]
+
+
 def place_kernel(half, term_scale, *refs):
-    bodies, edges = refs[:half], refs[half : 2 * half]
+    own, *moved = refs[: 2 * half]
+    moved = dict(zip(last_order(half), moved))
+    bodies = [own] + [moved["body", n] for n in range(1, half)]
+    edges = [moved["edge", n] for n in range(half)]
     out, source = refs[2 * half :]
     rows, pixels = out.shape[1:]
     per_device = source.shape[1]
@@ -291,10 +319,11 @@
 
 
 def call(kernel, outs, scratch=(), kind=F32, hbm=False):
+    kinds = kind if isinstance(kind, list) else [kind] * len(outs)
     held = {"in_specs": [pl.BlockSpec(memory_space=pltpu.HBM)] * 5} if hbm else {}
     return pl.pallas_call(
         kernel,
-        out_shape=[jax.ShapeDtypeStruct(shape, kind) for shape in outs],
+        out_shape=[jax.ShapeDtypeStruct(o, k) for o, k in zip(outs, kinds)],
         out_specs=[pl.BlockSpec(memory_space=pltpu.VMEM) for _ in outs],
         scratch_shapes=list(scratch),
         compiler_params=pltpu.CompilerParams(vmem_limit_bytes=VMEM_BUDGET),
@@ -374,34 +403,45 @@
         pin(source_weight.reshape(1, per_device)),
         pin(pupil_phase),
     )
-    blocks = [message] + [to_hub(message, 0, n) for n in range(1, half)]
-    blocks += [to_hub(message, 1, n) for n in reversed(range(half))][::-1]
+    order = (0, *(2, 1, 3))
+    blocks = [message] + [to_hub(message, d // half, d % half) for d in order[1:]]
     phases = [phases_to_hub(phase, n) for n in reversed(range(half))][::-1]
     tables = call(
         tables_kernel, [(2 * freqs, 2 * pixels)] * 2 + [(2 * pixels, 2 * freqs)] * 2, kind=BF16
     )()
 
     spec, goal, meta = call(
-        functools.partial(spectrum_kernel, half),
+        functools.partial(spectrum_kernel, half, order),
         [(2 * freqs, freqs), (src_count, rows, pixels), (half, PAD, pixels)],
         [pltpu.VMEM((2 * pixels, freqs), F32)],
     )(*blocks, *tables)
     spec_other = swap_rows(spec)
-    goal_other = swap_rows(goal)
-
-    field, pupil, inten = call(
-        functools.partial(fields_kernel, per_device, sources, half),
-        [(count, pixels, 2 * pixels), (count, 2 * freqs, freqs), (pixels, pixels)],
-        [pltpu.VMEM((2 * freqs, count * freqs), BF16)] * 2,
-    )(phase, *phases, spec, spec_other, meta, *tables)
-    inten_other = swap_rows(inten)
-
-    (grad,) = call(
-        functools.partial(adjoint_kernel, per_device, sources),
-        [(2 * freqs + PAD, freqs)],
-        [pltpu.VMEM((pixels, pixels), F32)]
-        + [pltpu.VMEM((2 * pixels, count * freqs), BF16)] * 2,
-    )(field, pupil, inten, inten_other, goal, goal_other, meta, *tables)
+
+    shape = (2 * freqs, count * freqs)
+    part = pixels // 2
+    outs = [(count, part, 2 * pixels), (part + part // 2, pixels)]
+    *first, pupil, amp_h, amp_l = call(
+        functools.partial(fields_kernel, per_device, sources, 0, half),
+        [*outs, (count, 2 * freqs, freqs), shape, shape],
+        [pltpu.VMEM((count * part, 2 * freqs), BF16)] * 2,
+        kind=[F32, F32, F32, BF16, BF16],
+    )(phase, *phases, spec, spec_other, meta, goal, *tables)
+    second = call(
+        functools.partial(fields_kernel, per_device, sources, part, half),
+        outs,
+        [pltpu.VMEM((count * part, 2 * freqs), BF16)] * 2,
+    )(meta, goal, amp_h, amp_l, *tables)
+    fields = [first, second]
+    others = [swap_rows(light) for _, light in fields]
+    grad = []
+    for first_row, (field, light), other in zip((0, part), fields, others):
+        grad = call(
+            functools.partial(adjoint_kernel, per_device, sources, first_row, rows),
+            [(2 * freqs + PAD, freqs)],
+            [pltpu.VMEM((part, pixels), F32)]
+            + [pltpu.VMEM((2 * part, count * freqs), BF16)] * 2,
+        )(*grad, field, pupil, light, other, meta, *tables)
+    (grad,) = grad
     grad_other = swap_rows(grad)
 
     outs = call(
@@ -425,7 +465,7 @@
     out, source = call(
         functools.partial(place_kernel, half, 1.0 / (sources * pixels * tile_count)),
         [(1, rows, pixels), (1, per_device)],
-    )(*bodies, *edges)
+    )(bodies[0], *[dict(body=bodies, edge=edges)[k][n] for k, n in last_order(half)])
     return out, source[0]
 
 

time: 31.3 us -> 29.8 us (0.952)
  starting transfers between devices: 10.9 us -> 9.49 us
    ppermute x8, starting transfers between devices: 10.1 us -> 8.63 us  [permute(): lax.ppermute(x, ('src', 'tile', 'row'), [(flat[a], flat[b]) for a, b in p...]
    ppermute x4, waiting for transfers between devices: 2.43 us -> 1.27 us  [swap_rows(): return lax.ppermute(x, 'row', [(0, 1), (1, 0)])]
    ppermute x8, waiting for transfers between devices: 7.89 us -> 8.75 us  [permute(): lax.ppermute(x, ('src', 'tile', 'row'), [(flat[a], flat[b]) for a, b in p...]
    pallas_call x3 -> x5, Pallas kernels: 6.36 us -> 6.66 us  [the longest x2 2.67 us: hub_shards(): call(functools.partial(adjoint_kernel, per_device, sources, first_row, ro...]
  transfers between devices with their start and end apart: 12 -> 12, of which waited for: 5 -> 4; matrix products, arithmetic and copies ran while one was open for 0% -> 0% of each run, Pallas kernels for 4% -> 13%
where the time goes in v4:
time: 29.8 us; the launch traced here: 29.7 us
  waiting for transfers between devices  10 us (34%)
  starting transfers between devices  9.49 us (32%)
  Pallas kernels  9.46 us (32%)
  between operations  0.72 us (2%)
    ppermute x8, waiting for transfers between devices, permute(): lax.ppermute(x, ('src', 'tile', 'row'), [(flat[a], flat[b]) for a, b in p...  8.75 us
    ppermute x8, starting transfers between devices, permute(): lax.ppermute(x, ('src', 'tile', 'row'), [(flat[a], flat[b]) for a, b in p...  8.63 us
    pallas_call x2, Pallas kernels, hub_shards(): call(functools.partial(adjoint_kernel, per_device, sources, first_row, ro...  2.67 us
    pallas_call x1, Pallas kernels, hub_shards(): call(functools.partial(fields_kernel, per_device, sources, 0, half), [*ou...  1.98 us
    pallas_call x1, Pallas kernels, hub_shards(): call(functools.partial(fields_kernel, per_device, sources, part, half), o...  1.32 us
    ppermute x4, waiting for transfers between devices, swap_rows(): return lax.ppermute(x, 'row', [(0, 1), (1, 0)])  1.27 us
    pallas_call x1, Pallas kernels, hub_shards(): call(fetch_kernel, [(2 * rows + PAD, pixels), pupil_phase.shape], [pltpu....  1.05 us
    ppermute x4, starting transfers between devices, swap_rows(): return lax.ppermute(x, 'row', [(0, 1), (1, 0)])  0.85 us
  transfers between devices with their start and end apart: 12, of which 4 were waited for; matrix products, arithmetic and copies ran while one was open for 0% of the time, Pallas kernels for 13%

profile of v4, /device:TPU:0, one launch (start us, length us, event | category | flops | bytes accessed | tf_op | source)
XLA Modules:
  0.0 29.7 jit_solution(6054232658270141126)
XLA Ops:
  0.6 1.0 %shard_map.68 = (f32[72,256]{1,0:T(8,128)S(1)}, f32[3,128,128]{2,1,0:T(8,128)S(1)}) custom-call(f32[1,32,256]{2,1,0:T(8,128)} %mask.1, f32[1,32,256]{2,1,0:T(8,128)} %goal.1, s32[3,2,128]{2,1,0:T(2,128)} %bitcast.3, f32[1,3]{1,0:T(1,128)} %bitcast.4, f32[3,128,128]{2,1,0:T(8,128)} %phase.1), custom_call_target="tpu_custom_call" | custom-call | tf_op jit(solution)/shard_map/pallas_call | solution.py:390
  1.7 4.1 %collective-permute-start.4 = (f32[72,256]{1,0:T(8,128)S(1)}, f32[72,256]{1,0:T(8,128)S(1)}, u32[]{:S(2)}, u32[]{:S(2)}) collective-permute-start(f32[72,256]{1,0:T(8,128)S(1)} %get-tuple-element.25.refs_0_), channel_id=1, source_target_pairs={{0,8},{1,9},{2,10},{3,11},{12,4},{13,5},{14,6},{15,7},{4,0},{5,1},... | collective-permute-start | bytes 221192 | tf_op jit(solution)/shard_map/ppermute | solution.py:350
  5.8 0.0 collective-permute-start.3
  5.8 0.0 collective-permute-start.2
  5.8 2.5 %collective-permute-start.1 = (f32[3,128,128]{2,1,0:T(8,128)S(1)}, f32[3,128,128]{2,1,0:T(8,128)S(1)}, u32[]{:S(2)}, u32[]{:S(2)}) collective-permute-start(f32[3,128,128]{2,1,0:T(8,128)S(1)} %get-tuple-element.24.refs_0_), channel_id=1, source_target_pairs={{0,4},{1,9},{2,6},{3,11},{12,8},{13,5},{14,10},{15,7},{4,0},{5,1},... | collective-permute-start | bytes 589832 | tf_op jit(solution)/shard_map/ppermute | solution.py:350
  8.3 0.0 collective-permute-start
  8.3 0.4 %shard_map.69 = (bf16[256,512]{1,0:T(8,128)(2,1)S(1)}, bf16[256,512]{1,0:T(8,128)(2,1)S(1)}, bf16[512,256]{1,0:T(8,128)(2,1)S(1)}, bf16[512,256]{1,0:T(8,128)(2,1)S(1)}) custom-call(), custom_call_target="tpu_custom_call" | custom-call | tf_op jit(solution)/shard_map/pallas_call | solution.py:409
  8.7 0.0 collective-permute-done.4.refs_3_
  8.7 2.1 %collective-permute-done.3.refs_2_ = f32[72,256]{1,0:T(8,128)S(1)} collective-permute-done((f32[72,256]{1,0:T(8,128)S(1)}, f32[72,256]{1,0:T(8,128)S(1)}, u32[]{:S(2)}, u32[]{:S(2)}) %collective-permute-start.3) | collective-permute-done | bytes 73760 | tf_op jit(solution)/shard_map/ppermute | solution.py:350
  10.8 0.0 collective-permute-done.2.refs_1_
  10.8 0.7 %shard_map.70 = (f32[256,128]{1,0:T(8,128)S(1)}, f32[4,32,256]{2,1,0:T(8,128)S(1)}, f32[2,8,256]{2,1,0:T(8,128)S(1)}) custom-call(f32[72,256]{1,0:T(8,128)S(1)} %get-tuple-element.25.refs_0_, f32[72,256]{1,0:T(8,128)S(1)} %collective-permute-done.2.refs_1_, f32[72,256]{1,0:T(8,128)S(1)} %collective-permute-done.3.refs_2_, ...), custom_call_target="tpu_custom_call" | custom-call | tf_op jit(solution)/shard_map/pallas_call | solution.py:413
  11.5 0.1 collective-permute-start.5
  11.6 2.3 %collective-permute-done.1.refs_2_ = f32[3,128,128]{2,1,0:T(8,128)S(1)} collective-permute-done((f32[3,128,128]{2,1,0:T(8,128)S(1)}, f32[3,128,128]{2,1,0:T(8,128)S(1)}, u32[]{:S(2)}, u32[]{:S(2)}) %collective-permute-start.1) | collective-permute-done | bytes 196640 | tf_op jit(solution)/shard_map/ppermute | solution.py:350
  13.9 0.0 collective-permute-done.refs_1_
  13.9 0.0 collective-permute-done.5.refs_4_
  13.9 2.0 %shard_map.71 = (f32[6,128,512]{2,1,0:T(8,128)S(1)}, f32[192,256]{1,0:T(8,128)S(1)}, f32[6,256,128]{2,1,0:T(8,128)S(1)}, bf16[256,768]{1,0:T(8,128)(2,1)S(1)}, bf16[256,768]{1,0:T(8,128)(2,1)S(1)}) custom-call(f32[3,128,128]{2,1,0:T(8,128)S(1)} %get-tuple-element.24.refs_0_, f32[3,128,128]{2,1,0:T(8,128)S(1)} %collective-permute-done.refs_1_, ...), custom_call_target="tpu_custom_call" | custom-call | tf_op jit(solution)/shard_map/pallas_call | solution.py:423
  15.9 0.1 collective-permute-start.6
  16.0 1.3 %shard_map.73 = (f32[6,128,512]{2,1,0:T(8,128)S(1)}, f32[192,256]{1,0:T(8,128)S(1)}) custom-call(f32[2,8,256]{2,1,0:T(8,128)S(1)} %get-tuple-element.31.refs_5_.refs_4_.refs_0_, f32[4,32,256]{2,1,0:T(8,128)S(1)} %get-tuple-element.32.refs_6_.refs_1_, bf16[256,768]{1,0:T(8,128)(2,1)S(1)} %get-tuple-element.36.refs_2_, ...), custom_call_target="tpu_custom_call" | custom-call | tf_op jit(solution)/shard_map/pallas_call | solution.py:429
  17.3 0.6 %collective-permute-start.7 = (f32[192,256]{1,0:T(8,128)S(1)}, f32[192,256]{1,0:T(8,128)S(1)}, u32[]{:S(2)}, u32[]{:S(2)}) collective-permute-start(f32[192,256]{1,0:T(8,128)S(1)} %get-tuple-element.39.refs_3_), channel_id=1, source_target_pairs={{0,1},{1,0},{2,3},{3,2},{4,5},{5,4},{6,7},{7,6},{8,9},{9,8},{10,11... | collective-permute-start | bytes 589832 | tf_op jit(solution)/shard_map/ppermute | solution.py:354
  17.8 0.0 collective-permute-done.6.refs_3_
  17.9 1.3 %shard_map.72.refs_0_ = f32[264,128]{1,0:T(8,128)S(1)} custom-call(f32[6,128,512]{2,1,0:T(8,128)S(1)} %get-tuple-element.33.refs_0_, f32[6,256,128]{2,1,0:T(8,128)S(1)} %get-tuple-element.34.refs_1_.refs_2_, f32[192,256]{1,0:T(8,128)S(1)} %get-tuple-element.35.refs_2_, f32[192,256]{1,0:T(8,128)S(1)} %collective-permute-done.6.refs_3_, ...), custom_call_target="tpu_custom_call" | custom-call | tf_op jit(solution)/shard_map/pallas_call | solution.py:438
  19.2 0.0 collective-permute-done.7.refs_4_
  19.2 1.3 %shard_map.74.grad_a = f32[264,128]{1,0:T(8,128)S(1)} custom-call(f32[264,128]{1,0:T(8,128)S(1)} %shard_map.72.refs_0_, f32[6,128,512]{2,1,0:T(8,128)S(1)} %get-tuple-element.38.refs_1_, f32[6,256,128]{2,1,0:T(8,128)S(1)} %get-tuple-element.34.refs_1_.refs_2_, f32[192,256]{1,0:T(8,128)S(1)} %get-tuple-element.39.refs_3_, ...), custom_call_target="tpu_custom_call" | custom-call | tf_op jit(solution)/shard_map/pallas_call | solution.py:438
  20.5 0.2 collective-permute-start.8
  20.7 1.3 %collective-permute-done.8.grad_b = f32[264,128]{1,0:T(8,128)S(1)} collective-permute-done((f32[264,128]{1,0:T(8,128)S(1)}, f32[264,128]{1,0:T(8,128)S(1)}, u32[]{:S(2)}, u32[]{:S(2)}) %collective-permute-start.8) | collective-permute-done | bytes 135200 | tf_op jit(solution)/shard_map/ppermute | solution.py:354
  22.0 0.6 %shard_map.75 = (f32[40,256]{1,0:T(8,128)S(1)}, f32[40,256]{1,0:T(8,128)S(1)}, f32[40,128]{1,0:T(8,128)S(1)}, f32[40,128]{1,0:T(8,128)S(1)}) custom-call(f32[264,128]{1,0:T(8,128)S(1)} %shard_map.74.grad_a, f32[264,128]{1,0:T(8,128)S(1)} %collective-permute-done.8.grad_b, bf16[256,512]{1,0:T(8,128)(2,1)S(1)} %get-tuple-element.26.refs_4_.refs_7_.refs_5_.refs_6_.fwd_h, ...), custom_call_target="tpu_custom_call" | custom-call | tf_op jit(solution)/shard_map/pallas_call | solution.py:447
  22.6 1.7 %collective-permute-start.9 = (f32[40,256]{1,0:T(8,128)S(1)}, f32[40,256]{1,0:T(8,128)S(1)}, u32[]{:S(2)}, u32[]{:S(2)}) collective-permute-start(f32[40,256]{1,0:T(8,128)S(1)} %get-tuple-element.41), channel_id=1, source_target_pairs={{4,0},{5,1},{6,2},{7,3},{8,12},{9,13},{10,14},{11,15},{0,4},{1,5},... | collective-permute-start | bytes 122888 | tf_op jit(solution)/shard_map/ppermute | solution.py:350
  24.3 0.3 %collective-permute-start.10 = (f32[40,128]{1,0:T(8,128)S(1)}, f32[40,128]{1,0:T(8,128)S(1)}, u32[]{:S(2)}, u32[]{:S(2)}) collective-permute-start(f32[40,128]{1,0:T(8,128)S(1)} %get-tuple-element.42), channel_id=1, source_target_pairs={{4,2},{5,3},{6,0},{7,1},{8,14},{9,15},{10,12},{11,13},{0,4},{1,5},... | collective-permute-start | bytes 61448 | tf_op jit(solution)/shard_map/ppermute | solution.py:350
  24.6 0.0 collective-permute-start.11
  24.6 4.3 %collective-permute-done.10.refs_2_ = f32[40,128]{1,0:T(8,128)S(1)} collective-permute-done((f32[40,128]{1,0:T(8,128)S(1)}, f32[40,128]{1,0:T(8,128)S(1)}, u32[]{:S(2)}, u32[]{:S(2)}) %collective-permute-start.10) | collective-permute-done | bytes 20512 | tf_op jit(solution)/shard_map/ppermute | solution.py:350
  29.0 0.0 collective-permute-done.11.refs_3_
  29.0 0.0 collective-permute-done.9.refs_1_
  29.0 0.7 %shard_map.76 = (f32[1,32,256]{2,1,0:T(8,128)}, f32[1,3]{1,0:T(1,128)}) custom-call(f32[40,256]{1,0:T(8,128)S(1)} %get-tuple-element.40.refs_0_, f32[40,256]{1,0:T(8,128)S(1)} %collective-permute-done.9.refs_1_, f32[40,128]{1,0:T(8,128)S(1)} %collective-permute-done.10.refs_2_, f32[40,128]{1,0:T(8,128)S(1)} %collective-permute-done.11.refs_3_), custom_call_target="tpu_custom_call" | custom-call | tf_op jit(solution)/shard_map/pallas_call | solution.py:465
Async XLA Ops:
  1.7 7.0 %collective-permute-start.4 = (f32[72,256]{1,0:T(8,128)S(1)}, f32[72,256]{1,0:T(8,128)S(1)}, u32[]{:S(2)}, u32[]{:S(2)}) collective-permute-start(f32[72,256]{1,0:T(8,128)S(1)} %get-tuple-element.25.refs_0_), channel_id=1, source_target_pairs={{0,8},{1,9},{2,10},{3,11},{12,4},{13,5},{14,6},{15,7},{4,0},{5,1},... | collective-permute-start | bytes 221192 | tf_op jit(solution)/shard_map/ppermute | solution.py:350
  5.8 5.1 %collective-permute-start.3 = (f32[72,256]{1,0:T(8,128)S(1)}, f32[72,256]{1,0:T(8,128)S(1)}, u32[]{:S(2)}, u32[]{:S(2)}) collective-permute-start(f32[72,256]{1,0:T(8,128)S(1)} %get-tuple-element.25.refs_0_), channel_id=1, source_target_pairs={{0,4},{1,5},{2,6},{3,7},{12,8},{13,9},{14,10},{15,11},{4,0},{5,1},... | collective-permute-start | bytes 221192 | tf_op jit(solution)/shard_map/ppermute | solution.py:350
  5.8 5.1 %collective-permute-start.2 = (f32[72,256]{1,0:T(8,128)S(1)}, f32[72,256]{1,0:T(8,128)S(1)}, u32[]{:S(2)}, u32[]{:S(2)}) collective-permute-start(f32[72,256]{1,0:T(8,128)S(1)} %get-tuple-element.25.refs_0_), channel_id=1, source_target_pairs={{4,8},{5,9},{6,10},{7,11},{8,4},{9,5},{10,6},{11,7},{0,1},{1,0},{2... | collective-permute-start | bytes 221192 | tf_op jit(solution)/shard_map/ppermute | solution.py:350
  5.8 8.1 %collective-permute-start.1 = (f32[3,128,128]{2,1,0:T(8,128)S(1)}, f32[3,128,128]{2,1,0:T(8,128)S(1)}, u32[]{:S(2)}, u32[]{:S(2)}) collective-permute-start(f32[3,128,128]{2,1,0:T(8,128)S(1)} %get-tuple-element.24.refs_0_), channel_id=1, source_target_pairs={{0,4},{1,9},{2,6},{3,11},{12,8},{13,5},{14,10},{15,7},{4,0},{5,1},... | collective-permute-start | bytes 589832 | tf_op jit(solution)/shard_map/ppermute | solution.py:350
  8.3 5.6 %collective-permute-start = (f32[3,128,128]{2,1,0:T(8,128)S(1)}, f32[3,128,128]{2,1,0:T(8,128)S(1)}, u32[]{:S(2)}, u32[]{:S(2)}) collective-permute-start(f32[3,128,128]{2,1,0:T(8,128)S(1)} %get-tuple-element.24.refs_0_), channel_id=1, source_target_pairs={{4,9},{6,11},{8,5},{10,7},{0,1},{1,0},{2,3},{3,2},{5,4},{7,6},{9,8... | collective-permute-start | bytes 589832 | tf_op jit(solution)/shard_map/ppermute | solution.py:350
  11.5 2.4 %collective-permute-start.5 = (f32[256,128]{1,0:T(8,128)S(1)}, f32[256,128]{1,0:T(8,128)S(1)}, u32[]{:S(2)}, u32[]{:S(2)}) collective-permute-start(f32[256,128]{1,0:T(8,128)S(1)} %get-tuple-element.30.refs_3_), channel_id=1, source_target_pairs={{0,1},{1,0},{2,3},{3,2},{4,5},{5,4},{6,7},{7,6},{8,9},{9,8},{10,11... | collective-permute-start | bytes 393224 | tf_op jit(solution)/shard_map/ppermute | solution.py:354
  15.9 2.0 %collective-permute-start.6 = (f32[192,256]{1,0:T(8,128)S(1)}, f32[192,256]{1,0:T(8,128)S(1)}, u32[]{:S(2)}, u32[]{:S(2)}) collective-permute-start(f32[192,256]{1,0:T(8,128)S(1)} %get-tuple-element.35.refs_2_), channel_id=1, source_target_pairs={{0,1},{1,0},{2,3},{3,2},{4,5},{5,4},{6,7},{7,6},{8,9},{9,8},{10,11... | collective-permute-start | bytes 589832 | tf_op jit(solution)/shard_map/ppermute | solution.py:354
  17.3 1.9 %collective-permute-start.7 = (f32[192,256]{1,0:T(8,128)S(1)}, f32[192,256]{1,0:T(8,128)S(1)}, u32[]{:S(2)}, u32[]{:S(2)}) collective-permute-start(f32[192,256]{1,0:T(8,128)S(1)} %get-tuple-element.39.refs_3_), channel_id=1, source_target_pairs={{0,1},{1,0},{2,3},{3,2},{4,5},{5,4},{6,7},{7,6},{8,9},{9,8},{10,11... | collective-permute-start | bytes 589832 | tf_op jit(solution)/shard_map/ppermute | solution.py:354
  20.5 1.4 %collective-permute-start.8 = (f32[264,128]{1,0:T(8,128)S(1)}, f32[264,128]{1,0:T(8,128)S(1)}, u32[]{:S(2)}, u32[]{:S(2)}) collective-permute-start(f32[264,128]{1,0:T(8,128)S(1)} %shard_map.74.grad_a), channel_id=1, source_target_pairs={{0,1},{1,0},{2,3},{3,2},{4,5},{5,4},{6,7},{7,6},{8,9},{9,8},{10,11... | collective-permute-start | bytes 405512 | tf_op jit(solution)/shard_map/ppermute | solution.py:354
  22.6 6.4 %collective-permute-start.9 = (f32[40,256]{1,0:T(8,128)S(1)}, f32[40,256]{1,0:T(8,128)S(1)}, u32[]{:S(2)}, u32[]{:S(2)}) collective-permute-start(f32[40,256]{1,0:T(8,128)S(1)} %get-tuple-element.41), channel_id=1, source_target_pairs={{4,0},{5,1},{6,2},{7,3},{8,12},{9,13},{10,14},{11,15},{0,4},{1,5},... | collective-permute-start | bytes 122888 | tf_op jit(solution)/shard_map/ppermute | solution.py:350
  24.3 4.7 %collective-permute-start.10 = (f32[40,128]{1,0:T(8,128)S(1)}, f32[40,128]{1,0:T(8,128)S(1)}, u32[]{:S(2)}, u32[]{:S(2)}) collective-permute-start(f32[40,128]{1,0:T(8,128)S(1)} %get-tuple-element.42), channel_id=1, source_target_pairs={{4,2},{5,3},{6,0},{7,1},{8,14},{9,15},{10,12},{11,13},{0,4},{1,5},... | collective-permute-start | bytes 61448 | tf_op jit(solution)/shard_map/ppermute | solution.py:350
  24.6 4.3 %collective-permute-start.11 = (f32[40,128]{1,0:T(8,128)S(1)}, f32[40,128]{1,0:T(8,128)S(1)}, u32[]{:S(2)}, u32[]{:S(2)}) collective-permute-start(f32[40,128]{1,0:T(8,128)S(1)} %get-tuple-element.43), channel_id=1, source_target_pairs={{4,6},{5,7},{6,4},{7,5},{8,10},{9,11},{10,8},{11,9},{0,1},{1,0},{2... | collective-permute-start | bytes 61448 | tf_op jit(solution)/shard_map/ppermute | solution.py:350

commit v5 on v4

--- a/solution.py
+++ b/solution.py
@@ -58,7 +58,7 @@
     return jnp.where(low, same if side == 0 else other, other if side == 0 else same)
 
 
-def fetch_kernel(mask, goal, bands, weight, phase, message, held, bands_in, weight_in, sems):
+def fetch_kernel(mask, goal, bands, weight, message, bands_in, weight_in, sems):
     rows = mask.shape[1]
     per_device, _, freqs = bands.shape
     message[2 * rows :] = jnp.zeros_like(message[2 * rows :])
@@ -70,7 +70,6 @@
                 (goal.at[0], message.at[pl.ds(rows, rows)]),
                 (bands, bands_in),
                 (weight, weight_in),
-                (phase, held),
             )
         )
     ]
@@ -87,7 +86,9 @@
     message[line : line + 1, :per_device] = weight_in[...]
 
 
-def tables_kernel(fwd_h, fwd_l, adj_h, adj_l):
+def tables_kernel(phase, fwd_h, fwd_l, adj_h, adj_l, held, sem):
+    copy = pltpu.make_async_copy(phase, held, sem)
+    copy.start()
     freqs, pixels = fwd_h.shape[0] // 2, fwd_h.shape[1] // 2
 
     def waves(shape, freq_dim):
@@ -109,6 +110,7 @@
         table[:pixels, freqs:] = -sin
         table[pixels:, :freqs] = sin
         table[pixels:, freqs:] = cos
+    copy.wait()
 
 
 def spectrum_kernel(half, order, *refs):
@@ -271,7 +273,8 @@
     for table in (adj_h, adj_l):
         parts = []
         for steps in range(half):
-            start = (block_of(src, 0, steps, half) * 2 + row) * rows
+            core = row if steps == 0 else 1 - row
+            start = (block_of(src, 0, steps, half) * 2 + core) * rows
             parts.append(table[pl.ds(pl.multiple_of(start, rows), rows), :])
         tables.append(jnp.concatenate(parts, axis=0))
     window = mm3(tables, split(waves))
@@ -318,9 +321,9 @@
     source[...] = (mine(bodies, *term) + mine(edges, *term)) * term_scale
 
 
-def call(kernel, outs, scratch=(), kind=F32, hbm=False):
+def call(kernel, outs, scratch=(), kind=F32, hbm=0):
     kinds = kind if isinstance(kind, list) else [kind] * len(outs)
-    held = {"in_specs": [pl.BlockSpec(memory_space=pltpu.HBM)] * 5} if hbm else {}
+    held = {"in_specs": [pl.BlockSpec(memory_space=pltpu.HBM)] * hbm} if hbm else {}
     return pl.pallas_call(
         kernel,
         out_shape=[jax.ShapeDtypeStruct(o, k) for o, k in zip(outs, kinds)],
@@ -387,28 +390,31 @@
         return permute(x, pairs)
 
     pin = functools.partial(pltpu.with_memory_space_constraint, memory_space=pltpu.HBM)
-    message, phase = call(
+    (message,) = call(
         fetch_kernel,
-        [(2 * rows + PAD, pixels), pupil_phase.shape],
+        [(2 * rows + PAD, pixels)],
         [
             pltpu.VMEM((per_device, 2, freqs), jnp.int32),
             pltpu.VMEM((1, per_device), F32),
-            pltpu.SemaphoreType.DMA((5,)),
+            pltpu.SemaphoreType.DMA((4,)),
         ],
-        hbm=True,
+        hbm=4,
     )(
         pin(mask_windows),
         pin(target_windows),
         pin(pupil_bands.transpose(0, 2, 1)),
         pin(source_weight.reshape(1, per_device)),
-        pin(pupil_phase),
-    )
-    order = (0, *(2, 1, 3))
+    )
+    order = (0, half, *range(1, half), *range(half + 1, 2 * half))
     blocks = [message] + [to_hub(message, d // half, d % half) for d in order[1:]]
-    phases = [phases_to_hub(phase, n) for n in reversed(range(half))][::-1]
-    tables = call(
-        tables_kernel, [(2 * freqs, 2 * pixels)] * 2 + [(2 * pixels, 2 * freqs)] * 2, kind=BF16
-    )()
+    phases = [phases_to_hub(pupil_phase, n) for n in reversed(range(half))][::-1]
+    *tables, phase = call(
+        tables_kernel,
+        [(2 * freqs, 2 * pixels)] * 2 + [(2 * pixels, 2 * freqs)] * 2 + [pupil_phase.shape],
+        [pltpu.SemaphoreType.DMA],
+        kind=[BF16] * 4 + [F32],
+        hbm=1,
+    )(pin(pupil_phase))
 
     spec, goal, meta = call(
         functools.partial(spectrum_kernel, half, order),
@@ -454,7 +460,11 @@
         return permute(
             x,
             {
-                (chip(low, 0), t, c): (chip(low, steps), 1 - t if flip else t, c)
+                (chip(low, 0), t, c): (
+                    chip(low, steps),
+                    1 - t if flip else t,
+                    1 - c if steps else c,
+                )
                 for low in halves
                 for t, c in cores
             },

time: 29.8 us -> 29.3 us (0.983)
  waiting for transfers between devices: 10 us -> 9.29 us
  Pallas kernels: 9.46 us -> 9.78 us
    ppermute x8, waiting for transfers between devices: 8.75 us -> 8.01 us  [permute(): lax.ppermute(x, ('src', 'tile', 'row'), [(flat[a], flat[b]) for a, b in p...]
    pallas_call x1, Pallas kernels: 0.44 us -> 0.97 us  [hub_shards(): call(tables_kernel, [(2 * freqs, 2 * pixels)] * 2 + [(2 * pixels, 2 * fre...]
  transfers between devices with their start and end apart: 12 -> 12, of which waited for: 4 -> 4; matrix products, arithmetic and copies ran while one was open for 0% -> 0% of each run, Pallas kernels for 13% -> 15%
where the time goes in v5:
time: 29.3 us; the launch traced here: 29.1 us
  Pallas kernels  9.78 us (33%)
  starting transfers between devices  9.3 us (32%)
  waiting for transfers between devices  9.29 us (32%)
  between operations  0.72 us (2%)
    ppermute x8, starting transfers between devices, permute(): lax.ppermute(x, ('src', 'tile', 'row'), [(flat[a], flat[b]) for a, b in p...  8.46 us
    ppermute x8, waiting for transfers between devices, permute(): lax.ppermute(x, ('src', 'tile', 'row'), [(flat[a], flat[b]) for a, b in p...  8.01 us
    pallas_call x2, Pallas kernels, hub_shards(): call(functools.partial(adjoint_kernel, per_device, sources, first_row, ro...  2.67 us
    pallas_call x1, Pallas kernels, hub_shards(): call(functools.partial(fields_kernel, per_device, sources, 0, half), [*ou...  1.99 us
    pallas_call x1, Pallas kernels, hub_shards(): call(functools.partial(fields_kernel, per_device, sources, part, half), o...  1.32 us
    ppermute x4, waiting for transfers between devices, swap_rows(): return lax.ppermute(x, 'row', [(0, 1), (1, 0)])  1.28 us
    pallas_call x1, Pallas kernels, hub_shards(): call(tables_kernel, [(2 * freqs, 2 * pixels)] * 2 + [(2 * pixels, 2 * fre...  0.97 us
    ppermute x4, starting transfers between devices, swap_rows(): return lax.ppermute(x, 'row', [(0, 1), (1, 0)])  0.85 us
  transfers between devices with their start and end apart: 12, of which 4 were waited for; matrix products, arithmetic and copies ran while one was open for 0% of the time, Pallas kernels for 15%

profile of v5, /device:TPU:0, one launch (start us, length us, event | category | flops | bytes accessed | tf_op | source)
XLA Modules:
  0.0 29.1 jit_solution(7803266815692487402)
XLA Ops:
  0.6 0.8 %shard_map.69.refs_0_ = f32[72,256]{1,0:T(8,128)S(1)} custom-call(f32[1,32,256]{2,1,0:T(8,128)} %mask.1, f32[1,32,256]{2,1,0:T(8,128)} %goal.1, s32[3,2,128]{2,1,0:T(2,128)} %bitcast.3, f32[1,3]{1,0:T(1,128)} %bitcast.4), custom_call_target="tpu_custom_call" | custom-call | tf_op jit(solution)/shard_map/pallas_call | solution.py:393
  1.5 4.1 %collective-permute-start.4 = (f32[72,256]{1,0:T(8,128)S(1)}, f32[72,256]{1,0:T(8,128)S(1)}, u32[]{:S(2)}, u32[]{:S(2)}) collective-permute-start(f32[72,256]{1,0:T(8,128)S(1)} %shard_map.69.refs_0_), channel_id=1, source_target_pairs={{0,8},{1,9},{2,10},{3,11},{12,4},{13,5},{14,6},{15,7},{4,0},{5,1},... | collective-permute-start | bytes 221192 | tf_op jit(solution)/shard_map/ppermute | solution.py:353
  5.5 0.0 collective-permute-start.3
  5.5 0.0 collective-permute-start.2
  5.6 2.5 %collective-permute-start.1 = (f32[3,128,128]{2,1,0:T(8,128)}, f32[3,128,128]{2,1,0:T(8,128)S(1)}, u32[]{:S(2)}, u32[]{:S(2)}) collective-permute-start(f32[3,128,128]{2,1,0:T(8,128)} %phase.1), channel_id=1, source_target_pairs={{0,4},{1,9},{2,6},{3,11},{12,8},{13,5},{14,10},{15,7},{4,0},{5,1},... | collective-permute-start | bytes 589832 | tf_op jit(solution)/shard_map/ppermute | solution.py:353
  8.0 0.0 collective-permute-start
  8.0 1.0 %shard_map.68 = (bf16[256,512]{1,0:T(8,128)(2,1)S(1)}, bf16[256,512]{1,0:T(8,128)(2,1)S(1)}, bf16[512,256]{1,0:T(8,128)(2,1)S(1)}, bf16[512,256]{1,0:T(8,128)(2,1)S(1)}, f32[3,128,128]{2,1,0:T(8,128)S(1)}) custom-call(f32[3,128,128]{2,1,0:T(8,128)} %phase.1), custom_call_target="tpu_custom_call" | custom-call | tf_op jit(solution)/shard_map/pallas_call | solution.py:411
  9.0 0.0 collective-permute-done.4.refs_3_
  9.0 1.7 %collective-permute-done.3.refs_2_ = f32[72,256]{1,0:T(8,128)S(1)} collective-permute-done((f32[72,256]{1,0:T(8,128)S(1)}, f32[72,256]{1,0:T(8,128)S(1)}, u32[]{:S(2)}, u32[]{:S(2)}) %collective-permute-start.3) | collective-permute-done | bytes 73760 | tf_op jit(solution)/shard_map/ppermute | solution.py:353
  10.7 0.0 collective-permute-done.2.refs_1_
  10.7 0.7 %shard_map.70 = (f32[256,128]{1,0:T(8,128)S(1)}, f32[4,32,256]{2,1,0:T(8,128)S(1)}, f32[2,8,256]{2,1,0:T(8,128)S(1)}) custom-call(f32[72,256]{1,0:T(8,128)S(1)} %shard_map.69.refs_0_, f32[72,256]{1,0:T(8,128)S(1)} %collective-permute-done.2.refs_1_, f32[72,256]{1,0:T(8,128)S(1)} %collective-permute-done.3.refs_2_, ...), custom_call_target="tpu_custom_call" | custom-call | tf_op jit(solution)/shard_map/pallas_call | solution.py:419
  11.4 0.1 collective-permute-start.5
  11.5 2.4 %collective-permute-done.1.refs_2_ = f32[3,128,128]{2,1,0:T(8,128)S(1)} collective-permute-done((f32[3,128,128]{2,1,0:T(8,128)}, f32[3,128,128]{2,1,0:T(8,128)S(1)}, u32[]{:S(2)}, u32[]{:S(2)}) %collective-permute-start.1) | collective-permute-done | bytes 196640 | tf_op jit(solution)/shard_map/ppermute | solution.py:353
  13.9 0.0 collective-permute-done.refs_1_
  13.9 0.0 collective-permute-done.5.refs_4_
  13.9 2.0 %shard_map.71 = (f32[6,128,512]{2,1,0:T(8,128)S(1)}, f32[192,256]{1,0:T(8,128)S(1)}, f32[6,256,128]{2,1,0:T(8,128)S(1)}, bf16[256,768]{1,0:T(8,128)(2,1)S(1)}, bf16[256,768]{1,0:T(8,128)(2,1)S(1)}) custom-call(f32[3,128,128]{2,1,0:T(8,128)S(1)} %get-tuple-element.23.refs_0_, f32[3,128,128]{2,1,0:T(8,128)S(1)} %collective-permute-done.refs_1_, ...), custom_call_target="tpu_custom_call" | custom-call | tf_op jit(solution)/shard_map/pallas_call | solution.py:429
  15.9 0.1 collective-permute-start.6
  15.9 1.3 %shard_map.73 = (f32[6,128,512]{2,1,0:T(8,128)S(1)}, f32[192,256]{1,0:T(8,128)S(1)}) custom-call(f32[2,8,256]{2,1,0:T(8,128)S(1)} %get-tuple-element.29.refs_5_.refs_4_.refs_0_, f32[4,32,256]{2,1,0:T(8,128)S(1)} %get-tuple-element.30.refs_6_.refs_1_, bf16[256,768]{1,0:T(8,128)(2,1)S(1)} %get-tuple-element.34.refs_2_, ...), custom_call_target="tpu_custom_call" | custom-call | tf_op jit(solution)/shard_map/pallas_call | solution.py:435
  17.3 0.6 %collective-permute-start.7 = (f32[192,256]{1,0:T(8,128)S(1)}, f32[192,256]{1,0:T(8,128)S(1)}, u32[]{:S(2)}, u32[]{:S(2)}) collective-permute-start(f32[192,256]{1,0:T(8,128)S(1)} %get-tuple-element.37.refs_3_), channel_id=1, source_target_pairs={{0,1},{1,0},{2,3},{3,2},{4,5},{5,4},{6,7},{7,6},{8,9},{9,8},{10,11... | collective-permute-start | bytes 589832 | tf_op jit(solution)/shard_map/ppermute | solution.py:357
  17.8 0.0 collective-permute-done.6.refs_3_
  17.8 1.3 %shard_map.72.refs_0_ = f32[264,128]{1,0:T(8,128)S(1)} custom-call(f32[6,128,512]{2,1,0:T(8,128)S(1)} %get-tuple-element.31.refs_0_, f32[6,256,128]{2,1,0:T(8,128)S(1)} %get-tuple-element.32.refs_1_.refs_2_, f32[192,256]{1,0:T(8,128)S(1)} %get-tuple-element.33.refs_2_, f32[192,256]{1,0:T(8,128)S(1)} %collective-permute-done.6.refs_3_, ...), custom_call_target="tpu_custom_call" | custom-call | tf_op jit(solution)/shard_map/pallas_call | solution.py:444
  19.2 0.0 collective-permute-done.7.refs_4_
  19.2 1.3 %shard_map.74.grad_a = f32[264,128]{1,0:T(8,128)S(1)} custom-call(f32[264,128]{1,0:T(8,128)S(1)} %shard_map.72.refs_0_, f32[6,128,512]{2,1,0:T(8,128)S(1)} %get-tuple-element.36.refs_1_, f32[6,256,128]{2,1,0:T(8,128)S(1)} %get-tuple-element.32.refs_1_.refs_2_, f32[192,256]{1,0:T(8,128)S(1)} %get-tuple-element.37.refs_3_, ...), custom_call_target="tpu_custom_call" | custom-call | tf_op jit(solution)/shard_map/pallas_call | solution.py:444
  20.5 0.1 collective-permute-start.8
  20.7 1.3 %collective-permute-done.8.grad_b = f32[264,128]{1,0:T(8,128)S(1)} collective-permute-done((f32[264,128]{1,0:T(8,128)S(1)}, f32[264,128]{1,0:T(8,128)S(1)}, u32[]{:S(2)}, u32[]{:S(2)}) %collective-permute-start.8) | collective-permute-done | bytes 135200 | tf_op jit(solution)/shard_map/ppermute | solution.py:357
  21.9 0.6 %shard_map.75 = (f32[40,256]{1,0:T(8,128)S(1)}, f32[40,256]{1,0:T(8,128)S(1)}, f32[40,128]{1,0:T(8,128)S(1)}, f32[40,128]{1,0:T(8,128)S(1)}) custom-call(f32[264,128]{1,0:T(8,128)S(1)} %shard_map.74.grad_a, f32[264,128]{1,0:T(8,128)S(1)} %collective-permute-done.8.grad_b, bf16[256,512]{1,0:T(8,128)(2,1)S(1)} %get-tuple-element.24.refs_4_.refs_7_.refs_5_.refs_6_.fwd_h, ...), custom_call_target="tpu_custom_call" | custom-call | tf_op jit(solution)/shard_map/pallas_call | solution.py:453
  22.6 1.6 %collective-permute-start.9 = (f32[40,256]{1,0:T(8,128)S(1)}, f32[40,256]{1,0:T(8,128)S(1)}, u32[]{:S(2)}, u32[]{:S(2)}) collective-permute-start(f32[40,256]{1,0:T(8,128)S(1)} %get-tuple-element.39), channel_id=1, source_target_pairs={{4,1},{5,0},{6,3},{7,2},{8,13},{9,12},{10,15},{11,14},{0,4},{1,5},... | collective-permute-start | bytes 122888 | tf_op jit(solution)/shard_map/ppermute | solution.py:353
  24.2 0.2 collective-permute-start.10
  24.4 0.1 collective-permute-start.11
  24.5 3.9 %collective-permute-done.10.refs_2_ = f32[40,128]{1,0:T(8,128)S(1)} collective-permute-done((f32[40,128]{1,0:T(8,128)S(1)}, f32[40,128]{1,0:T(8,128)S(1)}, u32[]{:S(2)}, u32[]{:S(2)}) %collective-permute-start.10) | collective-permute-done | bytes 20512 | tf_op jit(solution)/shard_map/ppermute | solution.py:353
  28.4 0.0 collective-permute-done.11.refs_3_
  28.4 0.0 collective-permute-done.9.refs_1_
  28.4 0.7 %shard_map.76 = (f32[1,32,256]{2,1,0:T(8,128)}, f32[1,3]{1,0:T(1,128)}) custom-call(f32[40,256]{1,0:T(8,128)S(1)} %get-tuple-element.38.refs_0_, f32[40,256]{1,0:T(8,128)S(1)} %collective-permute-done.9.refs_1_, f32[40,128]{1,0:T(8,128)S(1)} %collective-permute-done.10.refs_2_, f32[40,128]{1,0:T(8,128)S(1)} %collective-permute-done.11.refs_3_), custom_call_target="tpu_custom_call" | custom-call | tf_op jit(solution)/shard_map/pallas_call | solution.py:475
Async XLA Ops:
  1.5 7.5 %collective-permute-start.4 = (f32[72,256]{1,0:T(8,128)S(1)}, f32[72,256]{1,0:T(8,128)S(1)}, u32[]{:S(2)}, u32[]{:S(2)}) collective-permute-start(f32[72,256]{1,0:T(8,128)S(1)} %shard_map.69.refs_0_), channel_id=1, source_target_pairs={{0,8},{1,9},{2,10},{3,11},{12,4},{13,5},{14,6},{15,7},{4,0},{5,1},... | collective-permute-start | bytes 221192 | tf_op jit(solution)/shard_map/ppermute | solution.py:353
  5.5 5.1 %collective-permute-start.3 = (f32[72,256]{1,0:T(8,128)S(1)}, f32[72,256]{1,0:T(8,128)S(1)}, u32[]{:S(2)}, u32[]{:S(2)}) collective-permute-start(f32[72,256]{1,0:T(8,128)S(1)} %shard_map.69.refs_0_), channel_id=1, source_target_pairs={{0,4},{1,5},{2,6},{3,7},{12,8},{13,9},{14,10},{15,11},{4,0},{5,1},... | collective-permute-start | bytes 221192 | tf_op jit(solution)/shard_map/ppermute | solution.py:353
  5.5 5.1 %collective-permute-start.2 = (f32[72,256]{1,0:T(8,128)S(1)}, f32[72,256]{1,0:T(8,128)S(1)}, u32[]{:S(2)}, u32[]{:S(2)}) collective-permute-start(f32[72,256]{1,0:T(8,128)S(1)} %shard_map.69.refs_0_), channel_id=1, source_target_pairs={{4,8},{5,9},{6,10},{7,11},{8,4},{9,5},{10,6},{11,7},{0,1},{1,0},{2... | collective-permute-start | bytes 221192 | tf_op jit(solution)/shard_map/ppermute | solution.py:353
  5.6 8.3 %collective-permute-start.1 = (f32[3,128,128]{2,1,0:T(8,128)}, f32[3,128,128]{2,1,0:T(8,128)S(1)}, u32[]{:S(2)}, u32[]{:S(2)}) collective-permute-start(f32[3,128,128]{2,1,0:T(8,128)} %phase.1), channel_id=1, source_target_pairs={{0,4},{1,9},{2,6},{3,11},{12,8},{13,5},{14,10},{15,7},{4,0},{5,1},... | collective-permute-start | bytes 589832 | tf_op jit(solution)/shard_map/ppermute | solution.py:353
  8.0 5.8 %collective-permute-start = (f32[3,128,128]{2,1,0:T(8,128)}, f32[3,128,128]{2,1,0:T(8,128)S(1)}, u32[]{:S(2)}, u32[]{:S(2)}) collective-permute-start(f32[3,128,128]{2,1,0:T(8,128)} %phase.1), channel_id=1, source_target_pairs={{4,9},{6,11},{8,5},{10,7},{0,1},{1,0},{2,3},{3,2},{5,4},{7,6},{9,8... | collective-permute-start | bytes 589832 | tf_op jit(solution)/shard_map/ppermute | solution.py:353
  11.4 2.5 %collective-permute-start.5 = (f32[256,128]{1,0:T(8,128)S(1)}, f32[256,128]{1,0:T(8,128)S(1)}, u32[]{:S(2)}, u32[]{:S(2)}) collective-permute-start(f32[256,128]{1,0:T(8,128)S(1)} %get-tuple-element.28.refs_3_), channel_id=1, source_target_pairs={{0,1},{1,0},{2,3},{3,2},{4,5},{5,4},{6,7},{7,6},{8,9},{9,8},{10,11... | collective-permute-start | bytes 393224 | tf_op jit(solution)/shard_map/ppermute | solution.py:357
  15.9 2.0 %collective-permute-start.6 = (f32[192,256]{1,0:T(8,128)S(1)}, f32[192,256]{1,0:T(8,128)S(1)}, u32[]{:S(2)}, u32[]{:S(2)}) collective-permute-start(f32[192,256]{1,0:T(8,128)S(1)} %get-tuple-element.33.refs_2_), channel_id=1, source_target_pairs={{0,1},{1,0},{2,3},{3,2},{4,5},{5,4},{6,7},{7,6},{8,9},{9,8},{10,11... | collective-permute-start | bytes 589832 | tf_op jit(solution)/shard_map/ppermute | solution.py:357
  17.3 1.9 %collective-permute-start.7 = (f32[192,256]{1,0:T(8,128)S(1)}, f32[192,256]{1,0:T(8,128)S(1)}, u32[]{:S(2)}, u32[]{:S(2)}) collective-permute-start(f32[192,256]{1,0:T(8,128)S(1)} %get-tuple-element.37.refs_3_), channel_id=1, source_target_pairs={{0,1},{1,0},{2,3},{3,2},{4,5},{5,4},{6,7},{7,6},{8,9},{9,8},{10,11... | collective-permute-start | bytes 589832 | tf_op jit(solution)/shard_map/ppermute | solution.py:357
  20.5 1.4 %collective-permute-start.8 = (f32[264,128]{1,0:T(8,128)S(1)}, f32[264,128]{1,0:T(8,128)S(1)}, u32[]{:S(2)}, u32[]{:S(2)}) collective-permute-start(f32[264,128]{1,0:T(8,128)S(1)} %shard_map.74.grad_a), channel_id=1, source_target_pairs={{0,1},{1,0},{2,3},{3,2},{4,5},{5,4},{6,7},{7,6},{8,9},{9,8},{10,11... | collective-permute-start | bytes 405512 | tf_op jit(solution)/shard_map/ppermute | solution.py:357
  22.6 5.8 %collective-permute-start.9 = (f32[40,256]{1,0:T(8,128)S(1)}, f32[40,256]{1,0:T(8,128)S(1)}, u32[]{:S(2)}, u32[]{:S(2)}) collective-permute-start(f32[40,256]{1,0:T(8,128)S(1)} %get-tuple-element.39), channel_id=1, source_target_pairs={{4,1},{5,0},{6,3},{7,2},{8,13},{9,12},{10,15},{11,14},{0,4},{1,5},... | collective-permute-start | bytes 122888 | tf_op jit(solution)/shard_map/ppermute | solution.py:353
  24.2 4.2 %collective-permute-start.10 = (f32[40,128]{1,0:T(8,128)S(1)}, f32[40,128]{1,0:T(8,128)S(1)}, u32[]{:S(2)}, u32[]{:S(2)}) collective-permute-start(f32[40,128]{1,0:T(8,128)S(1)} %get-tuple-element.40), channel_id=1, source_target_pairs={{4,3},{5,2},{6,1},{7,0},{8,15},{9,14},{10,13},{11,12},{0,4},{1,5},... | collective-permute-start | bytes 61448 | tf_op jit(solution)/shard_map/ppermute | solution.py:353
  24.4 4.0 %collective-permute-start.11 = (f32[40,128]{1,0:T(8,128)S(1)}, f32[40,128]{1,0:T(8,128)S(1)}, u32[]{:S(2)}, u32[]{:S(2)}) collective-permute-start(f32[40,128]{1,0:T(8,128)S(1)} %get-tuple-element.41), channel_id=1, source_target_pairs={{4,6},{5,7},{6,4},{7,5},{8,10},{9,11},{10,8},{11,9},{0,1},{1,0},{2... | collective-permute-start | bytes 61448 | tf_op jit(solution)/shard_map/ppermute | solution.py:353

commit v6 on v5

--- a/solution.py
+++ b/solution.py
@@ -260,9 +260,8 @@
         grad[place] = value + before[0][place] if before else value
 
 
-def window_kernel(half, grad_a, grad_b, fwd_h, fwd_l, adj_h, adj_l, *outs):
-    bodies, edges = outs[:half], outs[half:]
-    rows, pixels = bodies[0].shape[0] - PAD, bodies[0].shape[1]
+def window_kernel(half, grad_a, grad_b, fwd_h, fwd_l, adj_h, adj_l, own, pay_a, pay_b, pay_c):
+    rows, pixels = own.shape[0] - PAD, own.shape[1]
     freqs = grad_a.shape[1]
     src, row, tile = lax.axis_index("src"), lax.axis_index("row"), lax.axis_index("tile")
     total = grad_a[: 2 * freqs] + grad_b[: 2 * freqs]
@@ -272,60 +271,64 @@
     tables = []
     for table in (adj_h, adj_l):
         parts = []
-        for steps in range(half):
-            core = row if steps == 0 else 1 - row
+        for steps, core in ((0, row), (1, 1 - row)):
             start = (block_of(src, 0, steps, half) * 2 + core) * rows
             parts.append(table[pl.ds(pl.multiple_of(start, rows), rows), :])
         tables.append(jnp.concatenate(parts, axis=0))
     window = mm3(tables, split(waves))
     terms = jnp.where(row == 0, grad_a[2 * freqs :], grad_b[2 * freqs :])
-    for steps in range(half):
-        block = window[steps * rows : (steps + 1) * rows]
-        term = terms[steps : steps + 1]
-        bodies[steps][:rows] = block
-        bodies[steps][rows : rows + 1, :freqs] = term
-        edge = jnp.where(tile == 0, block[:, pixels - OV :], block[:, :OV])
-        edges[steps][:rows, :OV] = edge
-        edges[steps][rows : rows + 1, :] = term
-
-
-def last_order(half):
-    far = range(1, half)
-    return [("body", n) for n in far] + [("edge", n) for n in far] + [("edge", 0)]
-
-
-def place_kernel(half, term_scale, *refs):
-    own, *moved = refs[: 2 * half]
-    moved = dict(zip(last_order(half), moved))
-    bodies = [own] + [moved["body", n] for n in range(1, half)]
-    edges = [moved["edge", n] for n in range(half)]
-    out, source = refs[2 * half :]
+    near, far = window[:rows], window[rows:]
+
+    def edge(block):
+        return jnp.where(tile == 0, block[:, pixels - OV :], block[:, :OV])
+
+    rest = jnp.zeros((rows, pixels - OV), F32)
+    strip_near = jnp.concatenate([edge(near), rest], axis=1)
+    strip_far = jnp.concatenate([edge(far), rest], axis=1)
+    low = src < half
+    for target, rows_low, n_low, rows_high, n_high in (
+        (own, near, 0, near, 0),
+        (pay_a, far, 1, strip_near, 0),
+        (pay_b, strip_far, 1, far, 1),
+        (pay_c, strip_near, 0, strip_far, 1),
+    ):
+        target[:rows] = jnp.where(low, rows_low, rows_high)
+        target[rows : rows + 1, :freqs] = jnp.where(
+            low, terms[n_low : n_low + 1], terms[n_high : n_high + 1]
+        )
+
+
+def place_kernel(half, term_scale, own, got_a, got_b, got_c, out, source):
     rows, pixels = out.shape[1:]
     per_device = source.shape[1]
     src, tile = lax.axis_index("src"), lax.axis_index("tile")
-    steps = jnp.where(src < half, half - 1 - src, src - half)
-
-    def mine(refs, *index):
-        value = refs[0][index]
-        for n in range(1, half):
-            value = jnp.where(steps == n, refs[n][index], value)
-        return value
-
-    body = mine(bodies, slice(0, rows), slice(None))
-    edge = mine(edges, slice(0, rows), slice(0, OV))
-    zero = jnp.zeros_like(edge)
+    low, hub = src < half, (src == half - 1) | (src == half)
+
+    def pick(low_hub, low_end, high_hub, high_end, *index):
+        at_hub = jnp.where(low, low_hub[index], high_hub[index])
+        at_end = jnp.where(low, low_end[index], high_end[index])
+        return jnp.where(hub, at_hub, at_end)
+
+    bodies, strips = (own, got_a, own, got_b), (got_c, got_b, got_a, got_c)
+    body = pick(*bodies, slice(0, rows), slice(None))
+    strip = pick(*strips, slice(0, rows), slice(0, OV))
+    zero = jnp.zeros_like(strip)
     middle = jnp.zeros((rows, pixels - 2 * OV), F32)
-    low, high = jnp.where(tile == 1, edge, zero), jnp.where(tile == 0, edge, zero)
-    out[0] = body + jnp.concatenate([low, middle, high], axis=1)
+    left, right = jnp.where(tile == 1, strip, zero), jnp.where(tile == 0, strip, zero)
+    out[0] = body + jnp.concatenate([left, middle, right], axis=1)
     term = slice(rows, rows + 1), slice(0, per_device)
-    source[...] = (mine(bodies, *term) + mine(edges, *term)) * term_scale
-
-
-def call(kernel, outs, scratch=(), kind=F32, hbm=0):
+    source[...] = (pick(*bodies, *term) + pick(*strips, *term)) * term_scale
+
+
+def call(kernel, outs, scratch=(), kind=F32, hbm=0, hub=False):
+    def at_hub(*refs):
+        src, half = lax.axis_index("src"), lax.axis_size("src") // 2
+        pl.when((src == half - 1) | (src == half))(functools.partial(kernel, *refs))
+
     kinds = kind if isinstance(kind, list) else [kind] * len(outs)
     held = {"in_specs": [pl.BlockSpec(memory_space=pltpu.HBM)] * hbm} if hbm else {}
     return pl.pallas_call(
-        kernel,
+        at_hub if hub else kernel,
         out_shape=[jax.ShapeDtypeStruct(o, k) for o, k in zip(outs, kinds)],
         out_specs=[pl.BlockSpec(memory_space=pltpu.VMEM) for _ in outs],
         scratch_shapes=list(scratch),
@@ -420,6 +423,7 @@
         functools.partial(spectrum_kernel, half, order),
         [(2 * freqs, freqs), (src_count, rows, pixels), (half, PAD, pixels)],
         [pltpu.VMEM((2 * pixels, freqs), F32)],
+        hub=True,
     )(*blocks, *tables)
     spec_other = swap_rows(spec)
 
@@ -431,11 +435,13 @@
         [*outs, (count, 2 * freqs, freqs), shape, shape],
         [pltpu.VMEM((count * part, 2 * freqs), BF16)] * 2,
         kind=[F32, F32, F32, BF16, BF16],
+        hub=True,
     )(phase, *phases, spec, spec_other, meta, goal, *tables)
     second = call(
         functools.partial(fields_kernel, per_device, sources, part, half),
         outs,
         [pltpu.VMEM((count * part, 2 * freqs), BF16)] * 2,
+        hub=True,
     )(meta, goal, amp_h, amp_l, *tables)
     fields = [first, second]
     others = [swap_rows(light) for _, light in fields]
@@ -446,36 +452,53 @@
             [(2 * freqs + PAD, freqs)],
             [pltpu.VMEM((part, pixels), F32)]
             + [pltpu.VMEM((2 * part, count * freqs), BF16)] * 2,
+            hub=True,
         )(*grad, field, pupil, light, other, meta, *tables)
     (grad,) = grad
     grad_other = swap_rows(grad)
 
-    outs = call(
-        functools.partial(window_kernel, half),
-        [(rows + PAD, pixels)] * half + [(rows + PAD, freqs)] * half,
+    own, pay_a, pay_b, pay_c = call(
+        functools.partial(window_kernel, half), [(rows + PAD, pixels)] * 4, hub=True
     )(grad, grad_other, *tables)
-    bodies, edges = outs[:half], outs[half:]
-
-    def from_hub(x, steps, flip):
-        return permute(
-            x,
-            {
-                (chip(low, 0), t, c): (
-                    chip(low, steps),
-                    1 - t if flip else t,
-                    1 - c if steps else c,
-                )
-                for low in halves
-                for t, c in cores
-            },
-        )
-
-    bodies = [bodies[0]] + [from_hub(bodies[n], n, False) for n in range(1, half)]
-    edges = [from_hub(edges[n], n, True) for n in range(half)]
+    low_end, low_hub, high_hub, high_end = chip(True, 1), chip(True, 0), chip(False, 0), chip(False, 1)
+
+    def moves(*chips):
+        return {
+            (z, t, c): (to, t ^ tile_flip, c ^ core_flip)
+            for z, to, tile_flip, core_flip in chips
+            for t, c in cores
+        }
+
+    got_a = permute(
+        pay_a,
+        moves(
+            (low_hub, low_end, 0, 1),
+            (high_hub, high_hub, 1, 0),
+            (low_end, high_end, 0, 0),
+            (high_end, low_hub, 0, 0),
+        ),
+    )
+    got_b = permute(
+        pay_b,
+        moves(
+            (low_hub, low_end, 1, 1),
+            (high_hub, high_end, 0, 1),
+            (low_end, low_hub, 0, 1),
+            (high_end, high_hub, 0, 1),
+        ),
+    )
+    got_c = permute(
+        pay_c,
+        moves(
+            (low_hub, low_hub, 1, 0),
+            (high_hub, high_end, 1, 1),
+            (high_end, high_hub, 0, 1),
+        ),
+    )
     out, source = call(
         functools.partial(place_kernel, half, 1.0 / (sources * pixels * tile_count)),
         [(1, rows, pixels), (1, per_device)],
-    )(bodies[0], *[dict(body=bodies, edge=edges)[k][n] for k, n in last_order(half)])
+    )(own, got_a, got_b, got_c)
     return out, source[0]
 
 
@@ -638,7 +661,7 @@
         mesh.shape["row"] == 2
         and mesh.shape["tile"] == 2
         and src_count % 2 == 0
-        and src_count // 2 <= PAD
+        and src_count // 2 == 2
         and per_device < PAD
         and mask_windows.shape[1] // (2 * src_count) % 16 == 0
         and pixels & (pixels - 1) == 0

time: 29.3 us -> 28.7 us (0.980)
  Pallas kernels: 9.78 us -> 2.51 us
  starting transfers between devices: 9.3 us -> 14.8 us
  waiting for transfers between devices: 9.29 us -> 10.5 us
    ppermute x8, starting transfers between devices: 8.46 us -> 14 us  [permute(): lax.ppermute(x, ('src', 'tile', 'row'), [(flat[a], flat[b]) for a, b in p...]
    pallas_call x2, Pallas kernels: 2.67 us -> 0.01 us  [hub_shards(): call(functools.partial(adjoint_kernel, per_device, sources, first_row, ro...]
    pallas_call x1, Pallas kernels: 1.99 us -> 0.01 us  [hub_shards(): call(functools.partial(fields_kernel, per_device, sources, 0, half), [*ou...]
    pallas_call x1, Pallas kernels: 1.32 us -> 0.02 us  [hub_shards(): call(functools.partial(fields_kernel, per_device, sources, part, half), o...]
    ppermute x4, waiting for transfers between devices: 1.28 us -> 2.34 us  [swap_rows(): return lax.ppermute(x, 'row', [(0, 1), (1, 0)])]
    pallas_call x1, Pallas kernels: 0.69 us -> 0.01 us  [hub_shards(): call(functools.partial(spectrum_kernel, half, order), [(2 * freqs, freqs)...]
    pallas_call x1, Pallas kernels: 0.62 us -> 0.01 us  [hub_shards(): call(functools.partial(window_kernel, half), [(rows + PAD, pixels)] * 4,...]
  transfers between devices with their start and end apart: 12 -> 12, of which waited for: 4 -> 7; matrix products, arithmetic and copies ran while one was open for 0% -> 0% of each run, Pallas kernels for 15% -> 3%
where the time goes in v6:
time: 28.7 us; the launch traced here: 28.5 us
  starting transfers between devices  14.8 us (52%)
  waiting for transfers between devices  10.5 us (37%)
  Pallas kernels  2.51 us (9%)
  between operations  0.68 us (2%)
    ppermute x8, starting transfers between devices, permute(): lax.ppermute(x, ('src', 'tile', 'row'), [(flat[a], flat[b]) for a, b in p...  14 us
    ppermute x8, waiting for transfers between devices, permute(): lax.ppermute(x, ('src', 'tile', 'row'), [(flat[a], flat[b]) for a, b in p...  8.14 us
    ppermute x4, waiting for transfers between devices, swap_rows(): return lax.ppermute(x, 'row', [(0, 1), (1, 0)])  2.34 us
    pallas_call x1, Pallas kernels, hub_shards(): call(tables_kernel, [(2 * freqs, 2 * pixels)] * 2 + [(2 * pixels, 2 * fre...  0.97 us
    pallas_call x1, Pallas kernels, hub_shards(): call(fetch_kernel, [(2 * rows + PAD, pixels)], [pltpu.VMEM((per_device, 2...  0.82 us
    ppermute x4, starting transfers between devices, swap_rows(): return lax.ppermute(x, 'row', [(0, 1), (1, 0)])  0.77 us
    pallas_call x1, Pallas kernels, hub_shards(): call(functools.partial(place_kernel, half, 1.0 / (sources * pixels * tile...  0.7 us
  transfers between devices with their start and end apart: 12, of which 7 were waited for; matrix products, arithmetic and copies ran while one was open for 0% of the time, Pallas kernels for 3%

profile of v6, /device:TPU:0, one launch (start us, length us, event | category | flops | bytes accessed | tf_op | source)
XLA Modules:
  0.0 28.5 jit_solution(9648763561535111717)
XLA Ops:
  0.6 0.8 %shard_map.69.refs_0_ = f32[72,256]{1,0:T(8,128)S(1)} custom-call(f32[1,32,256]{2,1,0:T(8,128)} %mask.1, f32[1,32,256]{2,1,0:T(8,128)} %goal.1, s32[3,2,128]{2,1,0:T(2,128)} %bitcast.3, f32[1,3]{1,0:T(1,128)} %bitcast.4), custom_call_target="tpu_custom_call" | custom-call | tf_op jit(solution)/shard_map/pallas_call | solution.py:396
  1.5 4.1 %collective-permute-start.4 = (f32[72,256]{1,0:T(8,128)S(1)}, f32[72,256]{1,0:T(8,128)S(1)}, u32[]{:S(2)}, u32[]{:S(2)}) collective-permute-start(f32[72,256]{1,0:T(8,128)S(1)} %shard_map.69.refs_0_), channel_id=1, source_target_pairs={{0,8},{1,9},{2,10},{3,11},{12,4},{13,5},{14,6},{15,7},{4,0},{5,1},... | collective-permute-start | bytes 221192 | tf_op jit(solution)/shard_map/ppermute | solution.py:356
  5.5 0.0 collective-permute-start.3
  5.5 0.0 collective-permute-start.2
  5.6 2.5 %collective-permute-start.1 = (f32[3,128,128]{2,1,0:T(8,128)}, f32[3,128,128]{2,1,0:T(8,128)S(1)}, u32[]{:S(2)}, u32[]{:S(2)}) collective-permute-start(f32[3,128,128]{2,1,0:T(8,128)} %phase.1), channel_id=1, source_target_pairs={{0,4},{1,9},{2,6},{3,11},{12,8},{13,5},{14,10},{15,7},{4,0},{5,1},... | collective-permute-start | bytes 589832 | tf_op jit(solution)/shard_map/ppermute | solution.py:356
  8.0 0.0 collective-permute-start
  8.0 1.0 %shard_map.68 = (bf16[256,512]{1,0:T(8,128)(2,1)S(1)}, bf16[256,512]{1,0:T(8,128)(2,1)S(1)}, bf16[512,256]{1,0:T(8,128)(2,1)S(1)}, bf16[512,256]{1,0:T(8,128)(2,1)S(1)}, f32[3,128,128]{2,1,0:T(8,128)S(1)}) custom-call(f32[3,128,128]{2,1,0:T(8,128)} %phase.1), custom_call_target="tpu_custom_call" | custom-call | tf_op jit(solution)/shard_map/pallas_call | solution.py:414
  9.0 0.0 collective-permute-done.4.refs_3_
  9.0 1.7 %collective-permute-done.3.refs_2_ = f32[72,256]{1,0:T(8,128)S(1)} collective-permute-done((f32[72,256]{1,0:T(8,128)S(1)}, f32[72,256]{1,0:T(8,128)S(1)}, u32[]{:S(2)}, u32[]{:S(2)}) %collective-permute-start.3) | collective-permute-done | bytes 73760 | tf_op jit(solution)/shard_map/ppermute | solution.py:356
  10.7 0.0 collective-permute-done.2.refs_1_
  10.7 0.0 collective-permute-start.5
  10.7 3.2 %collective-permute-done.1.refs_2_ = f32[3,128,128]{2,1,0:T(8,128)S(1)} collective-permute-done((f32[3,128,128]{2,1,0:T(8,128)}, f32[3,128,128]{2,1,0:T(8,128)S(1)}, u32[]{:S(2)}, u32[]{:S(2)}) %collective-permute-start.1) | collective-permute-done | bytes 196640 | tf_op jit(solution)/shard_map/ppermute | solution.py:356
  13.9 0.0 collective-permute-done.refs_1_
  13.9 0.0 collective-permute-done.5.refs_4_
  13.9 0.1 collective-permute-start.6
  14.0 0.5 %collective-permute-start.7 = (f32[192,256]{1,0:T(8,128)S(1)}, f32[192,256]{1,0:T(8,128)S(1)}, u32[]{:S(2)}, u32[]{:S(2)}) collective-permute-start(f32[192,256]{1,0:T(8,128)S(1)} %get-tuple-element.37.refs_3_), channel_id=1, source_target_pairs={{0,1},{1,0},{2,3},{3,2},{4,5},{5,4},{6,7},{7,6},{8,9},{9,8},{10,11... | collective-permute-start | bytes 589832 | tf_op jit(solution)/shard_map/ppermute | solution.py:360
  14.4 0.9 %collective-permute-done.6.refs_3_ = f32[192,256]{1,0:T(8,128)S(1)} collective-permute-done((f32[192,256]{1,0:T(8,128)S(1)}, f32[192,256]{1,0:T(8,128)S(1)}, u32[]{:S(2)}, u32[]{:S(2)}) %collective-permute-start.6) | collective-permute-done | bytes 196640 | tf_op jit(solution)/shard_map/ppermute | solution.py:360
  15.4 0.3 collective-permute-done.7.refs_4_
  15.7 0.2 collective-permute-start.8
  15.9 1.1 %collective-permute-done.8.refs_1_ = f32[264,128]{1,0:T(8,128)S(1)} collective-permute-done((f32[264,128]{1,0:T(8,128)S(1)}, f32[264,128]{1,0:T(8,128)S(1)}, u32[]{:S(2)}, u32[]{:S(2)}) %collective-permute-start.8) | collective-permute-done | bytes 135200 | tf_op jit(solution)/shard_map/ppermute | solution.py:360
  17.0 2.5 %collective-permute-start.9 = (f32[40,256]{1,0:T(8,128)S(1)}, f32[40,256]{1,0:T(8,128)S(1)}, u32[]{:S(2)}, u32[]{:S(2)}) collective-permute-start(f32[40,256]{1,0:T(8,128)S(1)} %get-tuple-element.39), channel_id=1, source_target_pairs={{4,1},{5,0},{6,3},{7,2},{8,10},{9,11},{10,8},{11,9},{0,12},{1,13},... | collective-permute-start | bytes 122888 | tf_op jit(solution)/shard_map/ppermute | solution.py:356
  19.5 4.7 %collective-permute-start.10 = (f32[40,256]{1,0:T(8,128)S(1)}, f32[40,256]{1,0:T(8,128)S(1)}, u32[]{:S(2)}, u32[]{:S(2)}) collective-permute-start(f32[40,256]{1,0:T(8,128)S(1)} %get-tuple-element.40), channel_id=1, source_target_pairs={{4,3},{5,2},{6,1},{7,0},{8,13},{9,12},{10,15},{11,14},{0,5},{1,4},... | collective-permute-start | bytes 122888 | tf_op jit(solution)/shard_map/ppermute | solution.py:356
  24.2 0.2 collective-permute-start.11
  24.5 1.5 %collective-permute-done.9.got_a = f32[40,256]{1,0:T(8,128)S(1)} collective-permute-done((f32[40,256]{1,0:T(8,128)S(1)}, f32[40,256]{1,0:T(8,128)S(1)}, u32[]{:S(2)}, u32[]{:S(2)}) %collective-permute-start.9) | collective-permute-done | bytes 40992 | tf_op jit(solution)/shard_map/ppermute | solution.py:356
  25.9 1.8 %collective-permute-done.10.got_b = f32[40,256]{1,0:T(8,128)S(1)} collective-permute-done((f32[40,256]{1,0:T(8,128)S(1)}, f32[40,256]{1,0:T(8,128)S(1)}, u32[]{:S(2)}, u32[]{:S(2)}) %collective-permute-start.10) | collective-permute-done | bytes 40992 | tf_op jit(solution)/shard_map/ppermute | solution.py:356
  27.8 0.0 collective-permute-done.11.got_c
  27.8 0.7 %shard_map.76 = (f32[1,32,256]{2,1,0:T(8,128)}, f32[1,3]{1,0:T(1,128)}) custom-call(f32[40,256]{1,0:T(8,128)S(1)} %get-tuple-element.38.own, f32[40,256]{1,0:T(8,128)S(1)} %collective-permute-done.9.got_a, f32[40,256]{1,0:T(8,128)S(1)} %collective-permute-done.10.got_b, f32[40,256]{1,0:T(8,128)S(1)} %collective-permute-done.11.got_c), custom_call_target="tpu_custom_call" | custom-call | tf_op jit(solution)/shard_map/pallas_call | solution.py:498
  (6 shorter events, 0.0 us)
Async XLA Ops:
  1.5 7.5 %collective-permute-start.4 = (f32[72,256]{1,0:T(8,128)S(1)}, f32[72,256]{1,0:T(8,128)S(1)}, u32[]{:S(2)}, u32[]{:S(2)}) collective-permute-start(f32[72,256]{1,0:T(8,128)S(1)} %shard_map.69.refs_0_), channel_id=1, source_target_pairs={{0,8},{1,9},{2,10},{3,11},{12,4},{13,5},{14,6},{15,7},{4,0},{5,1},... | collective-permute-start | bytes 221192 | tf_op jit(solution)/shard_map/ppermute | solution.py:356
  5.5 5.1 %collective-permute-start.3 = (f32[72,256]{1,0:T(8,128)S(1)}, f32[72,256]{1,0:T(8,128)S(1)}, u32[]{:S(2)}, u32[]{:S(2)}) collective-permute-start(f32[72,256]{1,0:T(8,128)S(1)} %shard_map.69.refs_0_), channel_id=1, source_target_pairs={{0,4},{1,5},{2,6},{3,7},{12,8},{13,9},{14,10},{15,11},{4,0},{5,1},... | collective-permute-start | bytes 221192 | tf_op jit(solution)/shard_map/ppermute | solution.py:356
  5.5 5.1 %collective-permute-start.2 = (f32[72,256]{1,0:T(8,128)S(1)}, f32[72,256]{1,0:T(8,128)S(1)}, u32[]{:S(2)}, u32[]{:S(2)}) collective-permute-start(f32[72,256]{1,0:T(8,128)S(1)} %shard_map.69.refs_0_), channel_id=1, source_target_pairs={{4,8},{5,9},{6,10},{7,11},{8,4},{9,5},{10,6},{11,7},{0,1},{1,0},{2... | collective-permute-start | bytes 221192 | tf_op jit(solution)/shard_map/ppermute | solution.py:356
  5.6 8.3 %collective-permute-start.1 = (f32[3,128,128]{2,1,0:T(8,128)}, f32[3,128,128]{2,1,0:T(8,128)S(1)}, u32[]{:S(2)}, u32[]{:S(2)}) collective-permute-start(f32[3,128,128]{2,1,0:T(8,128)} %phase.1), channel_id=1, source_target_pairs={{0,4},{1,9},{2,6},{3,11},{12,8},{13,5},{14,10},{15,7},{4,0},{5,1},... | collective-permute-start | bytes 589832 | tf_op jit(solution)/shard_map/ppermute | solution.py:356
  8.0 5.8 %collective-permute-start = (f32[3,128,128]{2,1,0:T(8,128)}, f32[3,128,128]{2,1,0:T(8,128)S(1)}, u32[]{:S(2)}, u32[]{:S(2)}) collective-permute-start(f32[3,128,128]{2,1,0:T(8,128)} %phase.1), channel_id=1, source_target_pairs={{4,9},{6,11},{8,5},{10,7},{0,1},{1,0},{2,3},{3,2},{5,4},{7,6},{9,8... | collective-permute-start | bytes 589832 | tf_op jit(solution)/shard_map/ppermute | solution.py:356
  10.7 3.2 %collective-permute-start.5 = (f32[256,128]{1,0:T(8,128)S(1)}, f32[256,128]{1,0:T(8,128)S(1)}, u32[]{:S(2)}, u32[]{:S(2)}) collective-permute-start(f32[256,128]{1,0:T(8,128)S(1)} %get-tuple-element.28.refs_3_), channel_id=1, source_target_pairs={{0,1},{1,0},{2,3},{3,2},{4,5},{5,4},{6,7},{7,6},{8,9},{9,8},{10,11... | collective-permute-start | bytes 393224 | tf_op jit(solution)/shard_map/ppermute | solution.py:360
  13.9 1.5 %collective-permute-start.6 = (f32[192,256]{1,0:T(8,128)S(1)}, f32[192,256]{1,0:T(8,128)S(1)}, u32[]{:S(2)}, u32[]{:S(2)}) collective-permute-start(f32[192,256]{1,0:T(8,128)S(1)} %get-tuple-element.33.refs_2_), channel_id=1, source_target_pairs={{0,1},{1,0},{2,3},{3,2},{4,5},{5,4},{6,7},{7,6},{8,9},{9,8},{10,11... | collective-permute-start | bytes 589832 | tf_op jit(solution)/shard_map/ppermute | solution.py:360
  14.0 1.7 %collective-permute-start.7 = (f32[192,256]{1,0:T(8,128)S(1)}, f32[192,256]{1,0:T(8,128)S(1)}, u32[]{:S(2)}, u32[]{:S(2)}) collective-permute-start(f32[192,256]{1,0:T(8,128)S(1)} %get-tuple-element.37.refs_3_), channel_id=1, source_target_pairs={{0,1},{1,0},{2,3},{3,2},{4,5},{5,4},{6,7},{7,6},{8,9},{9,8},{10,11... | collective-permute-start | bytes 589832 | tf_op jit(solution)/shard_map/ppermute | solution.py:360
  15.7 1.4 %collective-permute-start.8 = (f32[264,128]{1,0:T(8,128)S(1)}, f32[264,128]{1,0:T(8,128)S(1)}, u32[]{:S(2)}, u32[]{:S(2)}) collective-permute-start(f32[264,128]{1,0:T(8,128)S(1)} %shard_map.74.refs_0_), channel_id=1, source_target_pairs={{0,1},{1,0},{2,3},{3,2},{4,5},{5,4},{6,7},{7,6},{8,9},{9,8},{10,11... | collective-permute-start | bytes 405512 | tf_op jit(solution)/shard_map/ppermute | solution.py:360
  17.0 8.9 %collective-permute-start.9 = (f32[40,256]{1,0:T(8,128)S(1)}, f32[40,256]{1,0:T(8,128)S(1)}, u32[]{:S(2)}, u32[]{:S(2)}) collective-permute-start(f32[40,256]{1,0:T(8,128)S(1)} %get-tuple-element.39), channel_id=1, source_target_pairs={{4,1},{5,0},{6,3},{7,2},{8,10},{9,11},{10,8},{11,9},{0,12},{1,13},... | collective-permute-start | bytes 122888 | tf_op jit(solution)/shard_map/ppermute | solution.py:356
  19.5 8.2 %collective-permute-start.10 = (f32[40,256]{1,0:T(8,128)S(1)}, f32[40,256]{1,0:T(8,128)S(1)}, u32[]{:S(2)}, u32[]{:S(2)}) collective-permute-start(f32[40,256]{1,0:T(8,128)S(1)} %get-tuple-element.40), channel_id=1, source_target_pairs={{4,3},{5,2},{6,1},{7,0},{8,13},{9,12},{10,15},{11,14},{0,5},{1,4},... | collective-permute-start | bytes 122888 | tf_op jit(solution)/shard_map/ppermute | solution.py:356
  24.2 3.5 %collective-permute-start.11 = (f32[40,256]{1,0:T(8,128)S(1)}, f32[40,256]{1,0:T(8,128)S(1)}, u32[]{:S(2)}, u32[]{:S(2)}) collective-permute-start(f32[40,256]{1,0:T(8,128)S(1)} %get-tuple-element.41), channel_id=1, source_target_pairs={{4,6},{5,7},{6,4},{7,5},{8,15},{9,14},{10,13},{11,12},{12,9},{13,8... | collective-permute-start | bytes 122888 | tf_op jit(solution)/shard_map/ppermute | solution.py:356

commit v7 on v6

--- a/solution.py
+++ b/solution.py
@@ -260,7 +260,8 @@
         grad[place] = value + before[0][place] if before else value
 
 
-def window_kernel(half, grad_a, grad_b, fwd_h, fwd_l, adj_h, adj_l, own, pay_a, pay_b, pay_c):
+def window_kernel(half, grad_a, grad_b, fwd_h, fwd_l, adj_h, adj_l, own, *pays):
+    pay_a, pay_b, pay_c, pay_d = pays
     rows, pixels = own.shape[0] - PAD, own.shape[1]
     freqs = grad_a.shape[1]
     src, row, tile = lax.axis_index("src"), lax.axis_index("row"), lax.axis_index("tile")
@@ -282,23 +283,33 @@
     def edge(block):
         return jnp.where(tile == 0, block[:, pixels - OV :], block[:, :OV])
 
-    rest = jnp.zeros((rows, pixels - OV), F32)
-    strip_near = jnp.concatenate([edge(near), rest], axis=1)
-    strip_far = jnp.concatenate([edge(far), rest], axis=1)
-    low = src < half
-    for target, rows_low, n_low, rows_high, n_high in (
-        (own, near, 0, near, 0),
-        (pay_a, far, 1, strip_near, 0),
-        (pay_b, strip_far, 1, far, 1),
-        (pay_c, strip_near, 0, strip_far, 1),
-    ):
-        target[:rows] = jnp.where(low, rows_low, rows_high)
-        target[rows : rows + 1, :freqs] = jnp.where(
-            low, terms[n_low : n_low + 1], terms[n_high : n_high + 1]
-        )
-
-
-def place_kernel(half, term_scale, own, got_a, got_b, got_c, out, source):
+    def put_rows(target, block, n):
+        target[:rows] = block
+        target[rows : rows + 1, :freqs] = terms[n : n + 1]
+
+    def put_strip(target, block, n):
+        block = edge(block)
+        lines = range(0, rows, PAD)
+        block = jnp.concatenate([block[i : i + PAD] for i in lines], axis=1)
+        target[:PAD, : block.shape[1]] = block
+        target[PAD : PAD + 1, :freqs] = terms[n : n + 1]
+
+    put_rows(own, near, 0)
+    put_rows(pay_b, far, 1)
+    put_strip(pay_c, far, 1)
+
+    @pl.when(src < half)
+    def _():
+        put_rows(pay_a, far, 1)
+        put_strip(pay_d, near, 0)
+
+    @pl.when(src >= half)
+    def _():
+        put_strip(pay_a, near, 0)
+        put_strip(pay_d, far, 1)
+
+
+def place_kernel(half, term_scale, own, got_a, got_b, got_c, got_d, out, source):
     rows, pixels = out.shape[1:]
     per_device = source.shape[1]
     src, tile = lax.axis_index("src"), lax.axis_index("tile")
@@ -309,15 +320,18 @@
         at_end = jnp.where(low, low_end[index], high_end[index])
         return jnp.where(hub, at_hub, at_end)
 
-    bodies, strips = (own, got_a, own, got_b), (got_c, got_b, got_a, got_c)
+    bodies, strips = (own, got_a, own, got_b), (got_d, got_c, got_a, got_d)
     body = pick(*bodies, slice(0, rows), slice(None))
-    strip = pick(*strips, slice(0, rows), slice(0, OV))
+    strip = pick(*strips, slice(0, PAD), slice(0, rows // PAD * OV))
+    places = range(0, rows // PAD * OV, OV)
+    strip = jnp.concatenate([strip[:, i : i + OV] for i in places], axis=0)
     zero = jnp.zeros_like(strip)
     middle = jnp.zeros((rows, pixels - 2 * OV), F32)
     left, right = jnp.where(tile == 1, strip, zero), jnp.where(tile == 0, strip, zero)
     out[0] = body + jnp.concatenate([left, middle, right], axis=1)
-    term = slice(rows, rows + 1), slice(0, per_device)
-    source[...] = (pick(*bodies, *term) + pick(*strips, *term)) * term_scale
+    own_terms = pick(*bodies, slice(rows, rows + 1), slice(0, per_device))
+    other_terms = pick(*strips, slice(PAD, PAD + 1), slice(0, per_device))
+    source[...] = (own_terms + other_terms) * term_scale
 
 
 def call(kernel, outs, scratch=(), kind=F32, hbm=0, hub=False):
@@ -457,8 +471,9 @@
     (grad,) = grad
     grad_other = swap_rows(grad)
 
-    own, pay_a, pay_b, pay_c = call(
-        functools.partial(window_kernel, half), [(rows + PAD, pixels)] * 4, hub=True
+    wide, narrow = (rows + PAD, pixels), (2 * PAD, max(freqs, rows // PAD * OV))
+    own, pay_a, pay_b, pay_c, pay_d = call(
+        functools.partial(window_kernel, half), [wide] * 3 + [narrow] * 2, hub=True
     )(grad, grad_other, *tables)
     low_end, low_hub, high_hub, high_end = chip(True, 1), chip(True, 0), chip(False, 0), chip(False, 1)
 
@@ -478,27 +493,16 @@
             (high_end, low_hub, 0, 0),
         ),
     )
-    got_b = permute(
-        pay_b,
-        moves(
-            (low_hub, low_end, 1, 1),
-            (high_hub, high_end, 0, 1),
-            (low_end, low_hub, 0, 1),
-            (high_end, high_hub, 0, 1),
-        ),
-    )
-    got_c = permute(
-        pay_c,
-        moves(
-            (low_hub, low_hub, 1, 0),
-            (high_hub, high_end, 1, 1),
-            (high_end, high_hub, 0, 1),
-        ),
+    got_b = permute(pay_b, moves((high_hub, high_end, 0, 1), (high_end, high_hub, 0, 1)))
+    got_c = permute(pay_c, moves((low_hub, low_end, 1, 1), (low_end, low_hub, 0, 1)))
+    got_d = permute(
+        pay_d,
+        moves((low_hub, low_hub, 1, 0), (high_hub, high_end, 1, 1), (high_end, high_hub, 0, 1)),
     )
     out, source = call(
         functools.partial(place_kernel, half, 1.0 / (sources * pixels * tile_count)),
         [(1, rows, pixels), (1, per_device)],
-    )(own, got_a, got_b, got_c)
+    )(own, got_a, got_b, got_c, got_d)
     return out, source[0]
 
 

time: 28.7 us -> 28 us (0.976)
  waiting for transfers between devices: 10.5 us -> 9.52 us
    ppermute x8 -> x9, waiting for transfers between devices: 8.14 us -> 7.18 us  [permute(): lax.ppermute(x, ('src', 'tile', 'row'), [(flat[a], flat[b]) for a, b in p...]
    ppermute x8 -> x9, starting transfers between devices: 14 us -> 14.3 us  [permute(): lax.ppermute(x, ('src', 'tile', 'row'), [(flat[a], flat[b]) for a, b in p...]
  transfers between devices with their start and end apart: 12 -> 13, of which waited for: 7 -> 6; matrix products, arithmetic and copies ran while one was open for 0% -> 0% of each run, Pallas kernels for 3% -> 4%
where the time goes in v7:
time: 28 us; the launch traced here: 27.8 us
  starting transfers between devices  15 us (54%)
  waiting for transfers between devices  9.52 us (34%)
  Pallas kernels  2.58 us (9%)
  between operations  0.69 us (2%)
    ppermute x9, starting transfers between devices, permute(): lax.ppermute(x, ('src', 'tile', 'row'), [(flat[a], flat[b]) for a, b in p...  14.3 us
    ppermute x9, waiting for transfers between devices, permute(): lax.ppermute(x, ('src', 'tile', 'row'), [(flat[a], flat[b]) for a, b in p...  7.18 us
    ppermute x4, waiting for transfers between devices, swap_rows(): return lax.ppermute(x, 'row', [(0, 1), (1, 0)])  2.34 us
    pallas_call x1, Pallas kernels, hub_shards(): call(tables_kernel, [(2 * freqs, 2 * pixels)] * 2 + [(2 * pixels, 2 * fre...  0.97 us
    pallas_call x1, Pallas kernels, hub_shards(): call(fetch_kernel, [(2 * rows + PAD, pixels)], [pltpu.VMEM((per_device, 2...  0.82 us
    pallas_call x1, Pallas kernels, hub_shards(): call(functools.partial(place_kernel, half, 1.0 / (sources * pixels * tile...  0.77 us
    ppermute x4, starting transfers between devices, swap_rows(): return lax.ppermute(x, 'row', [(0, 1), (1, 0)])  0.77 us
  transfers between devices with their start and end apart: 13, of which 6 were waited for; matrix products, arithmetic and copies ran while one was open for 0% of the time, Pallas kernels for 4%

profile of v7, /device:TPU:0, one launch (start us, length us, event | category | flops | bytes accessed | tf_op | source)
XLA Modules:
  0.0 27.8 jit_solution(11224821411958170844)
XLA Ops:
  0.6 0.8 %shard_map.69.refs_0_ = f32[72,256]{1,0:T(8,128)S(1)} custom-call(f32[1,32,256]{2,1,0:T(8,128)} %mask.1, f32[1,32,256]{2,1,0:T(8,128)} %goal.1, s32[3,2,128]{2,1,0:T(2,128)} %bitcast.3, f32[1,3]{1,0:T(1,128)} %bitcast.4), custom_call_target="tpu_custom_call" | custom-call | tf_op jit(solution)/shard_map/pallas_call | solution.py:410
  1.5 4.1 %collective-permute-start.4 = (f32[72,256]{1,0:T(8,128)S(1)}, f32[72,256]{1,0:T(8,128)S(1)}, u32[]{:S(2)}, u32[]{:S(2)}) collective-permute-start(f32[72,256]{1,0:T(8,128)S(1)} %shard_map.69.refs_0_), channel_id=1, source_target_pairs={{0,8},{1,9},{2,10},{3,11},{12,4},{13,5},{14,6},{15,7},{4,0},{5,1},... | collective-permute-start | bytes 221192 | tf_op jit(solution)/shard_map/ppermute | solution.py:370
  5.5 0.0 collective-permute-start.3
  5.5 0.0 collective-permute-start.2
  5.6 2.5 %collective-permute-start.1 = (f32[3,128,128]{2,1,0:T(8,128)}, f32[3,128,128]{2,1,0:T(8,128)S(1)}, u32[]{:S(2)}, u32[]{:S(2)}) collective-permute-start(f32[3,128,128]{2,1,0:T(8,128)} %phase.1), channel_id=1, source_target_pairs={{0,4},{1,9},{2,6},{3,11},{12,8},{13,5},{14,10},{15,7},{4,0},{5,1},... | collective-permute-start | bytes 589832 | tf_op jit(solution)/shard_map/ppermute | solution.py:370
  8.0 0.0 collective-permute-start
  8.0 1.0 %shard_map.68 = (bf16[256,512]{1,0:T(8,128)(2,1)S(1)}, bf16[256,512]{1,0:T(8,128)(2,1)S(1)}, bf16[512,256]{1,0:T(8,128)(2,1)S(1)}, bf16[512,256]{1,0:T(8,128)(2,1)S(1)}, f32[3,128,128]{2,1,0:T(8,128)S(1)}) custom-call(f32[3,128,128]{2,1,0:T(8,128)} %phase.1), custom_call_target="tpu_custom_call" | custom-call | tf_op jit(solution)/shard_map/pallas_call | solution.py:428
  9.0 0.0 collective-permute-done.4.refs_3_
  9.0 1.7 %collective-permute-done.3.refs_2_ = f32[72,256]{1,0:T(8,128)S(1)} collective-permute-done((f32[72,256]{1,0:T(8,128)S(1)}, f32[72,256]{1,0:T(8,128)S(1)}, u32[]{:S(2)}, u32[]{:S(2)}) %collective-permute-start.3) | collective-permute-done | bytes 73760 | tf_op jit(solution)/shard_map/ppermute | solution.py:370
  10.7 0.0 collective-permute-done.2.refs_1_
  10.7 0.0 collective-permute-start.5
  10.7 3.2 %collective-permute-done.1.refs_2_ = f32[3,128,128]{2,1,0:T(8,128)S(1)} collective-permute-done((f32[3,128,128]{2,1,0:T(8,128)}, f32[3,128,128]{2,1,0:T(8,128)S(1)}, u32[]{:S(2)}, u32[]{:S(2)}) %collective-permute-start.1) | collective-permute-done | bytes 196640 | tf_op jit(solution)/shard_map/ppermute | solution.py:370
  13.9 0.0 collective-permute-done.refs_1_
  13.9 0.0 collective-permute-done.5.refs_4_
  13.9 0.1 collective-permute-start.6
  14.0 0.5 %collective-permute-start.7 = (f32[192,256]{1,0:T(8,128)S(1)}, f32[192,256]{1,0:T(8,128)S(1)}, u32[]{:S(2)}, u32[]{:S(2)}) collective-permute-start(f32[192,256]{1,0:T(8,128)S(1)} %get-tuple-element.38.refs_3_), channel_id=1, source_target_pairs={{0,1},{1,0},{2,3},{3,2},{4,5},{5,4},{6,7},{7,6},{8,9},{9,8},{10,11... | collective-permute-start | bytes 589832 | tf_op jit(solution)/shard_map/ppermute | solution.py:374
  14.4 0.9 %collective-permute-done.6.refs_3_ = f32[192,256]{1,0:T(8,128)S(1)} collective-permute-done((f32[192,256]{1,0:T(8,128)S(1)}, f32[192,256]{1,0:T(8,128)S(1)}, u32[]{:S(2)}, u32[]{:S(2)}) %collective-permute-start.6) | collective-permute-done | bytes 196640 | tf_op jit(solution)/shard_map/ppermute | solution.py:374
  15.4 0.3 %collective-permute-done.7.refs_4_ = f32[192,256]{1,0:T(8,128)S(1)} collective-permute-done((f32[192,256]{1,0:T(8,128)S(1)}, f32[192,256]{1,0:T(8,128)S(1)}, u32[]{:S(2)}, u32[]{:S(2)}) %collective-permute-start.7) | collective-permute-done | bytes 196640 | tf_op jit(solution)/shard_map/ppermute | solution.py:374
  15.7 0.2 collective-permute-start.8
  15.9 1.1 %collective-permute-done.8.refs_1_ = f32[264,128]{1,0:T(8,128)S(1)} collective-permute-done((f32[264,128]{1,0:T(8,128)S(1)}, f32[264,128]{1,0:T(8,128)S(1)}, u32[]{:S(2)}, u32[]{:S(2)}) %collective-permute-start.8) | collective-permute-done | bytes 135200 | tf_op jit(solution)/shard_map/ppermute | solution.py:374
  17.0 2.5 %collective-permute-start.9 = (f32[40,256]{1,0:T(8,128)S(1)}, f32[40,256]{1,0:T(8,128)S(1)}, u32[]{:S(2)}, u32[]{:S(2)}) collective-permute-start(f32[40,256]{1,0:T(8,128)S(1)} %get-tuple-element.40), channel_id=1, source_target_pairs={{4,1},{5,0},{6,3},{7,2},{8,10},{9,11},{10,8},{11,9},{0,12},{1,13},... | collective-permute-start | bytes 122888 | tf_op jit(solution)/shard_map/ppermute | solution.py:370
  19.5 0.0 collective-permute-start.10
  19.5 4.9 %collective-permute-start.11 = (f32[16,128]{1,0:T(8,128)S(1)}, f32[16,128]{1,0:T(8,128)S(1)}, u32[]{:S(2)}, u32[]{:S(2)}) collective-permute-start(f32[16,128]{1,0:T(8,128)S(1)} %get-tuple-element.42), channel_id=1, source_target_pairs={{4,3},{5,2},{6,1},{7,0},{0,5},{1,4},{2,7},{3,6},{8,9},{9,8},{10,11... | collective-permute-start | bytes 24584 | tf_op jit(solution)/shard_map/ppermute | solution.py:370
  24.4 0.3 collective-permute-start.12
  24.7 2.3 %collective-permute-done.11.got_c = f32[16,128]{1,0:T(8,128)S(1)} collective-permute-done((f32[16,128]{1,0:T(8,128)S(1)}, f32[16,128]{1,0:T(8,128)S(1)}, u32[]{:S(2)}, u32[]{:S(2)}) %collective-permute-start.11) | collective-permute-done | bytes 8224 | tf_op jit(solution)/shard_map/ppermute | solution.py:370
  27.0 0.0 collective-permute-done.12.got_d
  27.0 0.0 collective-permute-done.9.got_a
  27.0 0.0 collective-permute-done.10.got_b
  27.0 0.8 %shard_map.76 = (f32[1,32,256]{2,1,0:T(8,128)}, f32[1,3]{1,0:T(1,128)}) custom-call(f32[40,256]{1,0:T(8,128)S(1)} %get-tuple-element.39.own, f32[40,256]{1,0:T(8,128)S(1)} %collective-permute-done.9.got_a, f32[40,256]{1,0:T(8,128)S(1)} %collective-permute-done.10.got_b, f32[16,128]{1,0:T(8,128)S(1)} %collective-permute-done.11.got_c, ...), custom_call_target="tpu_custom_call" | custom-call | tf_op jit(solution)/shard_map/pallas_call | solution.py:502
  (6 shorter events, 0.0 us)
Async XLA Ops:
  1.5 7.5 %collective-permute-start.4 = (f32[72,256]{1,0:T(8,128)S(1)}, f32[72,256]{1,0:T(8,128)S(1)}, u32[]{:S(2)}, u32[]{:S(2)}) collective-permute-start(f32[72,256]{1,0:T(8,128)S(1)} %shard_map.69.refs_0_), channel_id=1, source_target_pairs={{0,8},{1,9},{2,10},{3,11},{12,4},{13,5},{14,6},{15,7},{4,0},{5,1},... | collective-permute-start | bytes 221192 | tf_op jit(solution)/shard_map/ppermute | solution.py:370
  5.5 5.1 %collective-permute-start.3 = (f32[72,256]{1,0:T(8,128)S(1)}, f32[72,256]{1,0:T(8,128)S(1)}, u32[]{:S(2)}, u32[]{:S(2)}) collective-permute-start(f32[72,256]{1,0:T(8,128)S(1)} %shard_map.69.refs_0_), channel_id=1, source_target_pairs={{0,4},{1,5},{2,6},{3,7},{12,8},{13,9},{14,10},{15,11},{4,0},{5,1},... | collective-permute-start | bytes 221192 | tf_op jit(solution)/shard_map/ppermute | solution.py:370
  5.5 5.1 %collective-permute-start.2 = (f32[72,256]{1,0:T(8,128)S(1)}, f32[72,256]{1,0:T(8,128)S(1)}, u32[]{:S(2)}, u32[]{:S(2)}) collective-permute-start(f32[72,256]{1,0:T(8,128)S(1)} %shard_map.69.refs_0_), channel_id=1, source_target_pairs={{4,8},{5,9},{6,10},{7,11},{8,4},{9,5},{10,6},{11,7},{0,1},{1,0},{2... | collective-permute-start | bytes 221192 | tf_op jit(solution)/shard_map/ppermute | solution.py:370
  5.6 8.3 %collective-permute-start.1 = (f32[3,128,128]{2,1,0:T(8,128)}, f32[3,128,128]{2,1,0:T(8,128)S(1)}, u32[]{:S(2)}, u32[]{:S(2)}) collective-permute-start(f32[3,128,128]{2,1,0:T(8,128)} %phase.1), channel_id=1, source_target_pairs={{0,4},{1,9},{2,6},{3,11},{12,8},{13,5},{14,10},{15,7},{4,0},{5,1},... | collective-permute-start | bytes 589832 | tf_op jit(solution)/shard_map/ppermute | solution.py:370
  8.0 5.8 %collective-permute-start = (f32[3,128,128]{2,1,0:T(8,128)}, f32[3,128,128]{2,1,0:T(8,128)S(1)}, u32[]{:S(2)}, u32[]{:S(2)}) collective-permute-start(f32[3,128,128]{2,1,0:T(8,128)} %phase.1), channel_id=1, source_target_pairs={{4,9},{6,11},{8,5},{10,7},{0,1},{1,0},{2,3},{3,2},{5,4},{7,6},{9,8... | collective-permute-start | bytes 589832 | tf_op jit(solution)/shard_map/ppermute | solution.py:370
  10.7 3.2 %collective-permute-start.5 = (f32[256,128]{1,0:T(8,128)S(1)}, f32[256,128]{1,0:T(8,128)S(1)}, u32[]{:S(2)}, u32[]{:S(2)}) collective-permute-start(f32[256,128]{1,0:T(8,128)S(1)} %get-tuple-element.29.refs_3_), channel_id=1, source_target_pairs={{0,1},{1,0},{2,3},{3,2},{4,5},{5,4},{6,7},{7,6},{8,9},{9,8},{10,11... | collective-permute-start | bytes 393224 | tf_op jit(solution)/shard_map/ppermute | solution.py:374
  13.9 1.5 %collective-permute-start.6 = (f32[192,256]{1,0:T(8,128)S(1)}, f32[192,256]{1,0:T(8,128)S(1)}, u32[]{:S(2)}, u32[]{:S(2)}) collective-permute-start(f32[192,256]{1,0:T(8,128)S(1)} %get-tuple-element.34.refs_2_), channel_id=1, source_target_pairs={{0,1},{1,0},{2,3},{3,2},{4,5},{5,4},{6,7},{7,6},{8,9},{9,8},{10,11... | collective-permute-start | bytes 589832 | tf_op jit(solution)/shard_map/ppermute | solution.py:374
  14.0 1.7 %collective-permute-start.7 = (f32[192,256]{1,0:T(8,128)S(1)}, f32[192,256]{1,0:T(8,128)S(1)}, u32[]{:S(2)}, u32[]{:S(2)}) collective-permute-start(f32[192,256]{1,0:T(8,128)S(1)} %get-tuple-element.38.refs_3_), channel_id=1, source_target_pairs={{0,1},{1,0},{2,3},{3,2},{4,5},{5,4},{6,7},{7,6},{8,9},{9,8},{10,11... | collective-permute-start | bytes 589832 | tf_op jit(solution)/shard_map/ppermute | solution.py:374
  15.7 1.4 %collective-permute-start.8 = (f32[264,128]{1,0:T(8,128)S(1)}, f32[264,128]{1,0:T(8,128)S(1)}, u32[]{:S(2)}, u32[]{:S(2)}) collective-permute-start(f32[264,128]{1,0:T(8,128)S(1)} %shard_map.74.refs_0_), channel_id=1, source_target_pairs={{0,1},{1,0},{2,3},{3,2},{4,5},{5,4},{6,7},{7,6},{8,9},{9,8},{10,11... | collective-permute-start | bytes 405512 | tf_op jit(solution)/shard_map/ppermute | solution.py:374
  17.0 10.0 %collective-permute-start.9 = (f32[40,256]{1,0:T(8,128)S(1)}, f32[40,256]{1,0:T(8,128)S(1)}, u32[]{:S(2)}, u32[]{:S(2)}) collective-permute-start(f32[40,256]{1,0:T(8,128)S(1)} %get-tuple-element.40), channel_id=1, source_target_pairs={{4,1},{5,0},{6,3},{7,2},{8,10},{9,11},{10,8},{11,9},{0,12},{1,13},... | collective-permute-start | bytes 122888 | tf_op jit(solution)/shard_map/ppermute | solution.py:370
  19.5 7.5 %collective-permute-start.10 = (f32[40,256]{1,0:T(8,128)S(1)}, f32[40,256]{1,0:T(8,128)S(1)}, u32[]{:S(2)}, u32[]{:S(2)}) collective-permute-start(f32[40,256]{1,0:T(8,128)S(1)} %get-tuple-element.41), channel_id=1, source_target_pairs={{8,13},{9,12},{10,15},{11,14},{12,9},{13,8},{14,11},{15,10},{0,1},... | collective-permute-start | bytes 122888 | tf_op jit(solution)/shard_map/ppermute | solution.py:370
  19.5 7.5 %collective-permute-start.11 = (f32[16,128]{1,0:T(8,128)S(1)}, f32[16,128]{1,0:T(8,128)S(1)}, u32[]{:S(2)}, u32[]{:S(2)}) collective-permute-start(f32[16,128]{1,0:T(8,128)S(1)} %get-tuple-element.42), channel_id=1, source_target_pairs={{4,3},{5,2},{6,1},{7,0},{0,5},{1,4},{2,7},{3,6},{8,9},{9,8},{10,11... | collective-permute-start | bytes 24584 | tf_op jit(solution)/shard_map/ppermute | solution.py:370
  24.4 2.6 %collective-permute-start.12 = (f32[16,128]{1,0:T(8,128)S(1)}, f32[16,128]{1,0:T(8,128)S(1)}, u32[]{:S(2)}, u32[]{:S(2)}) collective-permute-start(f32[16,128]{1,0:T(8,128)S(1)} %get-tuple-element.43), channel_id=1, source_target_pairs={{4,6},{5,7},{6,4},{7,5},{8,15},{9,14},{10,13},{11,12},{12,9},{13,8... | collective-permute-start | bytes 24584 | tf_op jit(solution)/shard_map/ppermute | solution.py:370

commit v8 on v7

--- a/solution.py
+++ b/solution.py
@@ -32,6 +32,10 @@
     return lax.dot_general(a, b, (((1,), (1,)), ((), ())), preferred_element_type=F32)
 
 
+def dot_tn(a, b):
+    return lax.dot_general(a, b, (((0,), (0,)), ((), ())), preferred_element_type=F32)
+
+
 def mm3(left, right, op=dot):
     (lh, ll), (rh, rl) = left, right
     return op(lh, rh) + (op(lh, rl) + op(ll, rh))
@@ -40,12 +44,12 @@
 def sincos(phase):
     h = 0.5 * phase
     u = h * h
-    s = 1.0 / 6227020800.0
-    for coef in (-1.0 / 39916800.0, 1.0 / 362880.0, -1.0 / 5040.0, 1.0 / 120.0, -1.0 / 6.0, 1.0):
+    s = 2.59043003e-06
+    for coef in (-1.98008653e-04, 8.33289922e-03, -1.66666476e-01, 9.99999977e-01):
         s = s * u + coef
     s = s * h
-    c = 1.0 / 479001600.0
-    for coef in (-1.0 / 3628800.0, 1.0 / 40320.0, -1.0 / 720.0, 1.0 / 24.0, -0.5, 1.0):
+    c = -2.60510764e-07
+    for coef in (2.47601355e-05, -1.38883608e-03, 4.16666362e-02, -4.99999994e-01, 1.0):
         c = c * u + coef
     two_s = s + s
     return two_s * c, 1.0 - two_s * s
@@ -115,23 +119,25 @@
 
 def spectrum_kernel(half, order, *refs):
     blocks = [refs[order.index(d)] for d in range(2 * half)]
-    fwd_h, fwd_l, adj_h, adj_l, spec, goal, meta, part = refs[2 * half :]
+    _, _, adj_h, adj_l, spec, goal, meta = refs[2 * half :]
     rows, pixels = goal.shape[1], goal.shape[2]
     freqs = spec.shape[1]
     src, row = lax.axis_index("src"), lax.axis_index("row")
     own = jnp.concatenate([b[:rows] for b in blocks], axis=0)
     waves = mm3(split(own), (adj_h[:pixels], adj_l[:pixels]))
-    part[...] = jnp.zeros_like(part)
+    tables = []
+    starts = []
     for d in range(2 * half):
         block = block_of(src, d // half, d % half, half)
-        start = pl.multiple_of((block * 2 + row) * rows, rows)
-        mine = waves[d * rows : (d + 1) * rows]
-        part[pl.ds(start, rows), :] = mine[:, :freqs]
-        part[pl.ds(pl.multiple_of(pixels + start, rows), rows), :] = mine[:, freqs:]
+        starts.append(pl.multiple_of((block * 2 + row) * rows, rows))
         goal[block] = blocks[d][rows : 2 * rows]
+    for table in (adj_h, adj_l):
+        tables.append(jnp.concatenate([table[pl.ds(n, rows), :] for n in starts], axis=0))
     for j in range(half):
         meta[j] = jnp.where(row == 0, blocks[j][2 * rows :], blocks[half + j][2 * rows :])
-    spec[...] = mm3((fwd_h[...], fwd_l[...]), split(part[...]))
+    both = mm3(tables, split(waves), dot_tn)
+    spec[:freqs] = both[:freqs, :freqs] - both[freqs:, freqs:]
+    spec[freqs:] = both[:freqs, freqs:] + both[freqs:, :freqs]
 
 
 def weight_of(meta, source, per_device):
@@ -436,7 +442,6 @@
     spec, goal, meta = call(
         functools.partial(spectrum_kernel, half, order),
         [(2 * freqs, freqs), (src_count, rows, pixels), (half, PAD, pixels)],
-        [pltpu.VMEM((2 * pixels, freqs), F32)],
         hub=True,
     )(*blocks, *tables)
     spec_other = swap_rows(spec)

time: 28 us -> 28 us (level)
  no operation moved by 1% of the time
where the time goes in v8:
time: 28 us; the launch traced here: 27.7 us
  starting transfers between devices  15 us (54%)
  waiting for transfers between devices  9.51 us (34%)
  Pallas kernels  2.58 us (9%)
  between operations  0.69 us (2%)
    ppermute x9, starting transfers between devices, permute(): lax.ppermute(x, ('src', 'tile', 'row'), [(flat[a], flat[b]) for a, b in p...  14.2 us
    ppermute x9, waiting for transfers between devices, permute(): lax.ppermute(x, ('src', 'tile', 'row'), [(flat[a], flat[b]) for a, b in p...  7.17 us
    ppermute x4, waiting for transfers between devices, swap_rows(): return lax.ppermute(x, 'row', [(0, 1), (1, 0)])  2.34 us
    pallas_call x1, Pallas kernels, hub_shards(): call(tables_kernel, [(2 * freqs, 2 * pixels)] * 2 + [(2 * pixels, 2 * fre...  0.97 us
    pallas_call x1, Pallas kernels, hub_shards(): call(fetch_kernel, [(2 * rows + PAD, pixels)], [pltpu.VMEM((per_device, 2...  0.82 us
    pallas_call x1, Pallas kernels, hub_shards(): call(functools.partial(place_kernel, half, 1.0 / (sources * pixels * tile...  0.77 us
    ppermute x4, starting transfers between devices, swap_rows(): return lax.ppermute(x, 'row', [(0, 1), (1, 0)])  0.77 us
  transfers between devices with their start and end apart: 13, of which 6 were waited for; matrix products, arithmetic and copies ran while one was open for 0% of the time, Pallas kernels for 4%

profile of v8, /device:TPU:0, one launch (start us, length us, event | category | flops | bytes accessed | tf_op | source)
XLA Modules:
  0.0 27.7 jit_solution(7949327673609638940)
XLA Ops:
  0.6 0.8 %shard_map.69.refs_0_ = f32[72,256]{1,0:T(8,128)S(1)} custom-call(f32[1,32,256]{2,1,0:T(8,128)} %mask.1, f32[1,32,256]{2,1,0:T(8,128)} %goal.1, s32[3,2,128]{2,1,0:T(2,128)} %bitcast.3, f32[1,3]{1,0:T(1,128)} %bitcast.4), custom_call_target="tpu_custom_call" | custom-call | tf_op jit(solution)/shard_map/pallas_call | solution.py:416
  1.5 4.1 %collective-permute-start.4 = (f32[72,256]{1,0:T(8,128)S(1)}, f32[72,256]{1,0:T(8,128)S(1)}, u32[]{:S(2)}, u32[]{:S(2)}) collective-permute-start(f32[72,256]{1,0:T(8,128)S(1)} %shard_map.69.refs_0_), channel_id=1, source_target_pairs={{0,8},{1,9},{2,10},{3,11},{12,4},{13,5},{14,6},{15,7},{4,0},{5,1},... | collective-permute-start | bytes 221192 | tf_op jit(solution)/shard_map/ppermute | solution.py:376
  5.5 0.0 collective-permute-start.3
  5.5 0.0 collective-permute-start.2
  5.6 2.5 %collective-permute-start.1 = (f32[3,128,128]{2,1,0:T(8,128)}, f32[3,128,128]{2,1,0:T(8,128)S(1)}, u32[]{:S(2)}, u32[]{:S(2)}) collective-permute-start(f32[3,128,128]{2,1,0:T(8,128)} %phase.1), channel_id=1, source_target_pairs={{0,4},{1,9},{2,6},{3,11},{12,8},{13,5},{14,10},{15,7},{4,0},{5,1},... | collective-permute-start | bytes 589832 | tf_op jit(solution)/shard_map/ppermute | solution.py:376
  8.0 0.0 collective-permute-start
  8.0 1.0 %shard_map.68 = (bf16[256,512]{1,0:T(8,128)(2,1)S(1)}, bf16[256,512]{1,0:T(8,128)(2,1)S(1)}, bf16[512,256]{1,0:T(8,128)(2,1)S(1)}, bf16[512,256]{1,0:T(8,128)(2,1)S(1)}, f32[3,128,128]{2,1,0:T(8,128)S(1)}) custom-call(f32[3,128,128]{2,1,0:T(8,128)} %phase.1), custom_call_target="tpu_custom_call" | custom-call | tf_op jit(solution)/shard_map/pallas_call | solution.py:434
  9.0 0.0 collective-permute-done.4.refs_3_
  9.0 1.7 %collective-permute-done.3.refs_2_ = f32[72,256]{1,0:T(8,128)S(1)} collective-permute-done((f32[72,256]{1,0:T(8,128)S(1)}, f32[72,256]{1,0:T(8,128)S(1)}, u32[]{:S(2)}, u32[]{:S(2)}) %collective-permute-start.3) | collective-permute-done | bytes 73760 | tf_op jit(solution)/shard_map/ppermute | solution.py:376
  10.7 0.0 collective-permute-done.2.refs_1_
  10.7 0.0 collective-permute-start.5
  10.7 3.2 %collective-permute-done.1.refs_2_ = f32[3,128,128]{2,1,0:T(8,128)S(1)} collective-permute-done((f32[3,128,128]{2,1,0:T(8,128)}, f32[3,128,128]{2,1,0:T(8,128)S(1)}, u32[]{:S(2)}, u32[]{:S(2)}) %collective-permute-start.1) | collective-permute-done | bytes 196640 | tf_op jit(solution)/shard_map/ppermute | solution.py:376
  13.9 0.0 collective-permute-done.refs_1_
  13.9 0.0 collective-permute-done.5.refs_4_
  13.9 0.1 collective-permute-start.6
  14.0 0.5 %collective-permute-start.7 = (f32[192,256]{1,0:T(8,128)S(1)}, f32[192,256]{1,0:T(8,128)S(1)}, u32[]{:S(2)}, u32[]{:S(2)}) collective-permute-start(f32[192,256]{1,0:T(8,128)S(1)} %get-tuple-element.38.refs_3_), channel_id=1, source_target_pairs={{0,1},{1,0},{2,3},{3,2},{4,5},{5,4},{6,7},{7,6},{8,9},{9,8},{10,11... | collective-permute-start | bytes 589832 | tf_op jit(solution)/shard_map/ppermute | solution.py:380
  14.4 0.9 %collective-permute-done.6.refs_3_ = f32[192,256]{1,0:T(8,128)S(1)} collective-permute-done((f32[192,256]{1,0:T(8,128)S(1)}, f32[192,256]{1,0:T(8,128)S(1)}, u32[]{:S(2)}, u32[]{:S(2)}) %collective-permute-start.6) | collective-permute-done | bytes 196640 | tf_op jit(solution)/shard_map/ppermute | solution.py:380
  15.4 0.3 %collective-permute-done.7.refs_4_ = f32[192,256]{1,0:T(8,128)S(1)} collective-permute-done((f32[192,256]{1,0:T(8,128)S(1)}, f32[192,256]{1,0:T(8,128)S(1)}, u32[]{:S(2)}, u32[]{:S(2)}) %collective-permute-start.7) | collective-permute-done | bytes 196640 | tf_op jit(solution)/shard_map/ppermute | solution.py:380
  15.7 0.2 collective-permute-start.8
  15.9 1.1 %collective-permute-done.8.refs_1_ = f32[264,128]{1,0:T(8,128)S(1)} collective-permute-done((f32[264,128]{1,0:T(8,128)S(1)}, f32[264,128]{1,0:T(8,128)S(1)}, u32[]{:S(2)}, u32[]{:S(2)}) %collective-permute-start.8) | collective-permute-done | bytes 135200 | tf_op jit(solution)/shard_map/ppermute | solution.py:380
  17.0 2.5 %collective-permute-start.9 = (f32[40,256]{1,0:T(8,128)S(1)}, f32[40,256]{1,0:T(8,128)S(1)}, u32[]{:S(2)}, u32[]{:S(2)}) collective-permute-start(f32[40,256]{1,0:T(8,128)S(1)} %get-tuple-element.40), channel_id=1, source_target_pairs={{4,1},{5,0},{6,3},{7,2},{8,10},{9,11},{10,8},{11,9},{0,12},{1,13},... | collective-permute-start | bytes 122888 | tf_op jit(solution)/shard_map/ppermute | solution.py:376
  19.5 0.0 collective-permute-start.10
  19.5 4.8 %collective-permute-start.11 = (f32[16,128]{1,0:T(8,128)S(1)}, f32[16,128]{1,0:T(8,128)S(1)}, u32[]{:S(2)}, u32[]{:S(2)}) collective-permute-start(f32[16,128]{1,0:T(8,128)S(1)} %get-tuple-element.42), channel_id=1, source_target_pairs={{4,3},{5,2},{6,1},{7,0},{0,5},{1,4},{2,7},{3,6},{8,9},{9,8},{10,11... | collective-permute-start | bytes 24584 | tf_op jit(solution)/shard_map/ppermute | solution.py:376
  24.3 0.4 %collective-permute-start.12 = (f32[16,128]{1,0:T(8,128)S(1)}, f32[16,128]{1,0:T(8,128)S(1)}, u32[]{:S(2)}, u32[]{:S(2)}) collective-permute-start(f32[16,128]{1,0:T(8,128)S(1)} %get-tuple-element.43), channel_id=1, source_target_pairs={{4,6},{5,7},{6,4},{7,5},{8,15},{9,14},{10,13},{11,12},{12,9},{13,8... | collective-permute-start | bytes 24584 | tf_op jit(solution)/shard_map/ppermute | solution.py:376
  24.7 2.3 %collective-permute-done.11.got_c = f32[16,128]{1,0:T(8,128)S(1)} collective-permute-done((f32[16,128]{1,0:T(8,128)S(1)}, f32[16,128]{1,0:T(8,128)S(1)}, u32[]{:S(2)}, u32[]{:S(2)}) %collective-permute-start.11) | collective-permute-done | bytes 8224 | tf_op jit(solution)/shard_map/ppermute | solution.py:376
  27.0 0.0 collective-permute-done.12.got_d
  27.0 0.0 collective-permute-done.9.got_a
  27.0 0.0 collective-permute-done.10.got_b
  27.0 0.8 %shard_map.76 = (f32[1,32,256]{2,1,0:T(8,128)}, f32[1,3]{1,0:T(1,128)}) custom-call(f32[40,256]{1,0:T(8,128)S(1)} %get-tuple-element.39.own, f32[40,256]{1,0:T(8,128)S(1)} %collective-permute-done.9.got_a, f32[40,256]{1,0:T(8,128)S(1)} %collective-permute-done.10.got_b, f32[16,128]{1,0:T(8,128)S(1)} %collective-permute-done.11.got_c, ...), custom_call_target="tpu_custom_call" | custom-call | tf_op jit(solution)/shard_map/pallas_call | solution.py:507
  (6 shorter events, 0.0 us)
Async XLA Ops:
  1.5 7.5 %collective-permute-start.4 = (f32[72,256]{1,0:T(8,128)S(1)}, f32[72,256]{1,0:T(8,128)S(1)}, u32[]{:S(2)}, u32[]{:S(2)}) collective-permute-start(f32[72,256]{1,0:T(8,128)S(1)} %shard_map.69.refs_0_), channel_id=1, source_target_pairs={{0,8},{1,9},{2,10},{3,11},{12,4},{13,5},{14,6},{15,7},{4,0},{5,1},... | collective-permute-start | bytes 221192 | tf_op jit(solution)/shard_map/ppermute | solution.py:376
  5.5 5.1 %collective-permute-start.3 = (f32[72,256]{1,0:T(8,128)S(1)}, f32[72,256]{1,0:T(8,128)S(1)}, u32[]{:S(2)}, u32[]{:S(2)}) collective-permute-start(f32[72,256]{1,0:T(8,128)S(1)} %shard_map.69.refs_0_), channel_id=1, source_target_pairs={{0,4},{1,5},{2,6},{3,7},{12,8},{13,9},{14,10},{15,11},{4,0},{5,1},... | collective-permute-start | bytes 221192 | tf_op jit(solution)/shard_map/ppermute | solution.py:376
  5.5 5.1 %collective-permute-start.2 = (f32[72,256]{1,0:T(8,128)S(1)}, f32[72,256]{1,0:T(8,128)S(1)}, u32[]{:S(2)}, u32[]{:S(2)}) collective-permute-start(f32[72,256]{1,0:T(8,128)S(1)} %shard_map.69.refs_0_), channel_id=1, source_target_pairs={{4,8},{5,9},{6,10},{7,11},{8,4},{9,5},{10,6},{11,7},{0,1},{1,0},{2... | collective-permute-start | bytes 221192 | tf_op jit(solution)/shard_map/ppermute | solution.py:376
  5.6 8.3 %collective-permute-start.1 = (f32[3,128,128]{2,1,0:T(8,128)}, f32[3,128,128]{2,1,0:T(8,128)S(1)}, u32[]{:S(2)}, u32[]{:S(2)}) collective-permute-start(f32[3,128,128]{2,1,0:T(8,128)} %phase.1), channel_id=1, source_target_pairs={{0,4},{1,9},{2,6},{3,11},{12,8},{13,5},{14,10},{15,7},{4,0},{5,1},... | collective-permute-start | bytes 589832 | tf_op jit(solution)/shard_map/ppermute | solution.py:376
  8.0 5.8 %collective-permute-start = (f32[3,128,128]{2,1,0:T(8,128)}, f32[3,128,128]{2,1,0:T(8,128)S(1)}, u32[]{:S(2)}, u32[]{:S(2)}) collective-permute-start(f32[3,128,128]{2,1,0:T(8,128)} %phase.1), channel_id=1, source_target_pairs={{4,9},{6,11},{8,5},{10,7},{0,1},{1,0},{2,3},{3,2},{5,4},{7,6},{9,8... | collective-permute-start | bytes 589832 | tf_op jit(solution)/shard_map/ppermute | solution.py:376
  10.7 3.2 %collective-permute-start.5 = (f32[256,128]{1,0:T(8,128)S(1)}, f32[256,128]{1,0:T(8,128)S(1)}, u32[]{:S(2)}, u32[]{:S(2)}) collective-permute-start(f32[256,128]{1,0:T(8,128)S(1)} %get-tuple-element.29.refs_3_), channel_id=1, source_target_pairs={{0,1},{1,0},{2,3},{3,2},{4,5},{5,4},{6,7},{7,6},{8,9},{9,8},{10,11... | collective-permute-start | bytes 393224 | tf_op jit(solution)/shard_map/ppermute | solution.py:380
  13.9 1.5 %collective-permute-start.6 = (f32[192,256]{1,0:T(8,128)S(1)}, f32[192,256]{1,0:T(8,128)S(1)}, u32[]{:S(2)}, u32[]{:S(2)}) collective-permute-start(f32[192,256]{1,0:T(8,128)S(1)} %get-tuple-element.34.refs_2_), channel_id=1, source_target_pairs={{0,1},{1,0},{2,3},{3,2},{4,5},{5,4},{6,7},{7,6},{8,9},{9,8},{10,11... | collective-permute-start | bytes 589832 | tf_op jit(solution)/shard_map/ppermute | solution.py:380
  14.0 1.7 %collective-permute-start.7 = (f32[192,256]{1,0:T(8,128)S(1)}, f32[192,256]{1,0:T(8,128)S(1)}, u32[]{:S(2)}, u32[]{:S(2)}) collective-permute-start(f32[192,256]{1,0:T(8,128)S(1)} %get-tuple-element.38.refs_3_), channel_id=1, source_target_pairs={{0,1},{1,0},{2,3},{3,2},{4,5},{5,4},{6,7},{7,6},{8,9},{9,8},{10,11... | collective-permute-start | bytes 589832 | tf_op jit(solution)/shard_map/ppermute | solution.py:380
  15.7 1.4 %collective-permute-start.8 = (f32[264,128]{1,0:T(8,128)S(1)}, f32[264,128]{1,0:T(8,128)S(1)}, u32[]{:S(2)}, u32[]{:S(2)}) collective-permute-start(f32[264,128]{1,0:T(8,128)S(1)} %shard_map.74.refs_0_), channel_id=1, source_target_pairs={{0,1},{1,0},{2,3},{3,2},{4,5},{5,4},{6,7},{7,6},{8,9},{9,8},{10,11... | collective-permute-start | bytes 405512 | tf_op jit(solution)/shard_map/ppermute | solution.py:380
  17.0 10.0 %collective-permute-start.9 = (f32[40,256]{1,0:T(8,128)S(1)}, f32[40,256]{1,0:T(8,128)S(1)}, u32[]{:S(2)}, u32[]{:S(2)}) collective-permute-start(f32[40,256]{1,0:T(8,128)S(1)} %get-tuple-element.40), channel_id=1, source_target_pairs={{4,1},{5,0},{6,3},{7,2},{8,10},{9,11},{10,8},{11,9},{0,12},{1,13},... | collective-permute-start | bytes 122888 | tf_op jit(solution)/shard_map/ppermute | solution.py:376
  19.5 7.5 %collective-permute-start.10 = (f32[40,256]{1,0:T(8,128)S(1)}, f32[40,256]{1,0:T(8,128)S(1)}, u32[]{:S(2)}, u32[]{:S(2)}) collective-permute-start(f32[40,256]{1,0:T(8,128)S(1)} %get-tuple-element.41), channel_id=1, source_target_pairs={{8,13},{9,12},{10,15},{11,14},{12,9},{13,8},{14,11},{15,10},{0,1},... | collective-permute-start | bytes 122888 | tf_op jit(solution)/shard_map/ppermute | solution.py:376
  19.5 7.5 %collective-permute-start.11 = (f32[16,128]{1,0:T(8,128)S(1)}, f32[16,128]{1,0:T(8,128)S(1)}, u32[]{:S(2)}, u32[]{:S(2)}) collective-permute-start(f32[16,128]{1,0:T(8,128)S(1)} %get-tuple-element.42), channel_id=1, source_target_pairs={{4,3},{5,2},{6,1},{7,0},{0,5},{1,4},{2,7},{3,6},{8,9},{9,8},{10,11... | collective-permute-start | bytes 24584 | tf_op jit(solution)/shard_map/ppermute | solution.py:376
  24.3 2.7 %collective-permute-start.12 = (f32[16,128]{1,0:T(8,128)S(1)}, f32[16,128]{1,0:T(8,128)S(1)}, u32[]{:S(2)}, u32[]{:S(2)}) collective-permute-start(f32[16,128]{1,0:T(8,128)S(1)} %get-tuple-element.43), channel_id=1, source_target_pairs={{4,6},{5,7},{6,4},{7,5},{8,15},{9,14},{10,13},{11,12},{12,9},{13,8... | collective-permute-start | bytes 24584 | tf_op jit(solution)/shard_map/ppermute | solution.py:376

commit v9 on v8

--- a/solution.py
+++ b/solution.py
@@ -229,13 +229,12 @@
     line = lax.broadcasted_iota(jnp.int32, (PAD, freqs), 0)
     lane = lax.broadcasted_iota(jnp.int32, (PAD, freqs), 1)
     terms = jnp.zeros((PAD, freqs), F32)
+    powers = []
     for s in range(count):
         value = field[s]
         back_r, back_i = cot * value[:, :pixels], cot * value[:, pixels:]
         power = back_r * value[:, :pixels] + back_i * value[:, pixels:]
-        power = jnp.sum(jnp.sum(power, axis=0, keepdims=True), axis=1, keepdims=True)
-        j, i = divmod(s, per_device)
-        terms = terms + jnp.where((lane == i) & (line == j), power, 0.0)
+        powers.append(jnp.sum(power, axis=0, keepdims=True))
         back = jnp.concatenate([back_r, back_i], axis=1)
         half = mm3(split(back), (adj_h[...], adj_l[...]))
         lanes = slice(s * freqs, (s + 1) * freqs)
@@ -243,6 +242,10 @@
             high, low = split(half[:, n * freqs : (n + 1) * freqs])
             back_h[n * rows : (n + 1) * rows, lanes] = high
             back_l[n * rows : (n + 1) * rows, lanes] = low
+    powers = jnp.sum(jnp.concatenate(powers, axis=0), axis=1, keepdims=True)
+    for s in range(count):
+        j, i = divmod(s, per_device)
+        terms = terms + jnp.where((lane == i) & (line == j), powers[s : s + 1], 0.0)
     grad_r = jnp.zeros((freqs, freqs), F32)
     grad_i = jnp.zeros((freqs, freqs), F32)
     here, there = (slice(n, n + rows) for n in (first_row, pixels + first_row))
@@ -321,23 +324,23 @@
     src, tile = lax.axis_index("src"), lax.axis_index("tile")
     low, hub = src < half, (src == half - 1) | (src == half)
 
-    def pick(low_hub, low_end, high_hub, high_end, *index):
-        at_hub = jnp.where(low, low_hub[index], high_hub[index])
-        at_end = jnp.where(low, low_end[index], high_end[index])
-        return jnp.where(hub, at_hub, at_end)
-
-    bodies, strips = (own, got_a, own, got_b), (got_d, got_c, got_a, got_d)
-    body = pick(*bodies, slice(0, rows), slice(None))
-    strip = pick(*strips, slice(0, PAD), slice(0, rows // PAD * OV))
-    places = range(0, rows // PAD * OV, OV)
-    strip = jnp.concatenate([strip[:, i : i + OV] for i in places], axis=0)
-    zero = jnp.zeros_like(strip)
-    middle = jnp.zeros((rows, pixels - 2 * OV), F32)
-    left, right = jnp.where(tile == 1, strip, zero), jnp.where(tile == 0, strip, zero)
-    out[0] = body + jnp.concatenate([left, middle, right], axis=1)
-    own_terms = pick(*bodies, slice(rows, rows + 1), slice(0, per_device))
-    other_terms = pick(*strips, slice(PAD, PAD + 1), slice(0, per_device))
-    source[...] = (own_terms + other_terms) * term_scale
+    def place(at, rows_from, strips_from):
+        @pl.when(at)
+        def _():
+            strip = strips_from[:PAD, : rows // PAD * OV]
+            places = range(0, rows // PAD * OV, OV)
+            strip = jnp.concatenate([strip[:, i : i + OV] for i in places], axis=0)
+            zero = jnp.zeros_like(strip)
+            middle = jnp.zeros((rows, pixels - 2 * OV), F32)
+            left, right = jnp.where(tile == 1, strip, zero), jnp.where(tile == 0, strip, zero)
+            out[0] = rows_from[:rows] + jnp.concatenate([left, middle, right], axis=1)
+            own_terms = rows_from[rows : rows + 1, :per_device]
+            source[...] = (own_terms + strips_from[PAD : PAD + 1, :per_device]) * term_scale
+
+    place(low & hub, own, got_d)
+    place(low & ~hub, got_a, got_c)
+    place(~low & hub, own, got_a)
+    place(~(low | hub), got_b, got_d)
 
 
 def call(kernel, outs, scratch=(), kind=F32, hbm=0, hub=False):

time: 28 us -> 28 us (level)
  no operation moved by 1% of the time
where the time goes in v9:
time: 28 us; the launch traced here: 27.8 us
  starting transfers between devices  15 us (54%)
  waiting for transfers between devices  9.52 us (34%)
  Pallas kernels  2.58 us (9%)
  between operations  0.69 us (2%)
    ppermute x9, starting transfers between devices, permute(): lax.ppermute(x, ('src', 'tile', 'row'), [(flat[a], flat[b]) for a, b in p...  14.2 us
    ppermute x9, waiting for transfers between devices, permute(): lax.ppermute(x, ('src', 'tile', 'row'), [(flat[a], flat[b]) for a, b in p...  7.18 us
    ppermute x4, waiting for transfers between devices, swap_rows(): return lax.ppermute(x, 'row', [(0, 1), (1, 0)])  2.34 us
    pallas_call x1, Pallas kernels, hub_shards(): call(tables_kernel, [(2 * freqs, 2 * pixels)] * 2 + [(2 * pixels, 2 * fre...  0.97 us
    pallas_call x1, Pallas kernels, hub_shards(): call(fetch_kernel, [(2 * rows + PAD, pixels)], [pltpu.VMEM((per_device, 2...  0.82 us
    pallas_call x1, Pallas kernels, hub_shards(): call(functools.partial(place_kernel, half, 1.0 / (sources * pixels * tile...  0.78 us
    ppermute x4, starting transfers between devices, swap_rows(): return lax.ppermute(x, 'row', [(0, 1), (1, 0)])  0.77 us
  transfers between devices with their start and end apart: 13, of which 6 were waited for; matrix products, arithmetic and copies ran while one was open for 0% of the time, Pallas kernels for 4%

profile of v9, /device:TPU:0, one launch (start us, length us, event | category | flops | bytes accessed | tf_op | source)
XLA Modules:
  0.0 27.8 jit_solution(6453804096445691318)
XLA Ops:
  0.6 0.8 %shard_map.69.refs_0_ = f32[72,256]{1,0:T(8,128)S(1)} custom-call(f32[1,32,256]{2,1,0:T(8,128)} %mask.1, f32[1,32,256]{2,1,0:T(8,128)} %goal.1, s32[3,2,128]{2,1,0:T(2,128)} %bitcast.3, f32[1,3]{1,0:T(1,128)} %bitcast.4), custom_call_target="tpu_custom_call" | custom-call | tf_op jit(solution)/shard_map/pallas_call | solution.py:419
  1.5 4.1 %collective-permute-start.4 = (f32[72,256]{1,0:T(8,128)S(1)}, f32[72,256]{1,0:T(8,128)S(1)}, u32[]{:S(2)}, u32[]{:S(2)}) collective-permute-start(f32[72,256]{1,0:T(8,128)S(1)} %shard_map.69.refs_0_), channel_id=1, source_target_pairs={{0,8},{1,9},{2,10},{3,11},{12,4},{13,5},{14,6},{15,7},{4,0},{5,1},... | collective-permute-start | bytes 221192 | tf_op jit(solution)/shard_map/ppermute | solution.py:379
  5.5 0.0 collective-permute-start.3
  5.5 0.0 collective-permute-start.2
  5.6 2.5 %collective-permute-start.1 = (f32[3,128,128]{2,1,0:T(8,128)}, f32[3,128,128]{2,1,0:T(8,128)S(1)}, u32[]{:S(2)}, u32[]{:S(2)}) collective-permute-start(f32[3,128,128]{2,1,0:T(8,128)} %phase.1), channel_id=1, source_target_pairs={{0,4},{1,9},{2,6},{3,11},{12,8},{13,5},{14,10},{15,7},{4,0},{5,1},... | collective-permute-start | bytes 589832 | tf_op jit(solution)/shard_map/ppermute | solution.py:379
  8.0 0.0 collective-permute-start
  8.0 1.0 %shard_map.68 = (bf16[256,512]{1,0:T(8,128)(2,1)S(1)}, bf16[256,512]{1,0:T(8,128)(2,1)S(1)}, bf16[512,256]{1,0:T(8,128)(2,1)S(1)}, bf16[512,256]{1,0:T(8,128)(2,1)S(1)}, f32[3,128,128]{2,1,0:T(8,128)S(1)}) custom-call(f32[3,128,128]{2,1,0:T(8,128)} %phase.1), custom_call_target="tpu_custom_call" | custom-call | tf_op jit(solution)/shard_map/pallas_call | solution.py:437
  9.0 0.0 collective-permute-done.4.refs_3_
  9.0 1.7 %collective-permute-done.3.refs_2_ = f32[72,256]{1,0:T(8,128)S(1)} collective-permute-done((f32[72,256]{1,0:T(8,128)S(1)}, f32[72,256]{1,0:T(8,128)S(1)}, u32[]{:S(2)}, u32[]{:S(2)}) %collective-permute-start.3) | collective-permute-done | bytes 73760 | tf_op jit(solution)/shard_map/ppermute | solution.py:379
  10.7 0.0 collective-permute-done.2.refs_1_
  10.7 0.0 collective-permute-start.5
  10.7 3.2 %collective-permute-done.1.refs_2_ = f32[3,128,128]{2,1,0:T(8,128)S(1)} collective-permute-done((f32[3,128,128]{2,1,0:T(8,128)}, f32[3,128,128]{2,1,0:T(8,128)S(1)}, u32[]{:S(2)}, u32[]{:S(2)}) %collective-permute-start.1) | collective-permute-done | bytes 196640 | tf_op jit(solution)/shard_map/ppermute | solution.py:379
  13.9 0.0 collective-permute-done.refs_1_
  13.9 0.0 collective-permute-done.5.refs_4_
  13.9 0.1 collective-permute-start.6
  14.0 0.5 %collective-permute-start.7 = (f32[192,256]{1,0:T(8,128)S(1)}, f32[192,256]{1,0:T(8,128)S(1)}, u32[]{:S(2)}, u32[]{:S(2)}) collective-permute-start(f32[192,256]{1,0:T(8,128)S(1)} %get-tuple-element.38.refs_3_), channel_id=1, source_target_pairs={{0,1},{1,0},{2,3},{3,2},{4,5},{5,4},{6,7},{7,6},{8,9},{9,8},{10,11... | collective-permute-start | bytes 589832 | tf_op jit(solution)/shard_map/ppermute | solution.py:383
  14.4 0.9 %collective-permute-done.6.refs_3_ = f32[192,256]{1,0:T(8,128)S(1)} collective-permute-done((f32[192,256]{1,0:T(8,128)S(1)}, f32[192,256]{1,0:T(8,128)S(1)}, u32[]{:S(2)}, u32[]{:S(2)}) %collective-permute-start.6) | collective-permute-done | bytes 196640 | tf_op jit(solution)/shard_map/ppermute | solution.py:383
  15.4 0.3 %collective-permute-done.7.refs_4_ = f32[192,256]{1,0:T(8,128)S(1)} collective-permute-done((f32[192,256]{1,0:T(8,128)S(1)}, f32[192,256]{1,0:T(8,128)S(1)}, u32[]{:S(2)}, u32[]{:S(2)}) %collective-permute-start.7) | collective-permute-done | bytes 196640 | tf_op jit(solution)/shard_map/ppermute | solution.py:383
  15.7 0.2 collective-permute-start.8
  15.9 1.1 %collective-permute-done.8.refs_1_ = f32[264,128]{1,0:T(8,128)S(1)} collective-permute-done((f32[264,128]{1,0:T(8,128)S(1)}, f32[264,128]{1,0:T(8,128)S(1)}, u32[]{:S(2)}, u32[]{:S(2)}) %collective-permute-start.8) | collective-permute-done | bytes 135200 | tf_op jit(solution)/shard_map/ppermute | solution.py:383
  17.0 2.5 %collective-permute-start.9 = (f32[40,256]{1,0:T(8,128)S(1)}, f32[40,256]{1,0:T(8,128)S(1)}, u32[]{:S(2)}, u32[]{:S(2)}) collective-permute-start(f32[40,256]{1,0:T(8,128)S(1)} %get-tuple-element.40), channel_id=1, source_target_pairs={{4,1},{5,0},{6,3},{7,2},{8,10},{9,11},{10,8},{11,9},{0,12},{1,13},... | collective-permute-start | bytes 122888 | tf_op jit(solution)/shard_map/ppermute | solution.py:379
  19.5 0.0 collective-permute-start.10
  19.5 4.8 %collective-permute-start.11 = (f32[16,128]{1,0:T(8,128)S(1)}, f32[16,128]{1,0:T(8,128)S(1)}, u32[]{:S(2)}, u32[]{:S(2)}) collective-permute-start(f32[16,128]{1,0:T(8,128)S(1)} %get-tuple-element.42), channel_id=1, source_target_pairs={{4,3},{5,2},{6,1},{7,0},{0,5},{1,4},{2,7},{3,6},{8,9},{9,8},{10,11... | collective-permute-start | bytes 24584 | tf_op jit(solution)/shard_map/ppermute | solution.py:379
  24.3 0.4 %collective-permute-start.12 = (f32[16,128]{1,0:T(8,128)S(1)}, f32[16,128]{1,0:T(8,128)S(1)}, u32[]{:S(2)}, u32[]{:S(2)}) collective-permute-start(f32[16,128]{1,0:T(8,128)S(1)} %get-tuple-element.43), channel_id=1, source_target_pairs={{4,6},{5,7},{6,4},{7,5},{8,15},{9,14},{10,13},{11,12},{12,9},{13,8... | collective-permute-start | bytes 24584 | tf_op jit(solution)/shard_map/ppermute | solution.py:379
  24.7 2.3 %collective-permute-done.11.got_c = f32[16,128]{1,0:T(8,128)S(1)} collective-permute-done((f32[16,128]{1,0:T(8,128)S(1)}, f32[16,128]{1,0:T(8,128)S(1)}, u32[]{:S(2)}, u32[]{:S(2)}) %collective-permute-start.11) | collective-permute-done | bytes 8224 | tf_op jit(solution)/shard_map/ppermute | solution.py:379
  27.0 0.0 collective-permute-done.12.got_d
  27.0 0.0 collective-permute-done.9.got_a
  27.0 0.0 collective-permute-done.10.got_b
  27.0 0.8 %shard_map.76 = (f32[1,32,256]{2,1,0:T(8,128)}, f32[1,3]{1,0:T(1,128)}) custom-call(f32[40,256]{1,0:T(8,128)S(1)} %get-tuple-element.39.own, f32[40,256]{1,0:T(8,128)S(1)} %collective-permute-done.9.got_a, f32[40,256]{1,0:T(8,128)S(1)} %collective-permute-done.10.got_b, f32[16,128]{1,0:T(8,128)S(1)} %collective-permute-done.11.got_c, ...), custom_call_target="tpu_custom_call" | custom-call | tf_op jit(solution)/shard_map/pallas_call | solution.py:510
  (6 shorter events, 0.0 us)
Async XLA Ops:
  1.5 7.5 %collective-permute-start.4 = (f32[72,256]{1,0:T(8,128)S(1)}, f32[72,256]{1,0:T(8,128)S(1)}, u32[]{:S(2)}, u32[]{:S(2)}) collective-permute-start(f32[72,256]{1,0:T(8,128)S(1)} %shard_map.69.refs_0_), channel_id=1, source_target_pairs={{0,8},{1,9},{2,10},{3,11},{12,4},{13,5},{14,6},{15,7},{4,0},{5,1},... | collective-permute-start | bytes 221192 | tf_op jit(solution)/shard_map/ppermute | solution.py:379
  5.5 5.1 %collective-permute-start.3 = (f32[72,256]{1,0:T(8,128)S(1)}, f32[72,256]{1,0:T(8,128)S(1)}, u32[]{:S(2)}, u32[]{:S(2)}) collective-permute-start(f32[72,256]{1,0:T(8,128)S(1)} %shard_map.69.refs_0_), channel_id=1, source_target_pairs={{0,4},{1,5},{2,6},{3,7},{12,8},{13,9},{14,10},{15,11},{4,0},{5,1},... | collective-permute-start | bytes 221192 | tf_op jit(solution)/shard_map/ppermute | solution.py:379
  5.5 5.1 %collective-permute-start.2 = (f32[72,256]{1,0:T(8,128)S(1)}, f32[72,256]{1,0:T(8,128)S(1)}, u32[]{:S(2)}, u32[]{:S(2)}) collective-permute-start(f32[72,256]{1,0:T(8,128)S(1)} %shard_map.69.refs_0_), channel_id=1, source_target_pairs={{4,8},{5,9},{6,10},{7,11},{8,4},{9,5},{10,6},{11,7},{0,1},{1,0},{2... | collective-permute-start | bytes 221192 | tf_op jit(solution)/shard_map/ppermute | solution.py:379
  5.6 8.3 %collective-permute-start.1 = (f32[3,128,128]{2,1,0:T(8,128)}, f32[3,128,128]{2,1,0:T(8,128)S(1)}, u32[]{:S(2)}, u32[]{:S(2)}) collective-permute-start(f32[3,128,128]{2,1,0:T(8,128)} %phase.1), channel_id=1, source_target_pairs={{0,4},{1,9},{2,6},{3,11},{12,8},{13,5},{14,10},{15,7},{4,0},{5,1},... | collective-permute-start | bytes 589832 | tf_op jit(solution)/shard_map/ppermute | solution.py:379
  8.0 5.8 %collective-permute-start = (f32[3,128,128]{2,1,0:T(8,128)}, f32[3,128,128]{2,1,0:T(8,128)S(1)}, u32[]{:S(2)}, u32[]{:S(2)}) collective-permute-start(f32[3,128,128]{2,1,0:T(8,128)} %phase.1), channel_id=1, source_target_pairs={{4,9},{6,11},{8,5},{10,7},{0,1},{1,0},{2,3},{3,2},{5,4},{7,6},{9,8... | collective-permute-start | bytes 589832 | tf_op jit(solution)/shard_map/ppermute | solution.py:379
  10.7 3.2 %collective-permute-start.5 = (f32[256,128]{1,0:T(8,128)S(1)}, f32[256,128]{1,0:T(8,128)S(1)}, u32[]{:S(2)}, u32[]{:S(2)}) collective-permute-start(f32[256,128]{1,0:T(8,128)S(1)} %get-tuple-element.29.refs_3_), channel_id=1, source_target_pairs={{0,1},{1,0},{2,3},{3,2},{4,5},{5,4},{6,7},{7,6},{8,9},{9,8},{10,11... | collective-permute-start | bytes 393224 | tf_op jit(solution)/shard_map/ppermute | solution.py:383
  13.9 1.5 %collective-permute-start.6 = (f32[192,256]{1,0:T(8,128)S(1)}, f32[192,256]{1,0:T(8,128)S(1)}, u32[]{:S(2)}, u32[]{:S(2)}) collective-permute-start(f32[192,256]{1,0:T(8,128)S(1)} %get-tuple-element.34.refs_2_), channel_id=1, source_target_pairs={{0,1},{1,0},{2,3},{3,2},{4,5},{5,4},{6,7},{7,6},{8,9},{9,8},{10,11... | collective-permute-start | bytes 589832 | tf_op jit(solution)/shard_map/ppermute | solution.py:383
  14.0 1.7 %collective-permute-start.7 = (f32[192,256]{1,0:T(8,128)S(1)}, f32[192,256]{1,0:T(8,128)S(1)}, u32[]{:S(2)}, u32[]{:S(2)}) collective-permute-start(f32[192,256]{1,0:T(8,128)S(1)} %get-tuple-element.38.refs_3_), channel_id=1, source_target_pairs={{0,1},{1,0},{2,3},{3,2},{4,5},{5,4},{6,7},{7,6},{8,9},{9,8},{10,11... | collective-permute-start | bytes 589832 | tf_op jit(solution)/shard_map/ppermute | solution.py:383
  15.7 1.4 %collective-permute-start.8 = (f32[264,128]{1,0:T(8,128)S(1)}, f32[264,128]{1,0:T(8,128)S(1)}, u32[]{:S(2)}, u32[]{:S(2)}) collective-permute-start(f32[264,128]{1,0:T(8,128)S(1)} %shard_map.74.refs_0_), channel_id=1, source_target_pairs={{0,1},{1,0},{2,3},{3,2},{4,5},{5,4},{6,7},{7,6},{8,9},{9,8},{10,11... | collective-permute-start | bytes 405512 | tf_op jit(solution)/shard_map/ppermute | solution.py:383
  17.0 10.0 %collective-permute-start.9 = (f32[40,256]{1,0:T(8,128)S(1)}, f32[40,256]{1,0:T(8,128)S(1)}, u32[]{:S(2)}, u32[]{:S(2)}) collective-permute-start(f32[40,256]{1,0:T(8,128)S(1)} %get-tuple-element.40), channel_id=1, source_target_pairs={{4,1},{5,0},{6,3},{7,2},{8,10},{9,11},{10,8},{11,9},{0,12},{1,13},... | collective-permute-start | bytes 122888 | tf_op jit(solution)/shard_map/ppermute | solution.py:379
  19.5 7.5 %collective-permute-start.10 = (f32[40,256]{1,0:T(8,128)S(1)}, f32[40,256]{1,0:T(8,128)S(1)}, u32[]{:S(2)}, u32[]{:S(2)}) collective-permute-start(f32[40,256]{1,0:T(8,128)S(1)} %get-tuple-element.41), channel_id=1, source_target_pairs={{8,13},{9,12},{10,15},{11,14},{12,9},{13,8},{14,11},{15,10},{0,1},... | collective-permute-start | bytes 122888 | tf_op jit(solution)/shard_map/ppermute | solution.py:379
  19.5 7.5 %collective-permute-start.11 = (f32[16,128]{1,0:T(8,128)S(1)}, f32[16,128]{1,0:T(8,128)S(1)}, u32[]{:S(2)}, u32[]{:S(2)}) collective-permute-start(f32[16,128]{1,0:T(8,128)S(1)} %get-tuple-element.42), channel_id=1, source_target_pairs={{4,3},{5,2},{6,1},{7,0},{0,5},{1,4},{2,7},{3,6},{8,9},{9,8},{10,11... | collective-permute-start | bytes 24584 | tf_op jit(solution)/shard_map/ppermute | solution.py:379
  24.3 2.7 %collective-permute-start.12 = (f32[16,128]{1,0:T(8,128)S(1)}, f32[16,128]{1,0:T(8,128)S(1)}, u32[]{:S(2)}, u32[]{:S(2)}) collective-permute-start(f32[16,128]{1,0:T(8,128)S(1)} %get-tuple-element.43), channel_id=1, source_target_pairs={{4,6},{5,7},{6,4},{7,5},{8,15},{9,14},{10,13},{11,12},{12,9},{13,8... | collective-permute-start | bytes 24584 | tf_op jit(solution)/shard_map/ppermute | solution.py:379

commit v10 on v8

--- a/solution.py
+++ b/solution.py
@@ -428,7 +428,7 @@
         pin(pupil_bands.transpose(0, 2, 1)),
         pin(source_weight.reshape(1, per_device)),
     )
-    order = (0, half, *range(1, half), *range(half + 1, 2 * half))
+    order = (0, *range(1, half), half, *range(half + 1, 2 * half))
     blocks = [message] + [to_hub(message, d // half, d % half) for d in order[1:]]
     phases = [phases_to_hub(pupil_phase, n) for n in reversed(range(half))][::-1]
     *tables, phase = call(

time: 28 us -> 27.9 us (level)
  starting transfers between devices: 15 us -> 14.2 us
  waiting for transfers between devices: 9.51 us -> 10.2 us
    ppermute x9, starting transfers between devices: 14.2 us -> 13.4 us  [permute(): lax.ppermute(x, ('src', 'tile', 'row'), [(flat[a], flat[b]) for a, b in p...]
    ppermute x9, waiting for transfers between devices: 7.17 us -> 7.84 us  [permute(): lax.ppermute(x, ('src', 'tile', 'row'), [(flat[a], flat[b]) for a, b in p...]
where the time goes in v10:
time: 27.9 us; the launch traced here: 27.6 us
  starting transfers between devices  14.2 us (51%)
  waiting for transfers between devices  10.2 us (37%)
  Pallas kernels  2.58 us (9%)
  between operations  0.7 us (3%)
    ppermute x9, starting transfers between devices, permute(): lax.ppermute(x, ('src', 'tile', 'row'), [(flat[a], flat[b]) for a, b in p...  13.4 us
    ppermute x9, waiting for transfers between devices, permute(): lax.ppermute(x, ('src', 'tile', 'row'), [(flat[a], flat[b]) for a, b in p...  7.84 us
    ppermute x4, waiting for transfers between devices, swap_rows(): return lax.ppermute(x, 'row', [(0, 1), (1, 0)])  2.34 us
    pallas_call x1, Pallas kernels, hub_shards(): call(tables_kernel, [(2 * freqs, 2 * pixels)] * 2 + [(2 * pixels, 2 * fre...  0.97 us
    pallas_call x1, Pallas kernels, hub_shards(): call(fetch_kernel, [(2 * rows + PAD, pixels)], [pltpu.VMEM((per_device, 2...  0.82 us
    pallas_call x1, Pallas kernels, hub_shards(): call(functools.partial(place_kernel, half, 1.0 / (sources * pixels * tile...  0.77 us
    ppermute x4, starting transfers between devices, swap_rows(): return lax.ppermute(x, 'row', [(0, 1), (1, 0)])  0.77 us
  transfers between devices with their start and end apart: 13, of which 6 were waited for; matrix products, arithmetic and copies ran while one was open for 0% of the time, Pallas kernels for 4%

profile of v10, /device:TPU:0, one launch (start us, length us, event | category | flops | bytes accessed | tf_op | source)
XLA Modules:
  0.0 27.6 jit_solution(4147177606345762603)
XLA Ops:
  0.6 0.8 %shard_map.69.refs_0_ = f32[72,256]{1,0:T(8,128)S(1)} custom-call(f32[1,32,256]{2,1,0:T(8,128)} %mask.1, f32[1,32,256]{2,1,0:T(8,128)} %goal.1, s32[3,2,128]{2,1,0:T(2,128)} %bitcast.3, f32[1,3]{1,0:T(1,128)} %bitcast.4), custom_call_target="tpu_custom_call" | custom-call | tf_op jit(solution)/shard_map/pallas_call | solution.py:416
  1.5 4.1 %collective-permute-start.4 = (f32[72,256]{1,0:T(8,128)S(1)}, f32[72,256]{1,0:T(8,128)S(1)}, u32[]{:S(2)}, u32[]{:S(2)}) collective-permute-start(f32[72,256]{1,0:T(8,128)S(1)} %shard_map.69.refs_0_), channel_id=1, source_target_pairs={{0,8},{1,9},{2,10},{3,11},{12,4},{13,5},{14,6},{15,7},{4,0},{5,1},... | collective-permute-start | bytes 221192 | tf_op jit(solution)/shard_map/ppermute | solution.py:376
  5.5 0.0 collective-permute-start.3
  5.5 2.1 %collective-permute-start.2 = (f32[72,256]{1,0:T(8,128)S(1)}, f32[72,256]{1,0:T(8,128)S(1)}, u32[]{:S(2)}, u32[]{:S(2)}) collective-permute-start(f32[72,256]{1,0:T(8,128)S(1)} %shard_map.69.refs_0_), channel_id=1, source_target_pairs={{0,4},{1,5},{2,6},{3,7},{12,8},{13,9},{14,10},{15,11},{4,0},{5,1},... | collective-permute-start | bytes 221192 | tf_op jit(solution)/shard_map/ppermute | solution.py:376
  7.7 0.0 collective-permute-start.1
  7.7 0.0 collective-permute-start
  7.7 1.0 %shard_map.68 = (bf16[256,512]{1,0:T(8,128)(2,1)S(1)}, bf16[256,512]{1,0:T(8,128)(2,1)S(1)}, bf16[512,256]{1,0:T(8,128)(2,1)S(1)}, bf16[512,256]{1,0:T(8,128)(2,1)S(1)}, f32[3,128,128]{2,1,0:T(8,128)S(1)}) custom-call(f32[3,128,128]{2,1,0:T(8,128)} %phase.1), custom_call_target="tpu_custom_call" | custom-call | tf_op jit(solution)/shard_map/pallas_call | solution.py:434
  8.7 0.0 collective-permute-done.4.refs_3_
  8.7 0.0 collective-permute-done.3.refs_2_
  8.7 2.0 %collective-permute-done.2.refs_1_ = f32[72,256]{1,0:T(8,128)S(1)} collective-permute-done((f32[72,256]{1,0:T(8,128)S(1)}, f32[72,256]{1,0:T(8,128)S(1)}, u32[]{:S(2)}, u32[]{:S(2)}) %collective-permute-start.2) | collective-permute-done | bytes 73760 | tf_op jit(solution)/shard_map/ppermute | solution.py:376
  10.7 0.0 collective-permute-start.5
  10.7 3.7 %collective-permute-done.1.refs_2_ = f32[3,128,128]{2,1,0:T(8,128)S(1)} collective-permute-done((f32[3,128,128]{2,1,0:T(8,128)}, f32[3,128,128]{2,1,0:T(8,128)S(1)}, u32[]{:S(2)}, u32[]{:S(2)}) %collective-permute-start.1) | collective-permute-done | bytes 196640 | tf_op jit(solution)/shard_map/ppermute | solution.py:376
  14.4 0.0 collective-permute-done.refs_1_
  14.4 0.0 collective-permute-done.5.refs_4_
  14.4 0.1 collective-permute-start.6
  14.6 0.5 %collective-permute-start.7 = (f32[192,256]{1,0:T(8,128)S(1)}, f32[192,256]{1,0:T(8,128)S(1)}, u32[]{:S(2)}, u32[]{:S(2)}) collective-permute-start(f32[192,256]{1,0:T(8,128)S(1)} %get-tuple-element.38.refs_3_), channel_id=1, source_target_pairs={{0,1},{1,0},{2,3},{3,2},{4,5},{5,4},{6,7},{7,6},{8,9},{9,8},{10,11... | collective-permute-start | bytes 589832 | tf_op jit(solution)/shard_map/ppermute | solution.py:380
  15.0 0.9 %collective-permute-done.6.refs_3_ = f32[192,256]{1,0:T(8,128)S(1)} collective-permute-done((f32[192,256]{1,0:T(8,128)S(1)}, f32[192,256]{1,0:T(8,128)S(1)}, u32[]{:S(2)}, u32[]{:S(2)}) %collective-permute-start.6) | collective-permute-done | bytes 196640 | tf_op jit(solution)/shard_map/ppermute | solution.py:380
  16.0 0.3 %collective-permute-done.7.refs_4_ = f32[192,256]{1,0:T(8,128)S(1)} collective-permute-done((f32[192,256]{1,0:T(8,128)S(1)}, f32[192,256]{1,0:T(8,128)S(1)}, u32[]{:S(2)}, u32[]{:S(2)}) %collective-permute-start.7) | collective-permute-done | bytes 196640 | tf_op jit(solution)/shard_map/ppermute | solution.py:380
  16.2 0.2 collective-permute-start.8
  16.5 1.1 %collective-permute-done.8.refs_1_ = f32[264,128]{1,0:T(8,128)S(1)} collective-permute-done((f32[264,128]{1,0:T(8,128)S(1)}, f32[264,128]{1,0:T(8,128)S(1)}, u32[]{:S(2)}, u32[]{:S(2)}) %collective-permute-start.8) | collective-permute-done | bytes 135200 | tf_op jit(solution)/shard_map/ppermute | solution.py:380
  17.6 2.1 %collective-permute-start.9 = (f32[40,256]{1,0:T(8,128)S(1)}, f32[40,256]{1,0:T(8,128)S(1)}, u32[]{:S(2)}, u32[]{:S(2)}) collective-permute-start(f32[40,256]{1,0:T(8,128)S(1)} %get-tuple-element.40), channel_id=1, source_target_pairs={{4,1},{5,0},{6,3},{7,2},{8,10},{9,11},{10,8},{11,9},{0,12},{1,13},... | collective-permute-start | bytes 122888 | tf_op jit(solution)/shard_map/ppermute | solution.py:376
  19.7 0.0 collective-permute-start.10
  19.7 4.9 %collective-permute-start.11 = (f32[16,128]{1,0:T(8,128)S(1)}, f32[16,128]{1,0:T(8,128)S(1)}, u32[]{:S(2)}, u32[]{:S(2)}) collective-permute-start(f32[16,128]{1,0:T(8,128)S(1)} %get-tuple-element.42), channel_id=1, source_target_pairs={{4,3},{5,2},{6,1},{7,0},{0,5},{1,4},{2,7},{3,6},{8,9},{9,8},{10,11... | collective-permute-start | bytes 24584 | tf_op jit(solution)/shard_map/ppermute | solution.py:376
  24.6 0.2 collective-permute-start.12
  24.8 2.1 %collective-permute-done.11.got_c = f32[16,128]{1,0:T(8,128)S(1)} collective-permute-done((f32[16,128]{1,0:T(8,128)S(1)}, f32[16,128]{1,0:T(8,128)S(1)}, u32[]{:S(2)}, u32[]{:S(2)}) %collective-permute-start.11) | collective-permute-done | bytes 8224 | tf_op jit(solution)/shard_map/ppermute | solution.py:376
  26.9 0.0 collective-permute-done.12.got_d
  26.9 0.0 collective-permute-done.9.got_a
  26.9 0.0 collective-permute-done.10.got_b
  26.9 0.8 %shard_map.76 = (f32[1,32,256]{2,1,0:T(8,128)}, f32[1,3]{1,0:T(1,128)}) custom-call(f32[40,256]{1,0:T(8,128)S(1)} %get-tuple-element.39.own, f32[40,256]{1,0:T(8,128)S(1)} %collective-permute-done.9.got_a, f32[40,256]{1,0:T(8,128)S(1)} %collective-permute-done.10.got_b, f32[16,128]{1,0:T(8,128)S(1)} %collective-permute-done.11.got_c, ...), custom_call_target="tpu_custom_call" | custom-call | tf_op jit(solution)/shard_map/pallas_call | solution.py:507
  (6 shorter events, 0.0 us)
Async XLA Ops:
  1.5 7.2 %collective-permute-start.4 = (f32[72,256]{1,0:T(8,128)S(1)}, f32[72,256]{1,0:T(8,128)S(1)}, u32[]{:S(2)}, u32[]{:S(2)}) collective-permute-start(f32[72,256]{1,0:T(8,128)S(1)} %shard_map.69.refs_0_), channel_id=1, source_target_pairs={{0,8},{1,9},{2,10},{3,11},{12,4},{13,5},{14,6},{15,7},{4,0},{5,1},... | collective-permute-start | bytes 221192 | tf_op jit(solution)/shard_map/ppermute | solution.py:376
  5.5 3.2 %collective-permute-start.3 = (f32[72,256]{1,0:T(8,128)S(1)}, f32[72,256]{1,0:T(8,128)S(1)}, u32[]{:S(2)}, u32[]{:S(2)}) collective-permute-start(f32[72,256]{1,0:T(8,128)S(1)} %shard_map.69.refs_0_), channel_id=1, source_target_pairs={{4,8},{5,9},{6,10},{7,11},{8,4},{9,5},{10,6},{11,7},{0,1},{1,0},{2... | collective-permute-start | bytes 221192 | tf_op jit(solution)/shard_map/ppermute | solution.py:376
  5.5 5.2 %collective-permute-start.2 = (f32[72,256]{1,0:T(8,128)S(1)}, f32[72,256]{1,0:T(8,128)S(1)}, u32[]{:S(2)}, u32[]{:S(2)}) collective-permute-start(f32[72,256]{1,0:T(8,128)S(1)} %shard_map.69.refs_0_), channel_id=1, source_target_pairs={{0,4},{1,5},{2,6},{3,7},{12,8},{13,9},{14,10},{15,11},{4,0},{5,1},... | collective-permute-start | bytes 221192 | tf_op jit(solution)/shard_map/ppermute | solution.py:376
  7.7 6.8 %collective-permute-start.1 = (f32[3,128,128]{2,1,0:T(8,128)}, f32[3,128,128]{2,1,0:T(8,128)S(1)}, u32[]{:S(2)}, u32[]{:S(2)}) collective-permute-start(f32[3,128,128]{2,1,0:T(8,128)} %phase.1), channel_id=1, source_target_pairs={{0,4},{1,9},{2,6},{3,11},{12,8},{13,5},{14,10},{15,7},{4,0},{5,1},... | collective-permute-start | bytes 589832 | tf_op jit(solution)/shard_map/ppermute | solution.py:376
  7.7 6.7 %collective-permute-start = (f32[3,128,128]{2,1,0:T(8,128)}, f32[3,128,128]{2,1,0:T(8,128)S(1)}, u32[]{:S(2)}, u32[]{:S(2)}) collective-permute-start(f32[3,128,128]{2,1,0:T(8,128)} %phase.1), channel_id=1, source_target_pairs={{4,9},{6,11},{8,5},{10,7},{0,1},{1,0},{2,3},{3,2},{5,4},{7,6},{9,8... | collective-permute-start | bytes 589832 | tf_op jit(solution)/shard_map/ppermute | solution.py:376
  10.7 3.7 %collective-permute-start.5 = (f32[256,128]{1,0:T(8,128)S(1)}, f32[256,128]{1,0:T(8,128)S(1)}, u32[]{:S(2)}, u32[]{:S(2)}) collective-permute-start(f32[256,128]{1,0:T(8,128)S(1)} %get-tuple-element.29.refs_3_), channel_id=1, source_target_pairs={{0,1},{1,0},{2,3},{3,2},{4,5},{5,4},{6,7},{7,6},{8,9},{9,8},{10,11... | collective-permute-start | bytes 393224 | tf_op jit(solution)/shard_map/ppermute | solution.py:380
  14.4 1.5 %collective-permute-start.6 = (f32[192,256]{1,0:T(8,128)S(1)}, f32[192,256]{1,0:T(8,128)S(1)}, u32[]{:S(2)}, u32[]{:S(2)}) collective-permute-start(f32[192,256]{1,0:T(8,128)S(1)} %get-tuple-element.34.refs_2_), channel_id=1, source_target_pairs={{0,1},{1,0},{2,3},{3,2},{4,5},{5,4},{6,7},{7,6},{8,9},{9,8},{10,11... | collective-permute-start | bytes 589832 | tf_op jit(solution)/shard_map/ppermute | solution.py:380
  14.6 1.7 %collective-permute-start.7 = (f32[192,256]{1,0:T(8,128)S(1)}, f32[192,256]{1,0:T(8,128)S(1)}, u32[]{:S(2)}, u32[]{:S(2)}) collective-permute-start(f32[192,256]{1,0:T(8,128)S(1)} %get-tuple-element.38.refs_3_), channel_id=1, source_target_pairs={{0,1},{1,0},{2,3},{3,2},{4,5},{5,4},{6,7},{7,6},{8,9},{9,8},{10,11... | collective-permute-start | bytes 589832 | tf_op jit(solution)/shard_map/ppermute | solution.py:380
  16.2 1.4 %collective-permute-start.8 = (f32[264,128]{1,0:T(8,128)S(1)}, f32[264,128]{1,0:T(8,128)S(1)}, u32[]{:S(2)}, u32[]{:S(2)}) collective-permute-start(f32[264,128]{1,0:T(8,128)S(1)} %shard_map.74.refs_0_), channel_id=1, source_target_pairs={{0,1},{1,0},{2,3},{3,2},{4,5},{5,4},{6,7},{7,6},{8,9},{9,8},{10,11... | collective-permute-start | bytes 405512 | tf_op jit(solution)/shard_map/ppermute | solution.py:380
  17.6 9.3 %collective-permute-start.9 = (f32[40,256]{1,0:T(8,128)S(1)}, f32[40,256]{1,0:T(8,128)S(1)}, u32[]{:S(2)}, u32[]{:S(2)}) collective-permute-start(f32[40,256]{1,0:T(8,128)S(1)} %get-tuple-element.40), channel_id=1, source_target_pairs={{4,1},{5,0},{6,3},{7,2},{8,10},{9,11},{10,8},{11,9},{0,12},{1,13},... | collective-permute-start | bytes 122888 | tf_op jit(solution)/shard_map/ppermute | solution.py:376
  19.7 7.1 %collective-permute-start.10 = (f32[40,256]{1,0:T(8,128)S(1)}, f32[40,256]{1,0:T(8,128)S(1)}, u32[]{:S(2)}, u32[]{:S(2)}) collective-permute-start(f32[40,256]{1,0:T(8,128)S(1)} %get-tuple-element.41), channel_id=1, source_target_pairs={{8,13},{9,12},{10,15},{11,14},{12,9},{13,8},{14,11},{15,10},{0,1},... | collective-permute-start | bytes 122888 | tf_op jit(solution)/shard_map/ppermute | solution.py:376
  19.7 7.1 %collective-permute-start.11 = (f32[16,128]{1,0:T(8,128)S(1)}, f32[16,128]{1,0:T(8,128)S(1)}, u32[]{:S(2)}, u32[]{:S(2)}) collective-permute-start(f32[16,128]{1,0:T(8,128)S(1)} %get-tuple-element.42), channel_id=1, source_target_pairs={{4,3},{5,2},{6,1},{7,0},{0,5},{1,4},{2,7},{3,6},{8,9},{9,8},{10,11... | collective-permute-start | bytes 24584 | tf_op jit(solution)/shard_map/ppermute | solution.py:376
  24.6 2.3 %collective-permute-start.12 = (f32[16,128]{1,0:T(8,128)S(1)}, f32[16,128]{1,0:T(8,128)S(1)}, u32[]{:S(2)}, u32[]{:S(2)}) collective-permute-start(f32[16,128]{1,0:T(8,128)S(1)} %get-tuple-element.43), channel_id=1, source_target_pairs={{4,6},{5,7},{6,4},{7,5},{8,15},{9,14},{10,13},{11,12},{12,9},{13,8... | collective-permute-start | bytes 24584 | tf_op jit(solution)/shard_map/ppermute | solution.py:376
